TPU v7x, 32 devices: a whole 2x2x4 slice. The times are simulated.
32 devices in a mesh: exp: 16 (over z, y, core), feat: 2 (over x).
Axes of the slice: x: 2, y: 2, z: 4, core: 2. Of those that a mesh axis runs over, the one named last changes fastest.
Arguments:
- tokens: bfloat16 [256, 7168], P('exp', 'feat'), may hold values from -6 to 6
- route_ids: int32 [256, 8], P('exp'), may hold values from 0 to 15, all different within a row
- route_weights: float32 [256, 8], P('exp'), may hold values from 0.05 to 0.6
- gate_proj: bfloat16 [16, 7168, 1024], P('exp', 'feat'), may hold values from -0.0625 to 0.0625
- up_proj: bfloat16 [16, 7168, 1024], P('exp', 'feat'), may hold values from -0.0625 to 0.0625
- down_proj: bfloat16 [16, 1024, 7168], P('exp', None, 'feat'), may hold values from -0.1875 to 0.1875
- enc_weight: bfloat16 [7168, 65536], P('feat', 'exp'), may hold values from -0.0625 to 0.0625
- enc_bias: float32 [65536], P('exp'), may hold values from -3 to 3
- dec_weight: bfloat16 [65536, 7168], P('exp', 'feat'), may hold values from -0.0234375 to 0.0234375
- dec_bias: float32 [7168], P('feat'), may hold values from -3 to 3
- clamp_ids: int32 [64], replicated, may hold values from 0 to 65535, as said below
- clamp_values: bfloat16 [64], replicated, may hold values from 8 to 30
Outputs:
- error_term: float32 [256, 7168], P('exp', 'feat')
- steered: float32 [256, 7168], P('exp', 'feat')
Inputs may be any that keep to these rules, and one draw needn't show every extreme that they name: `route_ids`: each token names 8 different experts. `clamp_ids`: 64 different features.
All inputs are finite; a program needn't handle non-finite values.
Results may differ from a plain program's by a relative error of at most 0.0035.
Values may be sent and summed in bfloat16 or wider, within the bound.
No kernel may reach another device: no remote copies, remote signals or barrier semaphores. Data moves between devices by JAX's collectives and lax.ppermute only.
A program may use at most 128 MiB of HBM per device.

v0:
```python
import jax
import jax.numpy as jnp
from jax import lax
from jax.sharding import PartitionSpec as P

SLOT = 8


def local_codes(route_ids, slot_limit, expert_count):
    flat_ids = route_ids.reshape(-1)
    experts = jnp.arange(expert_count, dtype=jnp.int32)
    onehot = (flat_ids[:, None] == experts[None, :]).astype(jnp.int32)
    before = jnp.sum(jnp.cumsum(onehot, axis=0) * onehot, axis=1) - 1
    slot_code = jnp.where(before < slot_limit, flat_ids * slot_limit + before, -1)
    return slot_code.reshape(route_ids.shape)


def local(
    tokens,
    route_ids,
    route_weights,
    gate_proj,
    up_proj,
    down_proj,
    enc_weight,
    enc_bias,
    dec_weight,
    dec_bias,
    clamp_ids,
    clamp_values,
):
    expert_count = lax.axis_size("exp")
    row_count, shard_width = tokens.shape
    capacity = expert_count * SLOT
    slot_code = local_codes(route_ids, SLOT, expert_count)
    targets = jnp.arange(capacity, dtype=jnp.int32)
    matches = slot_code[None, :, :] == targets[:, None, None]
    partial_pre = jnp.dot(
        lax.all_gather(tokens, "exp", axis=0, tiled=True),
        enc_weight,
        preferred_element_type=jnp.float32,
    )
    picker = jnp.any(matches, axis=2).astype(jnp.bfloat16)
    outgoing = jnp.dot(picker, tokens, preferred_element_type=jnp.float32).astype(jnp.bfloat16)
    incoming = lax.all_to_all(
        outgoing.reshape(expert_count, SLOT, shard_width),
        "exp",
        split_axis=0,
        concat_axis=0,
        tiled=True,
    )
    expert_in = incoming.reshape(capacity, shard_width)
    gate_part = jnp.dot(expert_in, gate_proj[0], preferred_element_type=jnp.float32)
    up_part = jnp.dot(expert_in, up_proj[0], preferred_element_type=jnp.float32)
    pre_sum, gate_sum, up_sum = lax.psum((partial_pre, gate_part, up_part), "feat")
    feature_act = jax.nn.relu(pre_sum + enc_bias).astype(jnp.bfloat16)
    hidden = (jax.nn.silu(gate_sum) * up_sum).astype(jnp.bfloat16)
    expert_out = jnp.dot(hidden, down_proj[0], preferred_element_type=jnp.float32).astype(
        jnp.bfloat16
    )
    returned = lax.all_to_all(
        expert_out.reshape(expert_count, SLOT, shard_width),
        "exp",
        split_axis=0,
        concat_axis=0,
        tiled=True,
    )
    weighted = jnp.sum(jnp.where(matches, route_weights[None, :, :], 0.0), axis=2)
    returned_rows = returned.reshape(capacity, shard_width).astype(jnp.float32)
    moe_out = jnp.einsum("cr,cd->rd", weighted, returned_rows, precision=lax.Precision.HIGHEST)
    feature_count = enc_weight.shape[1]
    feature_base = lax.axis_index("exp") * feature_count
    local_ids = clamp_ids - feature_base
    inside = (local_ids >= 0) & (local_ids < feature_count)
    safe_ids = jnp.clip(local_ids, 0, feature_count - 1)
    chosen = jnp.take(feature_act, safe_ids, axis=1).astype(jnp.float32)
    change = jnp.where(inside[None, :], clamp_values.astype(jnp.float32)[None, :] - chosen, 0.0)
    rows_dec = jnp.take(dec_weight, safe_ids, axis=0).astype(jnp.float32)
    shift_part = jnp.dot(change, rows_dec, precision=lax.Precision.HIGHEST)
    rebuilt_rows = jnp.dot(feature_act, dec_weight, preferred_element_type=jnp.float32)
    summed = lax.psum_scatter(
        jnp.concatenate([rebuilt_rows, shift_part], axis=1), "exp", scatter_dimension=0, tiled=True
    )
    rebuilt = summed[:, :shard_width]
    clamp_shift = summed[:, shard_width:]
    error_term = moe_out - rebuilt - dec_bias
    steered = moe_out + clamp_shift
    return (error_term, steered)


def solution(mesh):
    placed = (
        P("exp", "feat"),
        P("exp", None),
        P("exp", None),
        P("exp", "feat", None),
        P("exp", "feat", None),
        P("exp", None, "feat"),
        P("feat", "exp"),
        P("exp"),
        P("exp", "feat"),
        P("feat"),
        P(),
        P(),
    )
    return jax.shard_map(
        local,
        mesh=mesh,
        in_specs=placed,
        out_specs=(P("exp", "feat"), P("exp", "feat")),
        check_vma=False,
    )
```

profile of v0, /device:TPU:0, one launch (start us, length us, event | category | flops | bytes accessed | tf_op | source)
XLA Modules:
  0.0 333.1 jit_solution(18415347704141830197)
XLA Ops:
  7.2 0.0 all-gather.2.cloned.1.call-start
  7.2 0.7 all-gather.2.cloned.1.call-update
  7.9 0.0 all-reduce.3.cloned.1.call-start
  7.9 0.8 copy.22
  8.7 0.1 eq.28
  8.8 0.1 fusion.27
  8.9 0.2 reduce_window_sum.11
  9.1 0.2 select_reduce_fusion.1
  9.2 0.1 sub.32
  9.3 0.1 fusion.26
  9.5 1.3 fusion.9
  10.8 0.0 slice-start
  10.8 33.7 %all_to_all.10 = bf16[16,8,3584]{2,1,0:T(8,128)(2,1)S(1)} all-to-all(bf16[16,8,3584]{2,1,0:T(8,128)(2,1)S(1)} %fusion.9), channel_id=1, replica_groups=mesh['exp'=16,'feat'=2] {'exp'}, dimensions={0} | all-to-all | bytes 1835008 | tf_op jit(solution)/shard_map/all_to_all | solution.py:45
  44.5 0.0 slice-start.1
  44.5 5.2 %fusion.2 = f32[128,1024]{1,0:T(8,128)} fusion(bf16[1,3584,1024]{2,1,0:T(8,128)(2,1)} %param.16, bf16[16,8,3584]{2,1,0:T(8,128)(2,1)S(1)} %all_to_all.10), kind=kOutput, calls=%fused_computation.5 | convolution fusion | flops 939524096 | bytes 8781824 | tf_op jit(solution)/shard_map/dot_general | solution.py:54
  49.7 0.0 slice-done
  49.7 0.0 slice-done.1
  49.7 1.9 fusion.4
  51.6 6.1 %all-gather.2.cloned.1.call-done = bf16[256,3584]{1,0:T(8,128)(2,1)} async-done(((bf16[16,3584]{1,0:T(8,128)(2,1)}), bf16[256,3584]{1,0:T(8,128)(2,1)}) %all-gather.2.cloned.1.call-update) | async-done | bytes 1835024 | tf_op jit(solution)/shard_map/all_gather | solution.py:39
  57.7 15.2 %fusion.37 = f32[256,4096]{1,0:T(8,128)} fusion(bf16[256,3584]{1,0:T(8,128)(2,1)} %all-gather.2.cloned.1.call-done, bf16[3584,4096]{1,0:T(8,128)(2,1)} %param.18), kind=kOutput, calls=%fused_computation.51 | convolution fusion | flops 7516192768 | bytes 35389440 | tf_op jit(solution)/shard_map/dot_general | solution.py:38
  72.8 0.0 copy-start.7
  72.8 0.0 copy-start.4
  72.8 0.0 copy-start.1
  72.8 0.0 all-reduce.3.cloned.1.call-update
  72.9 0.2 reduce-scatter.2.cloned.1.call-start
  73.1 0.4 copy-done.7
  73.5 0.0 copy-done.4
  73.5 15.3 %gather_fusion.1 = bf16[64,3584]{1,0:T(8,128)(2,1)S(1)} fusion(bf16[4096,3584]{1,0:T(8,128)(2,1)} %param.20, s32[1024]{0:T(1024)S(1)} %pad_clamp_fusion), kind=kCustom, calls=%fused_computation.1 | custom fusion | bytes 917760 | tf_op jit(solution)/shard_map/jit(_take)/gather | solution.py:78
  88.8 114.6 %all-reduce.3.cloned.1.call-done = (f32[128,1024]{1,0:T(8,128)}, f32[128,1024]{1,0:T(8,128)}, f32[256,4096]{1,0:T(8,128)}) async-done(((f32[128,1024]{1,0:T(8,128)}, f32[128,1024]{1,0:T(8,128)}, f32[256,4096]{1,0:T(8,128)}), (f32[128,1024]{1,0:T(8,128)}, f32[128,1024]{1,0:T(8,128)}, f32[256,4096]{1,0:T(8,128)})) %all-reduce.3.cloned.1.call-update) | async-done | bytes 5242896 | tf_op jit(solution)/shard_map/psum | solution.py:55
  203.5 0.0 copy-done.1
  203.5 2.6 maximum_convert_fusion
  206.1 2.5 copy.25
  208.6 15.1 %fusion.38 = f32[256,3584]{1,0:T(8,128)} fusion(bf16[256,4096]{1,0:T(8,128)(2,1)S(1)} %maximum_convert_fusion, bf16[4096,3584]{1,0:T(8,128)(2,1)} %param.20), kind=kOutput, calls=%fused_computation.52 | convolution fusion | flops 7516192768 | bytes 35127296 | tf_op jit(solution)/shard_map/dot_general | solution.py:80
  223.7 2.5 gather_fusion
  226.2 0.0 copy-start
  226.2 1.7 fusion.17
  227.9 0.3 copy-done
  228.2 3.4 %pad_maximum_fusion = f32[256,7168]{1,0:T(8,128)} fusion(f32[256,3584]{1,0:T(8,128)S(1)} %fusion.17, f32[256,3584]{1,0:T(8,128)S(1)} %copy-done), kind=kLoop, calls=%fused_computation.2 | loop fusion | flops 1835008 | bytes 14680064 | tf_op jit(solution)/shard_map/concatenate | solution.py:82
  231.7 0.0 copy-start.5
  231.7 0.0 copy-start.6
  231.7 0.0 reduce-scatter.2.cloned.1.call-update
  231.7 1.0 copy-done.5
  232.7 0.2 copy-done.6
  232.9 0.0 copy-start.3
  232.9 0.0 copy-start.2
  232.9 5.2 %fusion.10 = bf16[16,8,3584]{2,1,0:T(8,128)(2,1)} fusion(bf16[1,1024,3584]{2,1,0:T(8,128)(2,1)} %param.17, f32[128,1024]{1,0:T(8,128)S(1)} %copy-done.5, f32[128,1024]{1,0:T(8,128)S(1)} %copy-done.6), kind=kOutput, calls=%fused_computation.12 | convolution fusion | flops 940769280 | bytes 9306112 | tf_op jit(solution)/shard_map/dot_general | solution.py:58
  238.1 5.6 %all-to-all-start.1 = ((bf16[16,8,3584]{2,1,0:T(8,128)(2,1)}), bf16[16,8,3584]{2,1,0:T(8,128)(2,1)S(1)}, u32[]{:S(2)}, u32[]{:S(2)}) async-start(bf16[16,8,3584]{2,1,0:T(8,128)(2,1)} %fusion.10), calls=%async_computation.1 | async-start | bytes 1835008 | tf_op jit(solution)/shard_map/all_to_all | solution.py:61
  243.7 0.0 copy-done.3
  243.7 0.1 copy.24
  243.8 0.1 select_reduce_fusion
  243.9 20.6 %all-to-all-done.1 = bf16[16,8,3584]{2,1,0:T(8,128)(2,1)S(1)} async-done(((bf16[16,8,3584]{2,1,0:T(8,128)(2,1)}), bf16[16,8,3584]{2,1,0:T(8,128)(2,1)S(1)}, u32[]{:S(2)}, u32[]{:S(2)}) %all-to-all-start.1) | async-done | bytes 917536 | tf_op jit(solution)/shard_map/all_to_all | solution.py:61
  264.6 59.7 %reduce-scatter.2.cloned.1.call-done = f32[16,7168]{1,0:T(8,128)} async-done(((f32[256,7168]{1,0:T(8,128)}), f32[16,7168]{1,0:T(8,128)}) %reduce-scatter.2.cloned.1.call-update) | async-done | bytes 458768 | tf_op jit(solution)/shard_map/reduce_scatter | solution.py:81
  324.3 0.0 copy-done.2
  324.3 2.3 slice_add_fusion
  (6 shorter events, 0.0 us)
Async XLA Ops:
  7.2 50.5 %all-gather.2.cloned.1.call-start = ((), (), s32[]{:S(2)}) async-start(), calls=%async_computation.3 | async-start | bytes 1949696 | tf_op jit(solution)/shard_map/all_gather | solution.py:39
  7.9 195.6 %all-reduce.3.cloned.1.call-start = ((), (), s32[]{:S(2)}) async-start(), calls=%async_computation.5 | async-start | bytes 10485760 | tf_op jit(solution)/shard_map/psum | solution.py:55
  10.8 38.9 %slice-start = ((s8[7340032]{0:T(1024)(128)(4,1)}), s8[4194304]{0:T(1024)(128)(4,1)S(1)}, s32[]{:S(2)}) async-start(s8[7340032]{0:T(1024)(128)(4,1)} %bitcast.34), calls=%async_computation.6 | async-start | bytes 8388608
  44.5 5.2 %slice-start.1 = ((s8[7340032]{0:T(1024)(128)(4,1)}), s8[3145728]{0:T(1024)(128)(4,1)S(1)}, s32[]{:S(2)}) async-start(s8[7340032]{0:T(1024)(128)(4,1)} %bitcast.34), calls=%async_computation.7 | async-start | bytes 6291456
  72.8 0.7 copy-start.7
  72.8 0.7 copy-start.4
  72.8 130.6 %copy-start.1 = (f32[4096]{0:T(1024)S(1)}, f32[4096]{0:T(1024)}, u32[]{:S(2)}) copy-start(f32[4096]{0:T(1024)} %param.19) | copy-start | bytes 49156
  72.9 251.4 %reduce-scatter.2.cloned.1.call-start = ((), (), s32[]{:S(2)}) async-start(), calls=%async_computation.4 | async-start | bytes 7798784 | tf_op jit(solution)/shard_map/reduce_scatter | solution.py:81
  226.2 2.0 copy-start
  231.7 1.0 copy-start.5
  231.7 1.2 copy-start.6
  232.9 10.9 %copy-start.3 = (f32[16,8]{0,1:T(8,128)S(1)}, f32[16,8]{0,1:T(8,128)}, u32[]{:S(2)}) copy-start(f32[16,8]{0,1:T(8,128)} %param.14) | copy-start | bytes 1540
  232.9 91.4 %copy-start.2 = (f32[3584]{0:T(1024)S(1)}, f32[3584]{0:T(1024)}, u32[]{:S(2)}) copy-start(f32[3584]{0:T(1024)} %param.21) | copy-start | bytes 43012
  238.1 26.4 %all-to-all-start.1 = ((bf16[16,8,3584]{2,1,0:T(8,128)(2,1)}), bf16[16,8,3584]{2,1,0:T(8,128)(2,1)S(1)}, u32[]{:S(2)}, u32[]{:S(2)}) async-start(bf16[16,8,3584]{2,1,0:T(8,128)(2,1)} %fusion.10), calls=%async_computation.1 | async-start | bytes 1835008 | tf_op jit(solution)/shard_map/all_to_all | solution.py:61
Sparse Core Ops, SparseCore 0:
  10.3 47.3 all-gather.1
  73.0 130.4 all-reduce.2
  231.8 92.4 reduce-scatter.1
where the time goes:
time: 334 us; the launch traced here: 333 us
  waiting for transfers between devices  202 us (60%)
  matrix products  47.9 us (14%)
  blocking collectives  33.7 us (10%)
  local copies, waits for them, and re-layouts  23.2 us (7%)
  between operations  13.9 us (4%)
  other arithmetic  6.77 us (2%)
  starting transfers between devices  5.92 us (2%)
    psum x1, waiting for transfers between devices, local(): lax.psum((partial_pre, gate_part, up_part), 'feat')  115 us
    reduce_scatter x1, waiting for transfers between devices, local(): lax.psum_scatter(jnp.concatenate([rebuilt_rows, shift_part], axis=1), 'ex...  59.7 us
    all_to_all x1, blocking collectives, local(): lax.all_to_all(outgoing.reshape(expert_count, SLOT, shard_width), 'exp',...  33.7 us
    all_to_all x1, waiting for transfers between devices, local(): lax.all_to_all(expert_out.reshape(expert_count, SLOT, shard_width), 'exp'...  20.6 us
    gather x1, local copies, waits for them, and re-layouts, local(): rows_dec = jnp.take(dec_weight, safe_ids, axis=0).astype(jnp.float32)  15.3 us
    dot_general x1, matrix products, local(): jnp.dot(lax.all_gather(tokens, 'exp', axis=0, tiled=True), enc_weight, pr...  15.2 us
    dot_general x1, matrix products, local(): jnp.dot(feature_act, dec_weight, preferred_element_type=jnp.float32)  15.1 us
  transfers between devices with their start and end apart: 4, of which 4 were waited for; matrix products, arithmetic and copies ran while one was open for 9% of the time, Pallas kernels for 0%

commit v1 on v0

v1 whole, which is shorter than its diff:
```python
import jax
import jax.numpy as jnp
from jax import lax
from jax.experimental import pallas as pl
from jax.experimental.pallas import tpu as pltpu
from jax.sharding import PartitionSpec as P

SLOT = 8
HALVES = 2
CHUNKS = 4
PIECES = 2
LANES = 128
GROUP = 16


def swap(x, axis, mask):
    size = lax.axis_size(axis)
    return lax.ppermute(x, axis, [(i, i ^ mask) for i in range(size)])


def doublings(size):
    masks = []
    while size > 1:
        size //= 2
        masks.append(size)
    return masks


def gather_blocks(x):
    for mask in doublings(lax.axis_size("exp")):
        x = jnp.concatenate([x, swap(x, "exp", mask)], axis=0)
    return x


def block_offsets(size):
    offsets = [0]
    for mask in doublings(size):
        offsets = offsets + [o ^ mask for o in offsets]
    return offsets


def scatter_sum(x):
    for mask in reversed(doublings(lax.axis_size("exp"))):
        half = x.shape[0] // 2
        x = x[:half] + swap(x[half:].astype(jnp.bfloat16), "exp", mask).astype(jnp.float32)
    return x


def sum_feat(x):
    for mask in doublings(lax.axis_size("feat")):
        x = x + swap(x.astype(jnp.bfloat16), "feat", mask).astype(jnp.float32)
    return x


def rows_kernel(ids_ref, pick_ref, dec_ref, out_ref, held, sems):
    count = ids_ref.shape[0]

    def copy(j):
        start = pl.multiple_of(ids_ref[j] // GROUP * GROUP, GROUP)
        return pltpu.make_async_copy(
            dec_ref.at[pl.ds(start, GROUP)], held.at[pl.ds(j * GROUP, GROUP)], sems.at[j]
        )

    for j in range(count):
        copy(j).start()
    for j in range(count):
        copy(j).wait()
    out_ref[...] = jnp.dot(pick_ref[...], held[...], preferred_element_type=jnp.float32).astype(
        out_ref.dtype
    )


def decoder_rows(dec_weight, safe_ids, inside):
    count, width = safe_ids.shape[0], dec_weight.shape[1]
    column = jnp.arange(count * GROUP, dtype=jnp.int32)
    wanted = jnp.arange(count, dtype=jnp.int32) * GROUP + safe_ids % GROUP
    pick = ((wanted[:, None] == column[None, :]) & inside[:, None]).astype(jnp.bfloat16)
    return pl.pallas_call(
        rows_kernel,
        out_shape=jax.ShapeDtypeStruct((count, width), jnp.bfloat16),
        in_specs=[
            pl.BlockSpec(memory_space=pltpu.SMEM),
            pl.BlockSpec(memory_space=pltpu.VMEM),
            pl.BlockSpec(memory_space=pl.ANY),
        ],
        out_specs=pl.BlockSpec(memory_space=pltpu.VMEM),
        scratch_shapes=[
            pltpu.VMEM((count * GROUP, width), jnp.bfloat16),
            pltpu.SemaphoreType.DMA((count,)),
        ],
        compiler_params=pltpu.CompilerParams(vmem_limit_bytes=24 * 1024 * 1024),
        cost_estimate=pl.CostEstimate(
            flops=2 * count * count * GROUP * width,
            bytes_accessed=2 * count * GROUP * width,
            transcendentals=0,
        ),
    )(safe_ids, pick, dec_weight)


def local_codes(route_ids, slot_limit, expert_count):
    flat_ids = route_ids.reshape(-1)
    experts = jnp.arange(expert_count, dtype=jnp.int32)
    onehot = (flat_ids[:, None] == experts[None, :]).astype(jnp.int32)
    before = jnp.sum(jnp.cumsum(onehot, axis=0) * onehot, axis=1) - 1
    slot_code = jnp.where(before < slot_limit, flat_ids * slot_limit + before, -1)
    return slot_code.reshape(route_ids.shape)


def local(
    tokens,
    route_ids,
    route_weights,
    gate_proj,
    up_proj,
    down_proj,
    enc_weight,
    enc_bias,
    dec_weight,
    dec_bias,
    clamp_ids,
    clamp_values,
):
    expert_count = lax.axis_size("exp")
    me = lax.axis_index("exp")
    row_count, width = tokens.shape
    top = route_ids.shape[1]
    half_rows = row_count // HALVES
    capacity = expert_count * SLOT
    feature_count = enc_weight.shape[1]
    offsets = jnp.array(block_offsets(expert_count), dtype=jnp.int32)

    ids_columns = jnp.pad(route_ids.astype(jnp.bfloat16), ((0, 0), (0, LANES - top)))
    outgoing = jnp.concatenate([tokens, ids_columns], axis=1)
    gathered = [
        gather_blocks(outgoing[h * half_rows : (h + 1) * half_rows]) for h in range(HALVES)
    ]
    all_tokens = [g[:, :width] for g in gathered]

    local_ids = clamp_ids - me * feature_count
    inside = (local_ids >= 0) & (local_ids < feature_count)
    safe_ids = jnp.clip(local_ids, 0, feature_count - 1)
    rows_dec = lax.psum(decoder_rows(dec_weight, safe_ids, inside), "exp")
    features = jnp.arange(feature_count, dtype=jnp.int32)
    clamp_count = clamp_ids.shape[0]
    clamp_pick = (features[:, None] == local_ids[None, :]).astype(jnp.bfloat16)
    clamp_pick = jnp.pad(clamp_pick, ((0, 0), (0, -clamp_count % LANES)))

    ids = jnp.concatenate(
        [g[:, width : width + top].reshape(expert_count, half_rows, top) for g in gathered], axis=1
    ).astype(jnp.int32)
    hit = jnp.any(ids == me, axis=2)
    order = jnp.arange(row_count)
    earlier = order[None, :] < order[:, None]
    slot = jnp.sum((hit[:, None, :] & earlier[None]).astype(jnp.int32), axis=2)
    code = jnp.where(hit & (slot < SLOT), (me ^ offsets)[:, None] * SLOT + slot, -1)
    targets = jnp.arange(capacity, dtype=jnp.int32)
    expert_in = 0.0
    for h in range(HALVES):
        part = code[:, h * half_rows : (h + 1) * half_rows].reshape(-1)
        picker = (part[None, :] == targets[:, None]).astype(jnp.bfloat16)
        expert_in += jnp.dot(picker, all_tokens[h], preferred_element_type=jnp.float32)
    expert_in = expert_in.astype(jnp.bfloat16)

    step = feature_count // CHUNKS

    def activations(h):
        acts = []
        for c in range(CHUNKS):
            part = jnp.dot(
                all_tokens[h],
                enc_weight[:, c * step : (c + 1) * step],
                preferred_element_type=jnp.float32,
            )
            pre = sum_feat(part) + enc_bias[c * step : (c + 1) * step]
            acts.append(jax.nn.relu(pre).astype(jnp.bfloat16))
        return acts

    def rebuild(acts):
        each = CHUNKS // PIECES
        rebuilt, chosen = 0.0, 0.0
        for p in range(PIECES):
            act = jnp.concatenate(acts[p * each : (p + 1) * each], axis=1)
            span = slice(p * each * step, (p + 1) * each * step)
            rebuilt += jnp.dot(act, dec_weight[span], preferred_element_type=jnp.float32)
            chosen += jnp.dot(act, clamp_pick[span], preferred_element_type=jnp.float32)
        return scatter_sum(jnp.concatenate([rebuilt, chosen], axis=1))

    acts = [activations(0)]

    gate_part = jnp.dot(expert_in, gate_proj[0], preferred_element_type=jnp.float32)
    up_part = jnp.dot(expert_in, up_proj[0], preferred_element_type=jnp.float32)
    both = sum_feat(jnp.concatenate([gate_part, up_part], axis=1))
    hidden_width = gate_part.shape[1]
    hidden = (jax.nn.silu(both[:, :hidden_width]) * both[:, hidden_width:]).astype(jnp.bfloat16)
    expert_out = jnp.dot(hidden, down_proj[0], preferred_element_type=jnp.float32).astype(
        jnp.bfloat16
    )
    returned = lax.all_to_all(
        expert_out.reshape(expert_count, SLOT, width),
        "exp",
        split_axis=0,
        concat_axis=0,
        tiled=True,
    )
    slot_code = local_codes(route_ids, SLOT, expert_count)
    matches = slot_code[None, :, :] == targets[:, None, None]
    weighted = jnp.sum(jnp.where(matches, route_weights[None, :, :], 0.0), axis=2)
    returned_rows = returned.reshape(capacity, width).astype(jnp.float32)
    moe_out = jnp.einsum("cr,cd->rd", weighted, returned_rows, precision=lax.Precision.HIGHEST)

    for h in range(1, HALVES):
        acts.append(activations(h))
    summed = jnp.concatenate([rebuild(a) for a in acts], axis=0)
    chosen = summed[:, width : width + clamp_count]
    change = clamp_values.astype(jnp.float32)[None, :] - chosen
    shift = jnp.dot(change, rows_dec.astype(jnp.float32), precision=lax.Precision.HIGHEST)
    error_term = moe_out - summed[:, :width] - dec_bias
    steered = moe_out + shift
    return (error_term, steered)


def solution(mesh):
    placed = (
        P("exp", "feat"),
        P("exp", None),
        P("exp", None),
        P("exp", "feat", None),
        P("exp", "feat", None),
        P("exp", None, "feat"),
        P("feat", "exp"),
        P("exp"),
        P("exp", "feat"),
        P("feat"),
        P(),
        P(),
    )
    return jax.shard_map(
        local,
        mesh=mesh,
        in_specs=placed,
        out_specs=(P("exp", "feat"), P("exp", "feat")),
        check_vma=False,
    )
```

time: 334 us -> 228 us (0.68)
  waiting for transfers between devices: 202 us -> 69.4 us
  blocking collectives: 33.7 us -> 0 us
  starting transfers between devices: 5.92 us -> 36.1 us
  matrix products: 47.9 us -> 72.8 us
  Pallas kernels: 0 us -> 13.5 us
  local copies, waits for them, and re-layouts: 23.2 us -> 11.4 us
    psum x1, waiting for transfers between devices: 115 us -> 0.01 us  [local(): rows_dec = lax.psum(decoder_rows(dec_weight, safe_ids, inside), 'exp')]
    ppermute x0 -> x25, waiting for transfers between devices: none -> 69.3 us  [swap(): return lax.ppermute(x, axis, [(i, i ^ mask) for i in range(size)])]
    reduce_scatter x1 -> x0, waiting for transfers between devices: 59.7 us -> none  [local(): lax.psum_scatter(jnp.concatenate([rebuilt_rows, shift_part], axis=1), 'ex...]
    all_to_all x1 -> x0, blocking collectives: 33.7 us -> none  [local(): lax.all_to_all(outgoing.reshape(expert_count, SLOT, shard_width), 'exp',...]
    dot_general x4 -> x19, matrix products: 33.3 us -> 64.1 us  [the longest x8 32.5 us: activations(): jnp.dot(all_tokens[h], enc_weight[:, c * step:(c + 1) * step], preferred_...]
    ppermute x0 -> x25, starting transfers between devices: none -> 29.9 us  [swap(): return lax.ppermute(x, axis, [(i, i ^ mask) for i in range(size)])]
    all_to_all x1, waiting for transfers between devices: 20.6 us -> 0.01 us  [local(): lax.all_to_all(expert_out.reshape(expert_count, SLOT, width), 'exp', spli...]
    gather x2 -> x0, local copies, waits for them, and re-layouts: 17.8 us -> none  [the longest x1 15.3 us: local(): rows_dec = jnp.take(dec_weight, safe_ids, axis=0).astype(jnp.float32)]
  transfers between devices with their start and end apart: 4 -> 27, of which waited for: 4 -> 12; matrix products, arithmetic and copies ran while one was open for 9% -> 35% of each run, Pallas kernels for 0% -> 6%
where the time goes in v1:
time: 228 us; the launch traced here: 227 us
  matrix products  72.8 us (32%)
  waiting for transfers between devices  69.4 us (30%)
  starting transfers between devices  36.1 us (16%)
  between operations  14.8 us (6%)
  Pallas kernels  13.5 us (6%)
  local copies, waits for them, and re-layouts  11.4 us (5%)
  other arithmetic  9.33 us (4%)
    ppermute x25, waiting for transfers between devices, swap(): return lax.ppermute(x, axis, [(i, i ^ mask) for i in range(size)])  69.3 us
    dot_general x8, matrix products, activations(): jnp.dot(all_tokens[h], enc_weight[:, c * step:(c + 1) * step], preferred_...  32.5 us
    ppermute x25, starting transfers between devices, swap(): return lax.ppermute(x, axis, [(i, i ^ mask) for i in range(size)])  29.9 us
    dot_general x4, matrix products, rebuild(): jnp.dot(act, dec_weight[span], preferred_element_type=jnp.float32)  25.9 us
    pallas_call x1, Pallas kernels, decoder_rows(): pl.pallas_call(rows_kernel, out_shape=jax.ShapeDtypeStruct((count, width)...  13.5 us
    unnamed x77, local copies, waits for them, and re-layouts  10.7 us
    all_to_all x1, starting transfers between devices, local(): lax.all_to_all(expert_out.reshape(expert_count, SLOT, width), 'exp', spli...  6.19 us
  transfers between devices with their start and end apart: 27, of which 12 were waited for; matrix products, arithmetic and copies ran while one was open for 35% of the time, Pallas kernels for 6%

profile of v1, /device:TPU:0, one launch (start us, length us, event | category | flops | bytes accessed | tf_op | source)
XLA Modules:
  0.0 227.3 jit_solution(16643340528667128414)
XLA Ops:
  7.2 0.7 convert_element_type.147
  8.0 0.9 fusion.75
  8.9 4.1 %collective-permute-start = (bf16[8,3712]{1,0:T(8,128)(2,1)S(1)}, bf16[8,3712]{1,0:T(8,128)(2,1)S(1)}, u32[]{:S(2)}, u32[]{:S(2)}) collective-permute-start(bf16[8,3712]{1,0:T(8,128)(2,1)S(1)} %get-tuple-element.4), channel_id=1, source_target_pairs={{0,16},{2,18},{4,20},{6,22},{8,24},{10,26},{12,28},{14,30},{16,0},... | collective-permute-start | bytes 178184 | tf_op jit(solution)/shard_map/ppermute | solution.py:18
  13.1 0.7 compare_and_fusion
  13.9 9.3 %copy-done = bf16[4096,3584]{1,0:T(8,128)(2,1)S(1)} copy-done((bf16[4096,3584]{1,0:T(8,128)(2,1)S(1)}, bf16[4096,3584]{1,0:T(8,128)(2,1)}, u32[]{:S(2)}) %copy-start) | copy-done | bytes 29360152
  23.3 13.5 %shard_map.140 = bf16[64,3584]{1,0:T(8,128)(2,1)} custom-call(s32[64]{0:T(128)S(1)} %get-tuple-element.23.ids_ref, bf16[64,1024]{1,0:T(8,128)(2,1)S(1)} %fusion.69.pick_ref, bf16[4096,3584]{1,0:T(8,128)(2,1)S(1)} %copy-done), custom_call_target="tpu_custom_call" | custom-call | flops 469762048 | bytes 7340032 | tf_op jit(solution)/shard_map/pallas_call | solution.py:78
  36.8 0.3 iota_compare_fusion
  38.2 1.9 collective-permute-start.1
  40.4 3.9 %collective-permute-done.1 = bf16[16,3712]{1,0:T(8,128)(2,1)S(1)} collective-permute-done((bf16[16,3712]{1,0:T(8,128)(2,1)S(1)}, bf16[16,3712]{1,0:T(8,128)(2,1)S(1)}, u32[]{:S(2)}, u32[]{:S(2)}) %collective-permute-start.1) | collective-permute-done | bytes 118816 | tf_op jit(solution)/shard_map/ppermute | solution.py:18
  44.3 1.6 collective-permute-start.2
  45.9 1.2 collective-permute-start.6
  47.2 5.5 %collective-permute-done.2 = bf16[32,3712]{1,0:T(8,128)(2,1)S(1)} collective-permute-done((bf16[32,3712]{1,0:T(8,128)(2,1)S(1)}, bf16[32,3712]{1,0:T(8,128)(2,1)S(1)}, u32[]{:S(2)}, u32[]{:S(2)}) %collective-permute-start.2) | collective-permute-done | bytes 237600 | tf_op jit(solution)/shard_map/ppermute | solution.py:18
  52.8 2.6 %collective-permute-done.6 = bf16[32,3712]{1,0:T(8,128)(2,1)S(1)} collective-permute-done((bf16[32,3712]{1,0:T(8,128)(2,1)S(1)}, bf16[32,3712]{1,0:T(8,128)(2,1)S(1)}, u32[]{:S(2)}, u32[]{:S(2)}) %collective-permute-start.6) | collective-permute-done | bytes 237600 | tf_op jit(solution)/shard_map/ppermute | solution.py:18
  55.7 1.7 collective-permute-done.7
  57.5 5.3 %fusion.109 = (bf16[128,1024]{1,0:T(8,128)(2,1)}, f32[128,1024]{1,0:T(8,128)}) fusion(bf16[3584,4096]{1,0:T(8,128)(2,1)} %param.19, bf16[128,3712]{1,0:T(8,128)(2,1)S(1)} %constant_dynamic-update-slice_fusion), kind=kOutput, calls=%fused_computation.181 | convolution fusion | flops 939655168 | bytes 9043968 | tf_op jit(solution)/shard_map/dot_general | solution.py:169
  62.7 5.3 %fusion.108 = (bf16[128,1024]{1,0:T(8,128)(2,1)}, f32[128,1024]{1,0:T(8,128)}) fusion(bf16[3584,4096]{1,0:T(8,128)(2,1)} %param.19, bf16[128,3712]{1,0:T(8,128)(2,1)S(1)} %constant_dynamic-update-slice_fusion.5), kind=kOutput, calls=%fused_computation.180 | convolution fusion | flops 939655168 | bytes 9043968 | tf_op jit(solution)/shard_map/dot_general | solution.py:169
  68.1 5.3 %fusion.107 = (bf16[128,1024]{1,0:T(8,128)(2,1)}, f32[128,1024]{1,0:T(8,128)}) fusion(bf16[3584,4096]{1,0:T(8,128)(2,1)} %param.19, bf16[128,3712]{1,0:T(8,128)(2,1)S(1)} %constant_dynamic-update-slice_fusion), kind=kOutput, calls=%fused_computation.179 | convolution fusion | flops 939655168 | bytes 9043968 | tf_op jit(solution)/shard_map/dot_general | solution.py:169
  73.3 5.3 %fusion.106 = (bf16[128,1024]{1,0:T(8,128)(2,1)}, f32[128,1024]{1,0:T(8,128)}) fusion(bf16[3584,4096]{1,0:T(8,128)(2,1)} %param.19, bf16[128,3712]{1,0:T(8,128)(2,1)S(1)} %constant_dynamic-update-slice_fusion.5), kind=kOutput, calls=%fused_computation.178 | convolution fusion | flops 939655168 | bytes 9043968 | tf_op jit(solution)/shard_map/dot_general | solution.py:169
  78.6 5.3 %fusion.105 = (bf16[128,1024]{1,0:T(8,128)(2,1)}, f32[128,1024]{1,0:T(8,128)}) fusion(bf16[3584,4096]{1,0:T(8,128)(2,1)} %param.19, bf16[128,3712]{1,0:T(8,128)(2,1)S(1)} %constant_dynamic-update-slice_fusion), kind=kOutput, calls=%fused_computation.177 | convolution fusion | flops 939655168 | bytes 9043968 | tf_op jit(solution)/shard_map/dot_general | solution.py:169
  83.9 2.0 fusion.104
  86.0 2.0 fusion.103
  88.0 2.0 fusion.102
  90.1 0.4 fusion.74
  90.4 0.4 convert_reduce_fusion
  91.0 0.4 fusion.57
  91.5 1.5 collective-permute-start.11
  93.1 0.5 collective-permute-start.19
  93.6 1.9 fusion.36
  95.5 4.4 %fusion.10 = f32[128,1024]{1,0:T(8,128)S(1)} fusion(bf16[128,3584]{1,0:T(8,128)(2,1)S(1)} %fusion.36, bf16[1,3584,1024]{2,1,0:T(8,128)(2,1)} %param.17), kind=kOutput, calls=%fused_computation.10 | convolution fusion | flops 939524096 | bytes 8781824 | tf_op jit(solution)/shard_map/dot_general | solution.py:191
  100.0 1.1 fusion.12
  101.2 1.6 collective-permute-start.8
  102.8 0.5 collective-permute-start.9
  103.3 1.5 collective-permute-start.17
  104.8 0.5 collective-permute-start.12
  105.3 1.2 collective-permute-done.19
  106.6 1.5 collective-permute-start.20
  108.2 26.4 %collective-permute-done.12 = bf16[128,1024]{1,0:T(8,128)(2,1)S(1)} collective-permute-done((bf16[128,1024]{1,0:T(8,128)(2,1)S(1)}, bf16[128,1024]{1,0:T(8,128)(2,1)S(1)}, u32[]{:S(2)}, u32[]{:S(2)}) %collective-permute-start.12) | collective-permute-done | bytes 262176 | tf_op jit(solution)/shard_map/ppermute | solution.py:18
  134.6 1.5 collective-permute-start.10
  136.1 4.1 %collective-permute-done.20 = bf16[128,1024]{1,0:T(8,128)(2,1)S(1)} collective-permute-done((bf16[128,1024]{1,0:T(8,128)(2,1)S(1)}, bf16[128,1024]{1,0:T(8,128)(2,1)S(1)}, u32[]{:S(2)}, u32[]{:S(2)}) %collective-permute-start.20) | collective-permute-done | bytes 262176 | tf_op jit(solution)/shard_map/ppermute | solution.py:18
  140.3 1.5 collective-permute-start.18
  142.0 6.5 %fusion = f32[128,3584]{1,0:T(8,128)S(1)} fusion(bf16[4096,3584]{1,0:T(8,128)(2,1)} %dec_ref.1, bf16[128,1024]{1,0:T(8,128)(2,1)S(1)} %get-tuple-element.20, bf16[128,1024]{1,0:T(8,128)(2,1)S(1)} %get-tuple-element.18), kind=kOutput, calls=%fused_computation | convolution fusion | flops 1880096768 | bytes 17039360 | tf_op jit(solution)/shard_map/dot_general | solution.py:184
  148.7 2.0 collective-permute-done.18
  151.6 6.4 %fusion.33 = f32[128,3584]{1,0:T(8,128)S(1)} fusion(f32[128,3584]{1,0:T(8,128)S(1)} %fusion, bf16[4096,3584]{1,0:T(8,128)(2,1)} %dec_ref.1, bf16[128,1024]{1,0:T(8,128)(2,1)S(1)} %get-tuple-element.16, bf16[128,1024]{1,0:T(8,128)(2,1)S(1)} %get-tuple-element.14), kind=kOutput, calls=%fused_computation.32 | convolution fusion | flops 1880555520 | bytes 18874368 | tf_op jit(solution)/shard_map/dot_general | solution.py:184
  158.0 0.8 fusion.47
  159.2 6.5 %fusion.2 = f32[128,3584]{1,0:T(8,128)S(1)} fusion(bf16[4096,3584]{1,0:T(8,128)(2,1)} %dec_ref.1, bf16[128,1024]{1,0:T(8,128)(2,1)S(1)} %get-tuple-element.21, bf16[128,1024]{1,0:T(8,128)(2,1)S(1)} %get-tuple-element.19), kind=kOutput, calls=%fused_computation.2 | convolution fusion | flops 1880096768 | bytes 17039360 | tf_op jit(solution)/shard_map/dot_general | solution.py:184
  165.7 6.5 %fusion.30 = f32[128,3584]{1,0:T(8,128)S(1)} fusion(f32[128,3584]{1,0:T(8,128)S(1)} %fusion.2, bf16[4096,3584]{1,0:T(8,128)(2,1)} %dec_ref.1, bf16[128,1024]{1,0:T(8,128)(2,1)S(1)} %get-tuple-element.17, bf16[128,1024]{1,0:T(8,128)(2,1)S(1)} %get-tuple-element.15), kind=kOutput, calls=%fused_computation.31 | convolution fusion | flops 1880555520 | bytes 18874368 | tf_op jit(solution)/shard_map/dot_general | solution.py:184
  172.6 0.9 copy-done.1
  173.5 0.8 fusion.48
  174.3 0.5 collective-permute-start.13
  175.0 2.1 fusion.40
  177.1 6.2 %all-to-all-start = ((bf16[16,8,3584]{2,1,0:T(8,128)(2,1)}), bf16[16,8,3584]{2,1,0:T(8,128)(2,1)S(1)}, u32[]{:S(2)}, u32[]{:S(2)}) async-start(bf16[16,8,3584]{2,1,0:T(8,128)(2,1)} %fusion.40), calls=%async_computation | async-start | bytes 1835008 | tf_op jit(solution)/shard_map/all_to_all | solution.py:198
  183.3 1.1 fusion.44
  184.4 2.0 collective-permute-start.22
  186.4 1.3 fusion.46
  187.9 11.5 %collective-permute-done.22 = bf16[32,3712]{1,0:T(8,128)(2,1)S(1)} collective-permute-done((bf16[32,3712]{1,0:T(8,128)(2,1)S(1)}, bf16[32,3712]{1,0:T(8,128)(2,1)S(1)}, u32[]{:S(2)}, u32[]{:S(2)}) %collective-permute-start.22) | collective-permute-done | bytes 237600 | tf_op jit(solution)/shard_map/ppermute | solution.py:18
  199.4 1.2 collective-permute-start.23
  200.6 5.8 %collective-permute-done.14 = bf16[32,3712]{1,0:T(8,128)(2,1)S(1)} collective-permute-done((bf16[32,3712]{1,0:T(8,128)(2,1)S(1)}, bf16[32,3712]{1,0:T(8,128)(2,1)S(1)}, u32[]{:S(2)}, u32[]{:S(2)}) %collective-permute-start.14) | collective-permute-done | bytes 237600 | tf_op jit(solution)/shard_map/ppermute | solution.py:18
  206.5 1.5 collective-permute-start.15
  208.1 2.4 %collective-permute-start.24 = (bf16[8,3712]{1,0:T(8,128)(2,1)S(1)}, bf16[8,3712]{1,0:T(8,128)(2,1)S(1)}, u32[]{:S(2)}, u32[]{:S(2)}) collective-permute-start(bf16[8,3712]{1,0:T(8,128)(2,1)S(1)} %slice.308), channel_id=1, source_target_pairs={{0,16},{2,18},{4,20},{6,22},{8,24},{10,26},{12,28},{14,30},{16,0},... | collective-permute-start | bytes 178184 | tf_op jit(solution)/shard_map/ppermute | solution.py:18
  210.5 1.5 collective-permute-done.15
  212.1 2.1 collective-permute-start.16
  214.2 3.0 %collective-permute-done.16 = bf16[8,3712]{1,0:T(8,128)(2,1)S(1)} collective-permute-done((bf16[8,3712]{1,0:T(8,128)(2,1)S(1)}, bf16[8,3712]{1,0:T(8,128)(2,1)S(1)}, u32[]{:S(2)}, u32[]{:S(2)}) %collective-permute-start.16) | collective-permute-done | bytes 59424 | tf_op jit(solution)/shard_map/ppermute | solution.py:18
  217.3 1.2 fusion.73
  218.4 2.0 convolution_add_fusion.1
  (152 shorter events, 5.2 us)
Async XLA Ops:
  7.2 211.3 %all-reduce.4.cloned.1.call-start = ((), (), s32[]{:S(2)}) async-start(), calls=%async_computation.1 | async-start | bytes 917504 | tf_op jit(solution)/shard_map/psum | solution.py:142
  8.9 29.2 %collective-permute-start = (bf16[8,3712]{1,0:T(8,128)(2,1)S(1)}, bf16[8,3712]{1,0:T(8,128)(2,1)S(1)}, u32[]{:S(2)}, u32[]{:S(2)}) collective-permute-start(bf16[8,3712]{1,0:T(8,128)(2,1)S(1)} %get-tuple-element.4), channel_id=1, source_target_pairs={{0,16},{2,18},{4,20},{6,22},{8,24},{10,26},{12,28},{14,30},{16,0},... | collective-permute-start | bytes 178184 | tf_op jit(solution)/shard_map/ppermute | solution.py:18
  13.0 27.0 %collective-permute-start.4 = (bf16[8,3712]{1,0:T(8,128)(2,1)S(1)}, bf16[8,3712]{1,0:T(8,128)(2,1)S(1)}, u32[]{:S(2)}, u32[]{:S(2)}) collective-permute-start(bf16[8,3712]{1,0:T(8,128)(2,1)S(1)} %get-tuple-element.7), channel_id=1, source_target_pairs={{0,16},{2,18},{4,20},{6,22},{8,24},{10,26},{12,28},{14,30},{16,0},... | collective-permute-start | bytes 178184 | tf_op jit(solution)/shard_map/ppermute | solution.py:18
  13.9 9.4 %copy-start = (bf16[4096,3584]{1,0:T(8,128)(2,1)S(1)}, bf16[4096,3584]{1,0:T(8,128)(2,1)}, u32[]{:S(2)}) copy-start(bf16[4096,3584]{1,0:T(8,128)(2,1)} %dec_ref.1) | copy-start | bytes 88080384
  23.3 13.9 %copy-start.12 = (s32[16,8]{0,1:T(8,128)S(1)}, s32[16,8]{0,1:T(8,128)}, u32[]{:S(2)}) copy-start(s32[16,8]{0,1:T(8,128)} %param.14) | copy-start | bytes 1540
  23.3 14.0 %copy-start.22 = (s32[16]{0:T(128)S(1)}, s32[16]{0:T(128)}, u32[]{:S(2)}) copy-start(s32[16]{0:T(128)} %constant.62.clone) | copy-start | bytes 196
  23.3 14.0 %copy-start.13 = (f32[4096]{0:T(1024)S(1)}, f32[4096]{0:T(1024)}, u32[]{:S(2)}) copy-start(f32[4096]{0:T(1024)} %param.20) | copy-start | bytes 49156
  23.3 14.7 %copy-start.14 = (f32[16,8]{0,1:T(8,128)S(1)}, f32[16,8]{0,1:T(8,128)}, u32[]{:S(2)}) copy-start(f32[16,8]{0,1:T(8,128)} %param.15) | copy-start | bytes 1540
  23.3 14.7 %copy-start.21 = (bf16[64]{0:T(256)(128)(2,1)S(1)}, bf16[64]{0:T(256)(128)(2,1)}, u32[]{:S(2)}) copy-start(bf16[64]{0:T(256)(128)(2,1)} %param.24) | copy-start | bytes 388
  38.2 6.1 %collective-permute-start.1 = (bf16[16,3712]{1,0:T(8,128)(2,1)S(1)}, bf16[16,3712]{1,0:T(8,128)(2,1)S(1)}, u32[]{:S(2)}, u32[]{:S(2)}) collective-permute-start(bf16[16,3712]{1,0:T(8,128)(2,1)S(1)} %pad_maximum_fusion.19), channel_id=1, source_target_pairs={{0,8},{2,10},{4,12},{6,14},{8,0},{10,2},{12,4},{14,6},{16,24},{18,... | collective-permute-start | bytes 356360 | tf_op jit(solution)/shard_map/ppermute | solution.py:18
  40.1 5.8 %collective-permute-start.5 = (bf16[16,3712]{1,0:T(8,128)(2,1)S(1)}, bf16[16,3712]{1,0:T(8,128)(2,1)S(1)}, u32[]{:S(2)}, u32[]{:S(2)}) collective-permute-start(bf16[16,3712]{1,0:T(8,128)(2,1)S(1)} %pad_maximum_fusion.20), channel_id=1, source_target_pairs={{0,8},{2,10},{4,12},{6,14},{8,0},{10,2},{12,4},{14,6},{16,24},{18,... | collective-permute-start | bytes 356360 | tf_op jit(solution)/shard_map/ppermute | solution.py:18
  44.3 8.3 %collective-permute-start.2 = (bf16[32,3712]{1,0:T(8,128)(2,1)S(1)}, bf16[32,3712]{1,0:T(8,128)(2,1)S(1)}, u32[]{:S(2)}, u32[]{:S(2)}) collective-permute-start(bf16[32,3712]{1,0:T(8,128)(2,1)S(1)} %pad_maximum_fusion.17), channel_id=1, source_target_pairs={{0,4},{2,6},{4,0},{6,2},{8,12},{10,14},{12,8},{14,10},{16,20},{18,... | collective-permute-start | bytes 712712 | tf_op jit(solution)/shard_map/ppermute | solution.py:18
  45.9 9.5 %collective-permute-start.6 = (bf16[32,3712]{1,0:T(8,128)(2,1)S(1)}, bf16[32,3712]{1,0:T(8,128)(2,1)S(1)}, u32[]{:S(2)}, u32[]{:S(2)}) collective-permute-start(bf16[32,3712]{1,0:T(8,128)(2,1)S(1)} %pad_maximum_fusion.18), channel_id=1, source_target_pairs={{0,4},{2,6},{4,0},{6,2},{8,12},{10,14},{12,8},{14,10},{16,20},{18,... | collective-permute-start | bytes 712712 | tf_op jit(solution)/shard_map/ppermute | solution.py:18
  52.7 2.9 %collective-permute-start.3 = (bf16[64,3712]{1,0:T(8,128)(2,1)S(1)}, bf16[64,3712]{1,0:T(8,128)(2,1)S(1)}, u32[]{:S(2)}, u32[]{:S(2)}) collective-permute-start(bf16[64,3712]{1,0:T(8,128)(2,1)S(1)} %pad_maximum_fusion.7), channel_id=1, source_target_pairs={{0,2},{2,0},{4,6},{6,4},{8,10},{10,8},{12,14},{14,12},{16,18},{18,... | collective-permute-start | bytes 1425416 | tf_op jit(solution)/shard_map/ppermute | solution.py:18
  55.5 1.9 collective-permute-start.7
  55.7 30.3 %copy-start.2 = (bf16[128,3712]{1,0:T(8,128)(2,1)}, bf16[128,3712]{1,0:T(8,128)(2,1)S(1)}, u32[]{:S(2)}) copy-start(bf16[128,3712]{1,0:T(8,128)(2,1)S(1)} %constant_dynamic-update-slice_fusion) | copy-start | bytes 2850820
  57.4 26.5 %slice-start.2 = ((s8[29360128]{0:T(1024)(128)(4,1)}), s8[4194304]{0:T(1024)(128)(4,1)S(1)}, s32[]{:S(2)}) async-start(s8[29360128]{0:T(1024)(128)(4,1)} %bitcast.30), calls=%async_computation.4 | async-start | bytes 8388608
  57.4 26.4 %slice-start.3 = ((s8[29360128]{0:T(1024)(128)(4,1)}), s8[4194304]{0:T(1024)(128)(4,1)S(1)}, s32[]{:S(2)}) async-start(s8[29360128]{0:T(1024)(128)(4,1)} %bitcast.30), calls=%async_computation.5 | async-start | bytes 8388608
  62.7 21.2 %slice-start.4 = ((s8[29360128]{0:T(1024)(128)(4,1)}), s8[4194304]{0:T(1024)(128)(4,1)S(1)}, s32[]{:S(2)}) async-start(s8[29360128]{0:T(1024)(128)(4,1)} %bitcast.30), calls=%async_computation.6 | async-start | bytes 8388608
  68.1 15.8 %slice-start.5 = ((s8[29360128]{0:T(1024)(128)(4,1)}), s8[4194304]{0:T(1024)(128)(4,1)S(1)}, s32[]{:S(2)}) async-start(s8[29360128]{0:T(1024)(128)(4,1)} %bitcast.30), calls=%async_computation.7 | async-start | bytes 8388608
  68.1 15.8 %slice-start.6 = ((s8[29360128]{0:T(1024)(128)(4,1)}), s8[4194304]{0:T(1024)(128)(4,1)S(1)}, s32[]{:S(2)}) async-start(s8[29360128]{0:T(1024)(128)(4,1)} %bitcast.30), calls=%async_computation.8 | async-start | bytes 8388608
  73.3 10.6 %slice-start.7 = ((s8[29360128]{0:T(1024)(128)(4,1)}), s8[4194304]{0:T(1024)(128)(4,1)S(1)}, s32[]{:S(2)}) async-start(s8[29360128]{0:T(1024)(128)(4,1)} %bitcast.30), calls=%async_computation.9 | async-start | bytes 8388608
  78.6 5.3 %slice-start.8 = ((s8[29360128]{0:T(1024)(128)(4,1)}), s8[4194304]{0:T(1024)(128)(4,1)S(1)}, s32[]{:S(2)}) async-start(s8[29360128]{0:T(1024)(128)(4,1)} %bitcast.30), calls=%async_computation.10 | async-start | bytes 8388608
  91.5 13.3 %collective-permute-start.11 = (bf16[128,1024]{1,0:T(8,128)(2,1)}, bf16[128,1024]{1,0:T(8,128)(2,1)S(1)}, u32[]{:S(2)}, u32[]{:S(2)}) collective-permute-start(bf16[128,1024]{1,0:T(8,128)(2,1)} %get-tuple-element.30), channel_id=1, source_target_pairs={{0,1},{1,0},{2,3},{3,2},{4,5},{5,4},{6,7},{7,6},{8,9},{9,8},{10,11... | collective-permute-start | bytes 786440 | tf_op jit(solution)/shard_map/ppermute | solution.py:18
  93.1 13.5 %collective-permute-start.19 = (bf16[128,1024]{1,0:T(8,128)(2,1)}, bf16[128,1024]{1,0:T(8,128)(2,1)S(1)}, u32[]{:S(2)}, u32[]{:S(2)}) collective-permute-start(bf16[128,1024]{1,0:T(8,128)(2,1)} %get-tuple-element.28), channel_id=1, source_target_pairs={{0,1},{1,0},{2,3},{3,2},{4,5},{5,4},{6,7},{7,6},{8,9},{9,8},{10,11... | collective-permute-start | bytes 786440 | tf_op jit(solution)/shard_map/ppermute | solution.py:18
  93.6 6.3 %slice-start = ((s8[7340032]{0:T(1024)(128)(4,1)}), s8[4194304]{0:T(1024)(128)(4,1)S(1)}, s32[]{:S(2)}) async-start(s8[7340032]{0:T(1024)(128)(4,1)} %bitcast.28), calls=%async_computation.2 | async-start | bytes 8388608
  95.5 4.4 %slice-start.1 = ((s8[7340032]{0:T(1024)(128)(4,1)}), s8[3145728]{0:T(1024)(128)(4,1)S(1)}, s32[]{:S(2)}) async-start(s8[7340032]{0:T(1024)(128)(4,1)} %bitcast.28), calls=%async_computation.3 | async-start | bytes 6291456
  99.9 2.9 %copy-start.18 = (bf16[128,1024]{1,0:T(8,128)(2,1)S(1)}, bf16[128,1024]{1,0:T(8,128)(2,1)}, u32[]{:S(2)}) copy-start(bf16[128,1024]{1,0:T(8,128)(2,1)} %get-tuple-element.38) | copy-start | bytes 786436
  99.9 3.4 %copy-start.17 = (bf16[128,1024]{1,0:T(8,128)(2,1)S(1)}, bf16[128,1024]{1,0:T(8,128)(2,1)}, u32[]{:S(2)}) copy-start(bf16[128,1024]{1,0:T(8,128)(2,1)} %get-tuple-element.36) | copy-start | bytes 786436
  99.9 4.9 %copy-start.20 = (bf16[128,1024]{1,0:T(8,128)(2,1)S(1)}, bf16[128,1024]{1,0:T(8,128)(2,1)}, u32[]{:S(2)}) copy-start(bf16[128,1024]{1,0:T(8,128)(2,1)} %get-tuple-element.26) | copy-start | bytes 786436
  100.0 6.6 %copy-start.19 = (bf16[128,1024]{1,0:T(8,128)(2,1)S(1)}, bf16[128,1024]{1,0:T(8,128)(2,1)}, u32[]{:S(2)}) copy-start(bf16[128,1024]{1,0:T(8,128)(2,1)} %get-tuple-element.24) | copy-start | bytes 786436
  100.0 8.1 %copy-start.9 = (f32[128,1024]{1,0:T(8,128)S(1)}, f32[128,1024]{1,0:T(8,128)}, u32[]{:S(2)}) copy-start(f32[128,1024]{1,0:T(8,128)} %get-tuple-element.31) | copy-start | bytes 1572868
  100.0 8.1 %copy-start.10 = (f32[128,1024]{1,0:T(8,128)S(1)}, f32[128,1024]{1,0:T(8,128)}, u32[]{:S(2)}) copy-start(f32[128,1024]{1,0:T(8,128)} %get-tuple-element.29) | copy-start | bytes 1572868
  100.0 34.7 %copy-start.16 = (bf16[128,1024]{1,0:T(8,128)(2,1)S(1)}, bf16[128,1024]{1,0:T(8,128)(2,1)}, u32[]{:S(2)}) copy-start(bf16[128,1024]{1,0:T(8,128)(2,1)} %get-tuple-element.34) | copy-start | bytes 786436
  100.0 40.3 %copy-start.15 = (bf16[128,1024]{1,0:T(8,128)(2,1)S(1)}, bf16[128,1024]{1,0:T(8,128)(2,1)}, u32[]{:S(2)}) copy-start(bf16[128,1024]{1,0:T(8,128)(2,1)} %get-tuple-element.32) | copy-start | bytes 786436
  100.0 41.8 %copy-start.7 = (f32[128,1024]{1,0:T(8,128)S(1)}, f32[128,1024]{1,0:T(8,128)}, u32[]{:S(2)}) copy-start(f32[128,1024]{1,0:T(8,128)} %get-tuple-element.27) | copy-start | bytes 1572868
  100.0 41.7 %copy-start.8 = (f32[128,1024]{1,0:T(8,128)S(1)}, f32[128,1024]{1,0:T(8,128)}, u32[]{:S(2)}) copy-start(f32[128,1024]{1,0:T(8,128)} %get-tuple-element.25) | copy-start | bytes 1572868
  101.2 73.6 %collective-permute-start.8 = (bf16[128,2048]{1,0:T(8,128)(2,1)S(1)}, bf16[128,2048]{1,0:T(8,128)(2,1)S(1)}, u32[]{:S(2)}, u32[]{:S(2)}) collective-permute-start(bf16[128,2048]{1,0:T(8,128)(2,1)S(1)} %fusion.51), channel_id=1, source_target_pairs={{0,1},{1,0},{2,3},{3,2},{4,5},{5,4},{6,7},{7,6},{8,9},{9,8},{10,11... | collective-permute-start | bytes 1572872 | tf_op jit(solution)/shard_map/ppermute | solution.py:18
  102.8 45.7 %collective-permute-start.9 = (bf16[128,1024]{1,0:T(8,128)(2,1)S(1)}, bf16[128,1024]{1,0:T(8,128)(2,1)S(1)}, u32[]{:S(2)}, u32[]{:S(2)}) collective-permute-start(bf16[128,1024]{1,0:T(8,128)(2,1)S(1)} %copy-done.18), channel_id=1, source_target_pairs={{0,1},{1,0},{2,3},{3,2},{4,5},{5,4},{6,7},{7,6},{8,9},{9,8},{10,11... | collective-permute-start | bytes 786440 | tf_op jit(solution)/shard_map/ppermute | solution.py:18
  103.3 45.2 %collective-permute-start.17 = (bf16[128,1024]{1,0:T(8,128)(2,1)S(1)}, bf16[128,1024]{1,0:T(8,128)(2,1)S(1)}, u32[]{:S(2)}, u32[]{:S(2)}) collective-permute-start(bf16[128,1024]{1,0:T(8,128)(2,1)S(1)} %copy-done.17), channel_id=1, source_target_pairs={{0,1},{1,0},{2,3},{3,2},{4,5},{5,4},{6,7},{7,6},{8,9},{9,8},{10,11... | collective-permute-start | bytes 786440 | tf_op jit(solution)/shard_map/ppermute | solution.py:18
  104.8 29.8 %collective-permute-start.12 = (bf16[128,1024]{1,0:T(8,128)(2,1)S(1)}, bf16[128,1024]{1,0:T(8,128)(2,1)S(1)}, u32[]{:S(2)}, u32[]{:S(2)}) collective-permute-start(bf16[128,1024]{1,0:T(8,128)(2,1)S(1)} %copy-done.20), channel_id=1, source_target_pairs={{0,1},{1,0},{2,3},{3,2},{4,5},{5,4},{6,7},{7,6},{8,9},{9,8},{10,11... | collective-permute-start | bytes 786440 | tf_op jit(solution)/shard_map/ppermute | solution.py:18
  106.6 33.7 %collective-permute-start.20 = (bf16[128,1024]{1,0:T(8,128)(2,1)S(1)}, bf16[128,1024]{1,0:T(8,128)(2,1)S(1)}, u32[]{:S(2)}, u32[]{:S(2)}) collective-permute-start(bf16[128,1024]{1,0:T(8,128)(2,1)S(1)} %copy-done.19), channel_id=1, source_target_pairs={{0,1},{1,0},{2,3},{3,2},{4,5},{5,4},{6,7},{7,6},{8,9},{9,8},{10,11... | collective-permute-start | bytes 786440 | tf_op jit(solution)/shard_map/ppermute | solution.py:18
  134.6 14.1 %collective-permute-start.10 = (bf16[128,1024]{1,0:T(8,128)(2,1)S(1)}, bf16[128,1024]{1,0:T(8,128)(2,1)S(1)}, u32[]{:S(2)}, u32[]{:S(2)}) collective-permute-start(bf16[128,1024]{1,0:T(8,128)(2,1)S(1)} %copy-done.16), channel_id=1, source_target_pairs={{0,1},{1,0},{2,3},{3,2},{4,5},{5,4},{6,7},{7,6},{8,9},{9,8},{10,11... | collective-permute-start | bytes 786440 | tf_op jit(solution)/shard_map/ppermute | solution.py:18
  140.3 10.4 %collective-permute-start.18 = (bf16[128,1024]{1,0:T(8,128)(2,1)S(1)}, bf16[128,1024]{1,0:T(8,128)(2,1)S(1)}, u32[]{:S(2)}, u32[]{:S(2)}) collective-permute-start(bf16[128,1024]{1,0:T(8,128)(2,1)S(1)} %copy-done.15), channel_id=1, source_target_pairs={{0,1},{1,0},{2,3},{3,2},{4,5},{5,4},{6,7},{7,6},{8,9},{9,8},{10,11... | collective-permute-start | bytes 786440 | tf_op jit(solution)/shard_map/ppermute | solution.py:18
  142.0 6.5 %copy-start.5 = (f32[128,1024]{1,0:T(8,128)S(1)}, f32[128,1024]{1,0:T(8,128)}, u32[]{:S(2)}) copy-start(f32[128,1024]{1,0:T(8,128)} %get-tuple-element.39) | copy-start | bytes 1572868
  142.0 6.5 %copy-start.6 = (f32[128,1024]{1,0:T(8,128)S(1)}, f32[128,1024]{1,0:T(8,128)}, u32[]{:S(2)}) copy-start(f32[128,1024]{1,0:T(8,128)} %get-tuple-element.37) | copy-start | bytes 1572868
  142.0 8.7 %copy-start.3 = (f32[128,1024]{1,0:T(8,128)S(1)}, f32[128,1024]{1,0:T(8,128)}, u32[]{:S(2)}) copy-start(f32[128,1024]{1,0:T(8,128)} %get-tuple-element.35) | copy-start | bytes 1572868
  142.0 8.7 %copy-start.4 = (f32[128,1024]{1,0:T(8,128)S(1)}, f32[128,1024]{1,0:T(8,128)}, u32[]{:S(2)}) copy-start(f32[128,1024]{1,0:T(8,128)} %get-tuple-element.33) | copy-start | bytes 1572868
  158.8 24.5 %collective-permute-start.21 = (bf16[64,3712]{1,0:T(8,128)(2,1)}, bf16[64,3712]{1,0:T(8,128)(2,1)}, u32[]{:S(2)}, u32[]{:S(2)}) collective-permute-start(bf16[64,3712]{1,0:T(8,128)(2,1)} %fusion.47), channel_id=1, source_target_pairs={{0,2},{2,0},{4,6},{6,4},{8,10},{10,8},{12,14},{14,12},{16,18},{18,... | collective-permute-start | bytes 1425416 | tf_op jit(solution)/shard_map/ppermute | solution.py:18
  159.2 15.8 %slice-start.9 = ((s8[7340032]{0:T(1024)(128)(4,1)}), s8[4194304]{0:T(1024)(128)(4,1)S(1)}, s32[]{:S(2)}) async-start(s8[7340032]{0:T(1024)(128)(4,1)} %bitcast.32), calls=%async_computation.11 | async-start | bytes 8388608
  165.7 9.3 %slice-start.10 = ((s8[7340032]{0:T(1024)(128)(4,1)}), s8[3145728]{0:T(1024)(128)(4,1)S(1)}, s32[]{:S(2)}) async-start(s8[7340032]{0:T(1024)(128)(4,1)} %bitcast.32), calls=%async_computation.12 | async-start | bytes 6291456
  172.2 1.3 copy-start.1
  174.3 12.1 %collective-permute-start.13 = (bf16[64,3712]{1,0:T(8,128)(2,1)}, bf16[64,3712]{1,0:T(8,128)(2,1)S(1)}, u32[]{:S(2)}, u32[]{:S(2)}) collective-permute-start(bf16[64,3712]{1,0:T(8,128)(2,1)} %fusion.48), channel_id=1, source_target_pairs={{0,2},{2,0},{4,6},{6,4},{8,10},{10,8},{12,14},{14,12},{16,18},{18,... | collective-permute-start | bytes 1425416 | tf_op jit(solution)/shard_map/ppermute | solution.py:18
  177.1 40.2 %copy-start.11 = (f32[3584]{0:T(1024)S(1)}, f32[3584]{0:T(1024)}, u32[]{:S(2)}) copy-start(f32[3584]{0:T(1024)} %param.22) | copy-start | bytes 43012
  177.1 40.2 %all-to-all-start = ((bf16[16,8,3584]{2,1,0:T(8,128)(2,1)}), bf16[16,8,3584]{2,1,0:T(8,128)(2,1)S(1)}, u32[]{:S(2)}, u32[]{:S(2)}) async-start(bf16[16,8,3584]{2,1,0:T(8,128)(2,1)} %fusion.40), calls=%async_computation | async-start | bytes 1835008 | tf_op jit(solution)/shard_map/all_to_all | solution.py:198
  184.4 14.9 %collective-permute-start.22 = (bf16[32,3712]{1,0:T(8,128)(2,1)S(1)}, bf16[32,3712]{1,0:T(8,128)(2,1)S(1)}, u32[]{:S(2)}, u32[]{:S(2)}) collective-permute-start(bf16[32,3712]{1,0:T(8,128)(2,1)S(1)} %slice.304), channel_id=1, source_target_pairs={{0,4},{2,6},{4,0},{6,2},{8,12},{10,14},{12,8},{14,10},{16,20},{18,... | collective-permute-start | bytes 712712 | tf_op jit(solution)/shard_map/ppermute | solution.py:18
  187.7 18.7 %collective-permute-start.14 = (bf16[32,3712]{1,0:T(8,128)(2,1)S(1)}, bf16[32,3712]{1,0:T(8,128)(2,1)S(1)}, u32[]{:S(2)}, u32[]{:S(2)}) collective-permute-start(bf16[32,3712]{1,0:T(8,128)(2,1)S(1)} %slice.305), channel_id=1, source_target_pairs={{0,4},{2,6},{4,0},{6,2},{8,12},{10,14},{12,8},{14,10},{16,20},{18,... | collective-permute-start | bytes 712712 | tf_op jit(solution)/shard_map/ppermute | solution.py:18
  199.4 8.6 %collective-permute-start.23 = (bf16[16,3712]{1,0:T(8,128)(2,1)S(1)}, bf16[16,3712]{1,0:T(8,128)(2,1)S(1)}, u32[]{:S(2)}, u32[]{:S(2)}) collective-permute-start(bf16[16,3712]{1,0:T(8,128)(2,1)S(1)} %slice.306), channel_id=1, source_target_pairs={{0,8},{2,10},{4,12},{6,14},{8,0},{10,2},{12,4},{14,6},{16,24},{18,... | collective-permute-start | bytes 356360 | tf_op jit(solution)/shard_map/ppermute | solution.py:18
  206.5 5.5 %collective-permute-start.15 = (bf16[16,3712]{1,0:T(8,128)(2,1)S(1)}, bf16[16,3712]{1,0:T(8,128)(2,1)S(1)}, u32[]{:S(2)}, u32[]{:S(2)}) collective-permute-start(bf16[16,3712]{1,0:T(8,128)(2,1)S(1)} %slice.307), channel_id=1, source_target_pairs={{0,8},{2,10},{4,12},{6,14},{8,0},{10,2},{12,4},{14,6},{16,24},{18,... | collective-permute-start | bytes 356360 | tf_op jit(solution)/shard_map/ppermute | solution.py:18
  208.1 6.1 %collective-permute-start.24 = (bf16[8,3712]{1,0:T(8,128)(2,1)S(1)}, bf16[8,3712]{1,0:T(8,128)(2,1)S(1)}, u32[]{:S(2)}, u32[]{:S(2)}) collective-permute-start(bf16[8,3712]{1,0:T(8,128)(2,1)S(1)} %slice.308), channel_id=1, source_target_pairs={{0,16},{2,18},{4,20},{6,22},{8,24},{10,26},{12,28},{14,30},{16,0},... | collective-permute-start | bytes 178184 | tf_op jit(solution)/shard_map/ppermute | solution.py:18
  212.1 5.2 %collective-permute-start.16 = (bf16[8,3712]{1,0:T(8,128)(2,1)S(1)}, bf16[8,3712]{1,0:T(8,128)(2,1)S(1)}, u32[]{:S(2)}, u32[]{:S(2)}) collective-permute-start(bf16[8,3712]{1,0:T(8,128)(2,1)S(1)} %slice.309), channel_id=1, source_target_pairs={{0,16},{2,18},{4,20},{6,22},{8,24},{10,26},{12,28},{14,30},{16,0},... | collective-permute-start | bytes 178184 | tf_op jit(solution)/shard_map/ppermute | solution.py:18
Sparse Core Ops, SparseCore 0:
  36.9 91.3 all-reduce.3

commit v2 on v1

v2 whole, which is shorter than its diff:
```python
import functools

import jax
import jax.numpy as jnp
from jax import lax
from jax.experimental import pallas as pl
from jax.experimental.pallas import tpu as pltpu
from jax.sharding import PartitionSpec as P

SLOT = 8
SPLIT = (8, 8)
CUTS = ((0, 2, 4), (0, 2, 4))
LANES = 128
GROUP = 16
VMEM_LIMIT = 40 * 1024 * 1024


def swap(x, axis, mask):
    size = lax.axis_size(axis)
    return lax.ppermute(x, axis, [(i, i ^ mask) for i in range(size)])


def doublings(size):
    masks = []
    while size > 1:
        size //= 2
        masks.append(size)
    return masks


def gather_blocks(x):
    for mask in doublings(lax.axis_size("exp")):
        x = jnp.concatenate([x, swap(x, "exp", mask)], axis=0)
    return x


def block_offsets(size):
    offsets = [0]
    for mask in doublings(size):
        offsets = offsets + [o ^ mask for o in offsets]
    return offsets


def scatter_sum(keep, send):
    masks = doublings(lax.axis_size("exp"))[::-1]
    for mask in masks[:-1]:
        x = keep + swap(send, "exp", mask).astype(jnp.float32)
        half = x.shape[0] // 2
        keep, send = x[:half], x[half:].astype(jnp.bfloat16)
    return keep + swap(send, "exp", masks[-1]).astype(jnp.float32)


def share_all(x):
    for mask in doublings(lax.axis_size("exp"))[::-1]:
        x = x + swap(x, "exp", mask)
    return x


def exchange(own, send):
    masks = doublings(lax.axis_size("feat"))
    for mask in masks[:-1]:
        own = own + swap(send, "feat", mask).astype(jnp.float32)
        send = own.astype(jnp.bfloat16)
    return own, swap(send, "feat", masks[-1])


def tile_of(size):
    return 256 if size % 256 == 0 else LANES


def whole():
    return pl.BlockSpec(memory_space=pltpu.VMEM)


def untouched():
    return pl.BlockSpec(memory_space=pl.ANY)


def encode_kernel(tile, tokens_ref, weight_ref, *refs):
    own_ref, send_ref = refs[-2:]
    depth = weight_ref.shape[0]
    part = jnp.dot(tokens_ref[:, :depth], weight_ref[...], preferred_element_type=jnp.float32)
    columns = pl.ds(pl.multiple_of(pl.program_id(0) * tile, tile), tile)
    own_ref[:, columns] = part
    send_ref[:, columns] = part.astype(send_ref.dtype)


def encode(rows, weight, first, last, after):
    depth, count = weight.shape[0], last - first
    tile = tile_of(count)
    base = first // tile
    return pl.pallas_call(
        functools.partial(encode_kernel, tile),
        grid=(count // tile,),
        out_shape=[
            jax.ShapeDtypeStruct((rows.shape[0], count), jnp.float32),
            jax.ShapeDtypeStruct((rows.shape[0], count), jnp.bfloat16),
        ],
        in_specs=[whole(), pl.BlockSpec((depth, tile), lambda j: (0, base + j))]
        + [untouched()] * len(after),
        out_specs=[whole(), whole()],
        compiler_params=pltpu.CompilerParams(vmem_limit_bytes=VMEM_LIMIT),
        cost_estimate=pl.CostEstimate(
            flops=rows.shape[0] * depth * count // 4,
            bytes_accessed=depth * count // 4,
            transcendentals=0,
        ),
    )(rows, weight, *after)


def decode_kernel(tile, tiles, first, last, own_ref, recv_ref, bias_ref, pick_ref, weight_ref, *refs):
    act = refs[-1]
    step = pl.program_id(0)
    width = tile * tiles

    @pl.when(step == 0)
    def _():
        pre = own_ref[...] + recv_ref[...].astype(jnp.float32) + bias_ref[...]
        act[...] = jnp.maximum(pre, 0.0).astype(act.dtype)

    def put(part, columns):
        if not first:
            part = part + refs[0][:, columns]
        if last:
            keep_ref, send_ref = refs[-3:-1]
            half = part.shape[0] // 2
            keep_ref[:, columns] = part[:half]
            send_ref[:, columns] = part[half:].astype(send_ref.dtype)
        else:
            refs[-2][:, columns] = part

    @pl.when(step < tiles)
    def _():
        put(
            jnp.dot(act[...], weight_ref[...], preferred_element_type=jnp.float32),
            pl.ds(pl.multiple_of(step * tile, tile), tile),
        )

    @pl.when(step == tiles)
    def _():
        put(
            jnp.dot(act[...], pick_ref[...], preferred_element_type=jnp.float32),
            slice(width, width + LANES),
        )


def decode(own, recv, bias, pick, weight, start, total, last, after):
    rows, count = own.shape
    width = weight.shape[1]
    tile = tile_of(width)
    tiles = width // tile
    block = start // count
    first = total is None
    if last:
        out_shape = [
            jax.ShapeDtypeStruct((rows // 2, width + LANES), jnp.float32),
            jax.ShapeDtypeStruct((rows // 2, width + LANES), jnp.float32),
        ]
    else:
        out_shape = [jax.ShapeDtypeStruct((rows, width + LANES), jnp.float32)]
    operands = [own, recv, bias[start : start + count].reshape(1, count), pick[start : start + count], weight]
    in_specs = [whole()] * 4 + [
        pl.BlockSpec((count, tile), lambda j: (block, jnp.minimum(j, tiles - 1)))
    ]
    if not first:
        operands.append(total)
        in_specs.append(whole())
    out = pl.pallas_call(
        functools.partial(decode_kernel, tile, tiles, first, last),
        grid=(tiles + 1,),
        out_shape=out_shape,
        in_specs=in_specs + [untouched()] * len(after),
        out_specs=[whole()] * len(out_shape),
        scratch_shapes=[pltpu.VMEM((rows, count), jnp.bfloat16)],
        compiler_params=pltpu.CompilerParams(vmem_limit_bytes=VMEM_LIMIT),
        cost_estimate=pl.CostEstimate(
            flops=rows * width * count // 4,
            bytes_accessed=width * count // 4,
            transcendentals=0,
        ),
    )(*operands, *after)
    return out if last else out[0]


def rows_kernel(ids_ref, pick_ref, dec_ref, *refs):
    out_ref, held, sems = refs[-3:]
    count = ids_ref.shape[0]

    def copy(j):
        start = pl.multiple_of(ids_ref[j] // GROUP * GROUP, GROUP)
        return pltpu.make_async_copy(
            dec_ref.at[pl.ds(start, GROUP)], held.at[pl.ds(j * GROUP, GROUP)], sems.at[j]
        )

    for j in range(count):
        copy(j).start()
    for j in range(count):
        copy(j).wait()
    out_ref[...] = jnp.dot(pick_ref[...], held[...], preferred_element_type=jnp.float32).astype(
        out_ref.dtype
    )


def decoder_rows(dec_weight, safe_ids, inside, after):
    count, width = safe_ids.shape[0], dec_weight.shape[1]
    column = jnp.arange(count * GROUP, dtype=jnp.int32)
    wanted = jnp.arange(count, dtype=jnp.int32) * GROUP + safe_ids % GROUP
    pick = ((wanted[:, None] == column[None, :]) & inside[:, None]).astype(jnp.bfloat16)
    return pl.pallas_call(
        rows_kernel,
        out_shape=jax.ShapeDtypeStruct((count, width), jnp.bfloat16),
        in_specs=[
            pl.BlockSpec(memory_space=pltpu.SMEM),
            whole(),
            pl.BlockSpec(memory_space=pltpu.HBM),
        ]
        + [untouched()] * len(after),
        out_specs=whole(),
        scratch_shapes=[
            pltpu.VMEM((count * GROUP, width), jnp.bfloat16),
            pltpu.SemaphoreType.DMA((count,)),
        ],
        compiler_params=pltpu.CompilerParams(vmem_limit_bytes=VMEM_LIMIT),
        cost_estimate=pl.CostEstimate(
            flops=count * count * GROUP * width,
            bytes_accessed=count * GROUP * width,
            transcendentals=0,
        ),
    )(safe_ids, pick, dec_weight, *after)


def local_codes(route_ids, slot_limit, expert_count):
    flat_ids = route_ids.reshape(-1)
    experts = jnp.arange(expert_count, dtype=jnp.int32)
    onehot = (flat_ids[:, None] == experts[None, :]).astype(jnp.int32)
    before = jnp.sum(jnp.cumsum(onehot, axis=0) * onehot, axis=1) - 1
    slot_code = jnp.where(before < slot_limit, flat_ids * slot_limit + before, -1)
    return slot_code.reshape(route_ids.shape)


def local(
    tokens,
    route_ids,
    route_weights,
    gate_proj,
    up_proj,
    down_proj,
    enc_weight,
    enc_bias,
    dec_weight,
    dec_bias,
    clamp_ids,
    clamp_values,
):
    expert_count = lax.axis_size("exp")
    me = lax.axis_index("exp")
    row_count, width = tokens.shape
    top = route_ids.shape[1]
    capacity = expert_count * SLOT
    feature_count = enc_weight.shape[1]
    offsets = jnp.array(block_offsets(expert_count), dtype=jnp.int32)
    edges = [0]
    for rows in SPLIT:
        edges.append(edges[-1] + rows)

    ids_columns = jnp.pad(route_ids.astype(jnp.bfloat16), ((0, 0), (0, LANES - top)))
    outgoing = jnp.concatenate([tokens, ids_columns], axis=1)
    gathered = [gather_blocks(outgoing[a:b]) for a, b in zip(edges, edges[1:])]

    cuts = [[feature_count * c // cut[-1] for c in cut] for cut in CUTS]

    own, recv, sends = {}, {}, {}

    def send_part(h, c, after):
        mine, send = encode(gathered[h], enc_weight, cuts[h][c], cuts[h][c + 1], after)
        sends[h, c] = send
        own[h, c], recv[h, c] = exchange(mine, send)

    send_part(0, 0, [])
    send_part(0, 1, [sends[0, 0]])

    ids = jnp.concatenate(
        [
            g[:, width : width + top].reshape(expert_count, rows, top)
            for g, rows in zip(gathered, SPLIT)
        ],
        axis=1,
    ).astype(jnp.int32)
    hit = jnp.any(ids == me, axis=2)
    order = jnp.arange(row_count)
    earlier = order[None, :] < order[:, None]
    slot = jnp.sum((hit[:, None, :] & earlier[None]).astype(jnp.int32), axis=2)
    code = jnp.where(hit & (slot < SLOT), (me ^ offsets)[:, None] * SLOT + slot, -1)
    targets = jnp.arange(capacity, dtype=jnp.int32)
    expert_in = 0.0
    for h, (a, b) in enumerate(zip(edges, edges[1:])):
        picker = (code[:, a:b].reshape(-1)[None, :] == targets[:, None]).astype(jnp.bfloat16)
        expert_in += jnp.dot(picker, gathered[h][:, :width], preferred_element_type=jnp.float32)
    expert_in = expert_in.astype(jnp.bfloat16)
    gate_part = jnp.dot(expert_in, gate_proj[0], preferred_element_type=jnp.float32)
    up_part = jnp.dot(expert_in, up_proj[0], preferred_element_type=jnp.float32)
    both_part = jnp.concatenate([gate_part, up_part], axis=1)
    both_send = both_part.astype(jnp.bfloat16)
    both_own, both_recv = exchange(both_part, both_send)

    send_part(1, 0, [recv[0, 0], both_send])
    send_part(1, 1, [recv[0, 1], sends[1, 0]])

    local_ids = clamp_ids - me * feature_count
    inside = (local_ids >= 0) & (local_ids < feature_count)
    safe_ids = jnp.clip(local_ids, 0, feature_count - 1)
    rows_dec = share_all(decoder_rows(dec_weight, safe_ids, inside, [sends[1, 1]]))
    features = jnp.arange(feature_count, dtype=jnp.int32)
    clamp_count = clamp_ids.shape[0]
    clamp_pick = (features[:, None] == local_ids[None, :]).astype(jnp.bfloat16)
    clamp_pick = jnp.pad(clamp_pick, ((0, 0), (0, -clamp_count % LANES)))

    def rebuild(h, after):
        total, parts = None, len(cuts[h]) - 1
        for c in range(parts):
            total = decode(
                own[h, c],
                recv[h, c],
                enc_bias,
                clamp_pick,
                dec_weight,
                cuts[h][c],
                total,
                c == parts - 1,
                after,
            )
        return scatter_sum(*total)

    summed = [rebuild(0, [sends[1, 1]])]

    both = both_own + both_recv.astype(jnp.float32)
    hidden_width = gate_part.shape[1]
    hidden = (jax.nn.silu(both[:, :hidden_width]) * both[:, hidden_width:]).astype(jnp.bfloat16)
    expert_out = jnp.dot(hidden, down_proj[0], preferred_element_type=jnp.float32).astype(
        jnp.bfloat16
    )
    returned = lax.all_to_all(
        expert_out.reshape(expert_count, SLOT, width),
        "exp",
        split_axis=0,
        concat_axis=0,
        tiled=True,
    )
    slot_code = local_codes(route_ids, SLOT, expert_count)
    matches = slot_code[None, :, :] == targets[:, None, None]
    weighted = jnp.sum(jnp.where(matches, route_weights[None, :, :], 0.0), axis=2)
    returned_rows = returned.reshape(capacity, width).astype(jnp.float32)
    moe_out = jnp.einsum("cr,cd->rd", weighted, returned_rows, precision=lax.Precision.HIGHEST)

    summed.append(rebuild(1, [expert_out]))
    summed = jnp.concatenate(summed, axis=0)
    chosen = summed[:, width : width + clamp_count]
    change = clamp_values.astype(jnp.float32)[None, :] - chosen
    shift = jnp.dot(change, rows_dec.astype(jnp.float32), precision=lax.Precision.HIGHEST)
    error_term = moe_out - summed[:, :width] - dec_bias
    steered = moe_out + shift
    return (error_term, steered)


def solution(mesh):
    placed = (
        P("exp", "feat"),
        P("exp", None),
        P("exp", None),
        P("exp", "feat", None),
        P("exp", "feat", None),
        P("exp", None, "feat"),
        P("feat", "exp"),
        P("exp"),
        P("exp", "feat"),
        P("feat"),
        P(),
        P(),
    )
    return jax.shard_map(
        local,
        mesh=mesh,
        in_specs=placed,
        out_specs=(P("exp", "feat"), P("exp", "feat")),
        check_vma=False,
    )
```

time: 228 us -> 221 us (0.969)
  Pallas kernels: 13.5 us -> 95.2 us
  matrix products: 72.8 us -> 13.5 us
  between operations: 14.8 us -> 1.18 us
  waiting for transfers between devices: 69.4 us -> 56.1 us
  local copies, waits for them, and re-layouts: 11.4 us -> 5.47 us
  other arithmetic: 9.33 us -> 14.9 us
  starting transfers between devices: 36.1 us -> 33 us
    pallas_call x0 -> x8, Pallas kernels: none -> 85.5 us  [the longest x4 50.1 us: decode(): pl.pallas_call(functools.partial(decode_kernel, tile, tiles, first, last)...]
    dot_general x18 -> x2, matrix products: 62 us -> 3.69 us  [local(): jnp.dot(picker, gathered[h][:, :width], preferred_element_type=jnp.float32)]
    ppermute x25, waiting for transfers between devices: 69.3 us -> 56.1 us  [swap(): return lax.ppermute(x, axis, [(i, i ^ mask) for i in range(size)])]
    unnamed x77 -> x36, local copies, waits for them, and re-layouts: 10.7 us -> 2.26 us
    add x9 -> x12, other arithmetic: 2.64 us -> 7.99 us  [the longest x6 4.71 us: scatter_sum(): x = keep + swap(send, 'exp', mask).astype(jnp.float32)]
    pallas_call x1, Pallas kernels: 13.5 us -> 9.68 us  [decoder_rows(): pl.pallas_call(rows_kernel, out_shape=jax.ShapeDtypeStruct((count, width)...]
    ppermute x25, starting transfers between devices: 29.9 us -> 26.5 us  [swap(): return lax.ppermute(x, axis, [(i, i ^ mask) for i in range(size)])]
    slice x9 -> x10, local copies, waits for them, and re-layouts: 0.2 us -> 2.7 us  [the longest x6 1.82 us: scatter_sum(): keep, send = (x[:half], x[half:].astype(jnp.bfloat16))]
  transfers between devices with their start and end apart: 27 -> 26, of which waited for: 12 -> 10; matrix products, arithmetic and copies ran while one was open for 35% -> 13% of each run, Pallas kernels for 6% -> 43%
where the time goes in v2:
time: 221 us; the launch traced here: 219 us
  Pallas kernels  95.2 us (43%)
  waiting for transfers between devices  56.1 us (25%)
  starting transfers between devices  33 us (15%)
  other arithmetic  14.9 us (7%)
  matrix products  13.5 us (6%)
  local copies, waits for them, and re-layouts  5.47 us (2%)
    ppermute x25, waiting for transfers between devices, swap(): return lax.ppermute(x, axis, [(i, i ^ mask) for i in range(size)])  56.1 us
    pallas_call x4, Pallas kernels, decode(): pl.pallas_call(functools.partial(decode_kernel, tile, tiles, first, last)...  50.1 us
    pallas_call x4, Pallas kernels, encode(): pl.pallas_call(functools.partial(encode_kernel, tile), grid=(count // til...  35.4 us
    ppermute x25, starting transfers between devices, swap(): return lax.ppermute(x, axis, [(i, i ^ mask) for i in range(size)])  26.5 us
    pallas_call x1, Pallas kernels, decoder_rows(): pl.pallas_call(rows_kernel, out_shape=jax.ShapeDtypeStruct((count, width)...  9.68 us
    all_to_all x1, starting transfers between devices, local(): lax.all_to_all(expert_out.reshape(expert_count, SLOT, width), 'exp', spli...  6.52 us
    add x6, other arithmetic, scatter_sum(): x = keep + swap(send, 'exp', mask).astype(jnp.float32)  4.71 us
  transfers between devices with their start and end apart: 26, of which 10 were waited for; matrix products, arithmetic and copies ran while one was open for 13% of the time, Pallas kernels for 43%

profile of v2, /device:TPU:0, one launch (start us, length us, event | category | flops | bytes accessed | tf_op | source)
XLA Modules:
  0.0 219.3 jit_solution(3306747849746537163)
XLA Ops:
  0.6 0.7 convert_element_type.67
  1.4 0.9 fusion.27
  2.3 4.1 %collective-permute-start = (bf16[8,3712]{1,0:T(8,128)(2,1)S(1)}, bf16[8,3712]{1,0:T(8,128)(2,1)S(1)}, u32[]{:S(2)}, u32[]{:S(2)}) collective-permute-start(bf16[8,3712]{1,0:T(8,128)(2,1)S(1)} %get-tuple-element.30), channel_id=1, source_target_pairs={{0,16},{2,18},{4,20},{6,22},{8,24},{10,26},{12,28},{14,30},{16,0},... | collective-permute-start | bytes 178184 | tf_op jit(solution)/shard_map/ppermute | solution.py:20
  6.5 0.7 compare_and_fusion
  7.2 0.3 iota_compare_fusion
  7.6 0.7 fusion.41
  8.3 1.3 pad_convert_fusion
  9.5 0.7 xor_multiply_fusion
  10.2 0.8 fusion.21.pick_ref
  11.0 1.9 collective-permute-start.1
  12.9 0.3 collective-permute-start.5
  13.2 3.9 %collective-permute-done.1 = bf16[16,3712]{1,0:T(8,128)(2,1)S(1)} collective-permute-done((bf16[16,3712]{1,0:T(8,128)(2,1)S(1)}, bf16[16,3712]{1,0:T(8,128)(2,1)S(1)}, u32[]{:S(2)}, u32[]{:S(2)}) %collective-permute-start.1) | collective-permute-done | bytes 118816 | tf_op jit(solution)/shard_map/ppermute | solution.py:20
  17.2 1.6 collective-permute-start.2
  18.8 1.2 collective-permute-start.6
  20.0 4.9 %collective-permute-done.2 = bf16[32,3712]{1,0:T(8,128)(2,1)S(1)} collective-permute-done((bf16[32,3712]{1,0:T(8,128)(2,1)S(1)}, bf16[32,3712]{1,0:T(8,128)(2,1)S(1)}, u32[]{:S(2)}, u32[]{:S(2)}) %collective-permute-start.2) | collective-permute-done | bytes 237600 | tf_op jit(solution)/shard_map/ppermute | solution.py:20
  25.1 2.4 %collective-permute-done.6 = bf16[32,3712]{1,0:T(8,128)(2,1)S(1)} collective-permute-done((bf16[32,3712]{1,0:T(8,128)(2,1)S(1)}, bf16[32,3712]{1,0:T(8,128)(2,1)S(1)}, u32[]{:S(2)}, u32[]{:S(2)}) %collective-permute-start.6) | collective-permute-done | bytes 237600 | tf_op jit(solution)/shard_map/ppermute | solution.py:20
  27.8 8.7 %shard_map.140 = (f32[128,2048]{1,0:T(8,128)S(1)}, bf16[128,2048]{1,0:T(8,128)(2,1)S(1)}) custom-call(bf16[128,3712]{1,0:T(8,128)(2,1)S(1)} %constant_dynamic-update-slice_fusion.tokens_ref, bf16[3584,4096]{1,0:T(8,128)(2,1)} %weight_ref.11), custom_call_target="tpu_custom_call" | custom-call | flops 234881024 | bytes 1835008 | tf_op jit(solution)/shard_map/pallas_call | solution.py:92
  36.4 1.0 copy-done.2
  37.4 1.2 collective-permute-start.10
  38.7 9.4 %shard_map.141 = (f32[128,2048]{1,0:T(8,128)S(1)}, bf16[128,2048]{1,0:T(8,128)(2,1)}) custom-call(bf16[128,3712]{1,0:T(8,128)(2,1)S(1)} %constant_dynamic-update-slice_fusion.tokens_ref, bf16[3584,4096]{1,0:T(8,128)(2,1)} %weight_ref.11, bf16[128,2048]{1,0:T(8,128)(2,1)S(1)} %get-tuple-element.14.refs_0_), custom_call_target="tpu_custom_call" | custom-call | flops 234881024 | bytes 1835008 | tf_op jit(solution)/shard_map/pallas_call | solution.py:92
  48.1 1.0 copy-done
  49.1 0.8 collective-permute-start.9
  49.9 0.4 fusion.26
  50.3 0.4 convert_reduce_fusion
  50.9 1.6 fusion.10
  52.6 2.0 fusion.6
  54.7 4.4 %fusion.2 = f32[128,1024]{1,0:T(8,128)S(1)} fusion(bf16[128,3584]{1,0:T(8,128)(2,1)S(1)} %fusion.6, bf16[1,3584,1024]{2,1,0:T(8,128)(2,1)} %param.17), kind=kOutput, calls=%fused_computation.2 | convolution fusion | flops 939524096 | bytes 8781824 | tf_op jit(solution)/shard_map/dot_general | solution.py:301
  59.1 1.1 fusion.4
  60.3 1.3 collective-permute-start.8
  61.7 8.7 %shard_map.142 = (f32[128,2048]{1,0:T(8,128)S(1)}, bf16[128,2048]{1,0:T(8,128)(2,1)S(1)}) custom-call(bf16[128,3712]{1,0:T(8,128)(2,1)S(1)} %constant_dynamic-update-slice_fusion.5.tokens_ref, bf16[3584,4096]{1,0:T(8,128)(2,1)} %weight_ref.11, bf16[128,2048]{1,0:T(8,128)(2,1)S(1)} %collective-permute-done.10.refs_0_.recv_ref, ...), custom_call_target="tpu_custom_call" | custom-call | flops 234881024 | bytes 1835008 | tf_op jit(solution)/shard_map/pallas_call | solution.py:92
  70.4 0.9 collective-permute-start.16
  71.2 8.7 %shard_map.143 = (f32[128,2048]{1,0:T(8,128)S(1)}, bf16[128,2048]{1,0:T(8,128)(2,1)S(1)}) custom-call(bf16[128,3712]{1,0:T(8,128)(2,1)S(1)} %constant_dynamic-update-slice_fusion.5.tokens_ref, bf16[3584,4096]{1,0:T(8,128)(2,1)} %weight_ref.11, bf16[128,2048]{1,0:T(8,128)(2,1)S(1)} %collective-permute-done.9.refs_0_.recv_ref, ...), custom_call_target="tpu_custom_call" | custom-call | flops 234881024 | bytes 1835008 | tf_op jit(solution)/shard_map/pallas_call | solution.py:92
  79.9 1.3 collective-permute-start.15
  81.2 12.6 %shard_map.144.refs_0_ = f32[128,3712]{1,0:T(8,128)S(1)} custom-call(f32[128,2048]{1,0:T(8,128)S(1)} %copy-done.3, bf16[128,2048]{1,0:T(8,128)(2,1)S(1)} %collective-permute-done.10.refs_0_.recv_ref, f32[1,2048]{1,0:T(1,128)S(1)} %bitcast.28, bf16[2048,128]{1,0:T(8,128)(2,1)S(1)} %get-tuple-element.28.pick_ref, bf16[4096,3584]{1,0:T(8,128)(2,1)} %dec_ref.1, ...), custom_call_target="tpu_custom_call" | custom-call | flops 234881024 | bytes 1835008 | tf_op jit(solution)/shard_map/pallas_call | solution.py:168
  93.8 13.2 %shard_map.145 = (f32[64,3712]{1,0:T(8,128)S(1)}, f32[64,3712]{1,0:T(8,128)}) custom-call(f32[128,2048]{1,0:T(8,128)S(1)} %copy-done.1, bf16[128,2048]{1,0:T(8,128)(2,1)S(1)} %collective-permute-done.9.refs_0_.recv_ref, f32[1,2048]{1,0:T(1,128)S(1)} %bitcast.26, bf16[2048,128]{1,0:T(8,128)(2,1)S(1)} %get-tuple-element.29.pick_ref, ...), custom_call_target="tpu_custom_call" | custom-call | flops 234881024 | bytes 1835008 | tf_op jit(solution)/shard_map/pallas_call | solution.py:168
  107.0 9.7 %shard_map.148 = bf16[64,3584]{1,0:T(8,128)(2,1)S(1)} custom-call(s32[64]{0:T(128)S(1)} %get-tuple-element.39.ids_ref, bf16[64,1024]{1,0:T(8,128)(2,1)S(1)} %copy-done.4, bf16[4096,3584]{1,0:T(8,128)(2,1)} %dec_ref.1, bf16[128,2048]{1,0:T(8,128)(2,1)S(1)} %get-tuple-element.19.refs_0_.refs_1_), custom_call_target="tpu_custom_call" | custom-call | flops 234881024 | bytes 3670016 | tf_op jit(solution)/shard_map/pallas_call | solution.py:209
  116.7 0.4 collective-permute-start.21
  117.3 2.1 fusion.7.refs_0_.refs_1_
  119.4 12.1 %shard_map.146.refs_0_ = f32[128,3712]{1,0:T(8,128)S(1)} custom-call(f32[128,2048]{1,0:T(8,128)S(1)} %get-tuple-element.23.own_ref, bf16[128,2048]{1,0:T(8,128)(2,1)S(1)} %collective-permute-done.16.recv_ref, f32[1,2048]{1,0:T(1,128)S(1)} %bitcast.29, bf16[2048,128]{1,0:T(8,128)(2,1)S(1)} %get-tuple-element.28.pick_ref, bf16[4096,3584]{1,0:T(8,128)(2,1)} %dec_ref.1, ...), custom_call_target="tpu_custom_call" | custom-call | flops 234881024 | bytes 1835008 | tf_op jit(solution)/shard_map/pallas_call | solution.py:168
  131.6 12.1 %shard_map.147 = (f32[64,3712]{1,0:T(8,128)S(1)}, f32[64,3712]{1,0:T(8,128)S(1)}) custom-call(f32[128,2048]{1,0:T(8,128)S(1)} %get-tuple-element.22.own_ref, bf16[128,2048]{1,0:T(8,128)(2,1)S(1)} %collective-permute-done.15.recv_ref, f32[1,2048]{1,0:T(1,128)S(1)} %bitcast.27, bf16[2048,128]{1,0:T(8,128)(2,1)S(1)} %get-tuple-element.29.pick_ref, ...), custom_call_target="tpu_custom_call" | custom-call | flops 234881024 | bytes 1835008 | tf_op jit(solution)/shard_map/pallas_call | solution.py:168
  144.7 1.9 add.93
  146.6 1.1 collective-permute-start.22
  147.8 2.2 %add.83 = f32[64,3712]{1,0:T(8,128)} add(f32[64,3712]{1,0:T(8,128)S(1)} %get-tuple-element.20, f32[64,3712]{1,0:T(8,128)} %collective-permute-done.11) | non-fusion elementwise | flops 237568 | bytes 2850816 | tf_op jit(solution)/shard_map/add | solution.py:47
  150.1 1.7 slice.185
  151.8 0.9 collective-permute-start.12
  152.9 6.5 %all-to-all-start = ((bf16[16,8,3584]{2,1,0:T(8,128)(2,1)}), bf16[16,8,3584]{2,1,0:T(8,128)(2,1)S(1)}, u32[]{:S(2)}, u32[]{:S(2)}) async-start(bf16[16,8,3584]{2,1,0:T(8,128)(2,1)} %bitcast.5), calls=%async_computation | async-start | bytes 1835008 | tf_op jit(solution)/shard_map/all_to_all | solution.py:342
  159.4 0.8 collective-permute-done.22
  160.1 1.1 add.94
  161.3 1.2 collective-permute-start.23
  162.5 1.3 add.87
  163.8 1.5 collective-permute-start.18
  165.4 2.0 collective-permute-done.12
  167.3 1.1 slice_add_fusion.1
  168.5 8.6 %collective-permute-done.18 = bf16[32,3712]{1,0:T(8,128)(2,1)S(1)} collective-permute-done((bf16[32,3712]{1,0:T(8,128)(2,1)S(1)}, bf16[32,3712]{1,0:T(8,128)(2,1)S(1)}, u32[]{:S(2)}, u32[]{:S(2)}) %collective-permute-start.18) | collective-permute-done | bytes 237600 | tf_op jit(solution)/shard_map/ppermute | solution.py:20
  177.2 0.3 collective-permute-start.19
  177.5 12.6 %collective-permute-done.13 = bf16[16,3712]{1,0:T(8,128)(2,1)S(1)} collective-permute-done((bf16[16,3712]{1,0:T(8,128)(2,1)S(1)}, bf16[16,3712]{1,0:T(8,128)(2,1)S(1)}, u32[]{:S(2)}, u32[]{:S(2)}) %collective-permute-start.13) | collective-permute-done | bytes 118816 | tf_op jit(solution)/shard_map/ppermute | solution.py:20
  190.2 2.6 %collective-permute-start.14 = (bf16[8,3712]{1,0:T(8,128)(2,1)S(1)}, bf16[8,3712]{1,0:T(8,128)(2,1)S(1)}, u32[]{:S(2)}, u32[]{:S(2)}) collective-permute-start(bf16[8,3712]{1,0:T(8,128)(2,1)S(1)} %slice.189), channel_id=1, source_target_pairs={{0,16},{2,18},{4,20},{6,22},{8,24},{10,26},{12,28},{14,30},{16,0},... | collective-permute-start | bytes 178184 | tf_op jit(solution)/shard_map/ppermute | solution.py:20
  192.8 2.5 %collective-permute-start.20 = (bf16[8,3712]{1,0:T(8,128)(2,1)S(1)}, bf16[8,3712]{1,0:T(8,128)(2,1)S(1)}, u32[]{:S(2)}, u32[]{:S(2)}) collective-permute-start(bf16[8,3712]{1,0:T(8,128)(2,1)S(1)} %slice.188), channel_id=1, source_target_pairs={{0,16},{2,18},{4,20},{6,22},{8,24},{10,26},{12,28},{14,30},{16,0},... | collective-permute-start | bytes 178184 | tf_op jit(solution)/shard_map/ppermute | solution.py:20
  195.3 2.0 collective-permute-done.14
  197.4 0.7 collective-permute-start.24
  198.1 10.9 %collective-permute-done.20 = bf16[8,3712]{1,0:T(8,128)(2,1)S(1)} collective-permute-done((bf16[8,3712]{1,0:T(8,128)(2,1)S(1)}, bf16[8,3712]{1,0:T(8,128)(2,1)S(1)}, u32[]{:S(2)}, u32[]{:S(2)}) %collective-permute-start.20) | collective-permute-done | bytes 59424 | tf_op jit(solution)/shard_map/ppermute | solution.py:20
  209.1 1.2 fusion.25
  210.3 8.0 %collective-permute-done.24 = bf16[64,3584]{1,0:T(8,128)(2,1)S(1)} collective-permute-done((bf16[64,3584]{1,0:T(8,128)(2,1)S(1)}, bf16[64,3584]{1,0:T(8,128)(2,1)S(1)}, u32[]{:S(2)}, u32[]{:S(2)}) %collective-permute-start.24) | collective-permute-done | bytes 458784 | tf_op jit(solution)/shard_map/ppermute | solution.py:20
  218.2 1.0 convolution_add_fusion.1
  (99 shorter events, 2.9 us)
Async XLA Ops:
  2.3 8.6 %collective-permute-start = (bf16[8,3712]{1,0:T(8,128)(2,1)S(1)}, bf16[8,3712]{1,0:T(8,128)(2,1)S(1)}, u32[]{:S(2)}, u32[]{:S(2)}) collective-permute-start(bf16[8,3712]{1,0:T(8,128)(2,1)S(1)} %get-tuple-element.30), channel_id=1, source_target_pairs={{0,16},{2,18},{4,20},{6,22},{8,24},{10,26},{12,28},{14,30},{16,0},... | collective-permute-start | bytes 178184 | tf_op jit(solution)/shard_map/ppermute | solution.py:20
  6.4 6.5 %collective-permute-start.4 = (bf16[8,3712]{1,0:T(8,128)(2,1)S(1)}, bf16[8,3712]{1,0:T(8,128)(2,1)S(1)}, u32[]{:S(2)}, u32[]{:S(2)}) collective-permute-start(bf16[8,3712]{1,0:T(8,128)(2,1)S(1)} %get-tuple-element.33), channel_id=1, source_target_pairs={{0,16},{2,18},{4,20},{6,22},{8,24},{10,26},{12,28},{14,30},{16,0},... | collective-permute-start | bytes 178184 | tf_op jit(solution)/shard_map/ppermute | solution.py:20
  11.0 6.1 %collective-permute-start.1 = (bf16[16,3712]{1,0:T(8,128)(2,1)S(1)}, bf16[16,3712]{1,0:T(8,128)(2,1)S(1)}, u32[]{:S(2)}, u32[]{:S(2)}) collective-permute-start(bf16[16,3712]{1,0:T(8,128)(2,1)S(1)} %pad_maximum_fusion.5), channel_id=1, source_target_pairs={{0,8},{2,10},{4,12},{6,14},{8,0},{10,2},{12,4},{14,6},{16,24},{18,... | collective-permute-start | bytes 356360 | tf_op jit(solution)/shard_map/ppermute | solution.py:20
  12.9 5.8 %collective-permute-start.5 = (bf16[16,3712]{1,0:T(8,128)(2,1)S(1)}, bf16[16,3712]{1,0:T(8,128)(2,1)S(1)}, u32[]{:S(2)}, u32[]{:S(2)}) collective-permute-start(bf16[16,3712]{1,0:T(8,128)(2,1)S(1)} %pad_maximum_fusion.6), channel_id=1, source_target_pairs={{0,8},{2,10},{4,12},{6,14},{8,0},{10,2},{12,4},{14,6},{16,24},{18,... | collective-permute-start | bytes 356360 | tf_op jit(solution)/shard_map/ppermute | solution.py:20
  17.2 7.8 %collective-permute-start.2 = (bf16[32,3712]{1,0:T(8,128)(2,1)S(1)}, bf16[32,3712]{1,0:T(8,128)(2,1)S(1)}, u32[]{:S(2)}, u32[]{:S(2)}) collective-permute-start(bf16[32,3712]{1,0:T(8,128)(2,1)S(1)} %pad_maximum_fusion.3), channel_id=1, source_target_pairs={{0,4},{2,6},{4,0},{6,2},{8,12},{10,14},{12,8},{14,10},{16,20},{18,... | collective-permute-start | bytes 712712 | tf_op jit(solution)/shard_map/ppermute | solution.py:20
  18.8 8.8 %collective-permute-start.6 = (bf16[32,3712]{1,0:T(8,128)(2,1)S(1)}, bf16[32,3712]{1,0:T(8,128)(2,1)S(1)}, u32[]{:S(2)}, u32[]{:S(2)}) collective-permute-start(bf16[32,3712]{1,0:T(8,128)(2,1)S(1)} %pad_maximum_fusion.4), channel_id=1, source_target_pairs={{0,4},{2,6},{4,0},{6,2},{8,12},{10,14},{12,8},{14,10},{16,20},{18,... | collective-permute-start | bytes 712712 | tf_op jit(solution)/shard_map/ppermute | solution.py:20
  25.0 2.7 %collective-permute-start.3 = (bf16[64,3712]{1,0:T(8,128)(2,1)S(1)}, bf16[64,3712]{1,0:T(8,128)(2,1)S(1)}, u32[]{:S(2)}, u32[]{:S(2)}) collective-permute-start(bf16[64,3712]{1,0:T(8,128)(2,1)S(1)} %pad_maximum_fusion.1), channel_id=1, source_target_pairs={{0,2},{2,0},{4,6},{6,4},{8,10},{10,8},{12,14},{14,12},{16,18},{18,... | collective-permute-start | bytes 1425416 | tf_op jit(solution)/shard_map/ppermute | solution.py:20
  27.6 22.3 %collective-permute-start.7 = (bf16[64,3712]{1,0:T(8,128)(2,1)S(1)}, bf16[64,3712]{1,0:T(8,128)(2,1)S(1)}, u32[]{:S(2)}, u32[]{:S(2)}) collective-permute-start(bf16[64,3712]{1,0:T(8,128)(2,1)S(1)} %pad_maximum_fusion.2), channel_id=1, source_target_pairs={{0,2},{2,0},{4,6},{6,4},{8,10},{10,8},{12,14},{14,12},{16,18},{18,... | collective-permute-start | bytes 1425416 | tf_op jit(solution)/shard_map/ppermute | solution.py:20
  36.4 1.0 copy-start.2
  37.4 24.2 %collective-permute-start.10 = (bf16[128,2048]{1,0:T(8,128)(2,1)S(1)}, bf16[128,2048]{1,0:T(8,128)(2,1)S(1)}, u32[]{:S(2)}, u32[]{:S(2)}) collective-permute-start(bf16[128,2048]{1,0:T(8,128)(2,1)S(1)} %get-tuple-element.14.refs_0_), channel_id=1, source_target_pairs={{0,1},{1,0},{2,3},{3,2},{4,5},{5,4},{6,7},{7,6},{8,9},{9,8},{10,11... | collective-permute-start | bytes 1572872 | tf_op jit(solution)/shard_map/ppermute | solution.py:20
  48.1 1.0 copy-start
  49.1 22.2 %collective-permute-start.9 = (bf16[128,2048]{1,0:T(8,128)(2,1)}, bf16[128,2048]{1,0:T(8,128)(2,1)S(1)}, u32[]{:S(2)}, u32[]{:S(2)}) collective-permute-start(bf16[128,2048]{1,0:T(8,128)(2,1)} %get-tuple-element.16), channel_id=1, source_target_pairs={{0,1},{1,0},{2,3},{3,2},{4,5},{5,4},{6,7},{7,6},{8,9},{9,8},{10,11... | collective-permute-start | bytes 1572872 | tf_op jit(solution)/shard_map/ppermute | solution.py:20
  52.6 6.4 %slice-start = ((s8[7340032]{0:T(1024)(128)(4,1)}), s8[4194304]{0:T(1024)(128)(4,1)S(1)}, s32[]{:S(2)}) async-start(s8[7340032]{0:T(1024)(128)(4,1)} %bitcast.30), calls=%async_computation.1 | async-start | bytes 8388608
  54.7 4.4 %slice-start.1 = ((s8[7340032]{0:T(1024)(128)(4,1)}), s8[3145728]{0:T(1024)(128)(4,1)S(1)}, s32[]{:S(2)}) async-start(s8[7340032]{0:T(1024)(128)(4,1)} %bitcast.30), calls=%async_computation.2 | async-start | bytes 6291456
  59.1 2.5 %copy-start.5 = (bf16[4096,128]{1,0:T(8,128)(2,1)S(1)}, bf16[4096,128]{1,0:T(8,128)(2,1)}, u32[]{:S(2)}) copy-start(bf16[4096,128]{1,0:T(8,128)(2,1)} %pad_convert_fusion) | copy-start | bytes 3145732
  60.3 56.9 %collective-permute-start.8 = (bf16[128,2048]{1,0:T(8,128)(2,1)S(1)}, bf16[128,2048]{1,0:T(8,128)(2,1)S(1)}, u32[]{:S(2)}, u32[]{:S(2)}) collective-permute-start(bf16[128,2048]{1,0:T(8,128)(2,1)S(1)} %fusion.15.refs_1_), channel_id=1, source_target_pairs={{0,1},{1,0},{2,3},{3,2},{4,5},{5,4},{6,7},{7,6},{8,9},{9,8},{10,11... | collective-permute-start | bytes 1572872 | tf_op jit(solution)/shard_map/ppermute | solution.py:20
  70.3 10.8 %copy-start.3 = (f32[128,2048]{1,0:T(8,128)S(1)}, f32[128,2048]{1,0:T(8,128)}, u32[]{:S(2)}) copy-start(f32[128,2048]{1,0:T(8,128)} %copy-done.2) | copy-start | bytes 3145732
  70.4 49.1 %collective-permute-start.16 = (bf16[128,2048]{1,0:T(8,128)(2,1)S(1)}, bf16[128,2048]{1,0:T(8,128)(2,1)S(1)}, u32[]{:S(2)}, u32[]{:S(2)}) collective-permute-start(bf16[128,2048]{1,0:T(8,128)(2,1)S(1)} %get-tuple-element.18.refs_1_), channel_id=1, source_target_pairs={{0,1},{1,0},{2,3},{3,2},{4,5},{5,4},{6,7},{7,6},{8,9},{9,8},{10,11... | collective-permute-start | bytes 1572872 | tf_op jit(solution)/shard_map/ppermute | solution.py:20
  79.9 51.7 %collective-permute-start.15 = (bf16[128,2048]{1,0:T(8,128)(2,1)S(1)}, bf16[128,2048]{1,0:T(8,128)(2,1)S(1)}, u32[]{:S(2)}, u32[]{:S(2)}) collective-permute-start(bf16[128,2048]{1,0:T(8,128)(2,1)S(1)} %get-tuple-element.19.refs_0_.refs_1_), channel_id=1, source_target_pairs={{0,1},{1,0},{2,3},{3,2},{4,5},{5,4},{6,7},{7,6},{8,9},{9,8},{10,11... | collective-permute-start | bytes 1572872 | tf_op jit(solution)/shard_map/ppermute | solution.py:20
  81.2 12.6 %copy-start.1 = (f32[128,2048]{1,0:T(8,128)S(1)}, f32[128,2048]{1,0:T(8,128)}, u32[]{:S(2)}) copy-start(f32[128,2048]{1,0:T(8,128)} %copy-done) | copy-start | bytes 3145732
  81.2 36.1 %slice-start.2 = ((s8[7340032]{0:T(1024)(128)(4,1)}), s8[4194304]{0:T(1024)(128)(4,1)S(1)}, s32[]{:S(2)}) async-start(s8[7340032]{0:T(1024)(128)(4,1)} %bitcast.32), calls=%async_computation.3 | async-start | bytes 8388608
  93.8 13.3 %copy-start.4 = (bf16[64,1024]{1,0:T(8,128)(2,1)S(1)}, bf16[64,1024]{1,0:T(8,128)(2,1)}, u32[]{:S(2)}) copy-start(bf16[64,1024]{1,0:T(8,128)(2,1)} %fusion.21.pick_ref) | copy-start | bytes 393220
  93.8 23.5 %slice-start.3 = ((s8[7340032]{0:T(1024)(128)(4,1)}), s8[3145728]{0:T(1024)(128)(4,1)S(1)}, s32[]{:S(2)}) async-start(s8[7340032]{0:T(1024)(128)(4,1)} %bitcast.32), calls=%async_computation.4 | async-start | bytes 6291456
  107.0 40.8 %collective-permute-start.11 = (f32[64,3712]{1,0:T(8,128)}, f32[64,3712]{1,0:T(8,128)}, u32[]{:S(2)}, u32[]{:S(2)}) collective-permute-start(f32[64,3712]{1,0:T(8,128)} %get-tuple-element.21), channel_id=1, source_target_pairs={{0,2},{2,0},{4,6},{6,4},{8,10},{10,8},{12,14},{14,12},{16,18},{18,... | collective-permute-start | bytes 2850824 | tf_op jit(solution)/shard_map/ppermute | solution.py:20
  116.7 28.0 %collective-permute-start.21 = (bf16[64,3584]{1,0:T(8,128)(2,1)S(1)}, bf16[64,3584]{1,0:T(8,128)(2,1)}, u32[]{:S(2)}, u32[]{:S(2)}) collective-permute-start(bf16[64,3584]{1,0:T(8,128)(2,1)S(1)} %shard_map.148), channel_id=1, source_target_pairs={{0,2},{2,0},{4,6},{6,4},{8,10},{10,8},{12,14},{14,12},{16,18},{18,... | collective-permute-start | bytes 1376264 | tf_op jit(solution)/shard_map/ppermute | solution.py:20
  131.6 12.4 %copy-start.7 = (s32[16,8]{0,1:T(8,128)S(1)}, s32[16,8]{0,1:T(8,128)}, u32[]{:S(2)}) copy-start(s32[16,8]{0,1:T(8,128)} %param.14) | copy-start | bytes 1540
  131.6 12.5 %copy-start.8 = (f32[16,8]{0,1:T(8,128)S(1)}, f32[16,8]{0,1:T(8,128)}, u32[]{:S(2)}) copy-start(f32[16,8]{0,1:T(8,128)} %param.15) | copy-start | bytes 1540
  131.6 16.2 %copy-start.9 = (bf16[64]{0:T(256)(128)(2,1)S(1)}, bf16[64]{0:T(256)(128)(2,1)}, u32[]{:S(2)}) copy-start(bf16[64]{0:T(256)(128)(2,1)} %param.24) | copy-start | bytes 388
  143.8 18.7 %collective-permute-start.17 = (f32[64,3712]{1,0:T(8,128)S(1)}, f32[64,3712]{1,0:T(8,128)}, u32[]{:S(2)}, u32[]{:S(2)}) collective-permute-start(f32[64,3712]{1,0:T(8,128)S(1)} %get-tuple-element.25), channel_id=1, source_target_pairs={{0,2},{2,0},{4,6},{6,4},{8,10},{10,8},{12,14},{14,12},{16,18},{18,... | collective-permute-start | bytes 2850824 | tf_op jit(solution)/shard_map/ppermute | solution.py:20
  146.6 13.6 %collective-permute-start.22 = (bf16[64,3584]{1,0:T(8,128)(2,1)}, bf16[64,3584]{1,0:T(8,128)(2,1)S(1)}, u32[]{:S(2)}, u32[]{:S(2)}) collective-permute-start(bf16[64,3584]{1,0:T(8,128)(2,1)} %add.93), channel_id=1, source_target_pairs={{0,4},{2,6},{4,0},{6,2},{8,12},{10,14},{12,8},{14,10},{16,20},{18,... | collective-permute-start | bytes 1376264 | tf_op jit(solution)/shard_map/ppermute | solution.py:20
  150.1 59.0 %copy-start.6 = (f32[3584]{0:T(1024)S(1)}, f32[3584]{0:T(1024)}, u32[]{:S(2)}) copy-start(f32[3584]{0:T(1024)} %param.22) | copy-start | bytes 43012
  151.8 15.5 %collective-permute-start.12 = (bf16[32,3712]{1,0:T(8,128)(2,1)}, bf16[32,3712]{1,0:T(8,128)(2,1)S(1)}, u32[]{:S(2)}, u32[]{:S(2)}) collective-permute-start(bf16[32,3712]{1,0:T(8,128)(2,1)} %slice.185), channel_id=1, source_target_pairs={{0,4},{2,6},{4,0},{6,2},{8,12},{10,14},{12,8},{14,10},{16,20},{18,... | collective-permute-start | bytes 712712 | tf_op jit(solution)/shard_map/ppermute | solution.py:20
  152.9 56.2 %all-to-all-start = ((bf16[16,8,3584]{2,1,0:T(8,128)(2,1)}), bf16[16,8,3584]{2,1,0:T(8,128)(2,1)S(1)}, u32[]{:S(2)}, u32[]{:S(2)}) async-start(bf16[16,8,3584]{2,1,0:T(8,128)(2,1)} %bitcast.5), calls=%async_computation | async-start | bytes 1835008 | tf_op jit(solution)/shard_map/all_to_all | solution.py:342
  161.3 36.0 %collective-permute-start.23 = (bf16[64,3584]{1,0:T(8,128)(2,1)S(1)}, bf16[64,3584]{1,0:T(8,128)(2,1)S(1)}, u32[]{:S(2)}, u32[]{:S(2)}) collective-permute-start(bf16[64,3584]{1,0:T(8,128)(2,1)S(1)} %add.94), channel_id=1, source_target_pairs={{0,8},{2,10},{4,12},{6,14},{8,0},{10,2},{12,4},{14,6},{16,24},{18,... | collective-permute-start | bytes 1376264 | tf_op jit(solution)/shard_map/ppermute | solution.py:20
  163.8 13.3 %collective-permute-start.18 = (bf16[32,3712]{1,0:T(8,128)(2,1)S(1)}, bf16[32,3712]{1,0:T(8,128)(2,1)S(1)}, u32[]{:S(2)}, u32[]{:S(2)}) collective-permute-start(bf16[32,3712]{1,0:T(8,128)(2,1)S(1)} %slice.184), channel_id=1, source_target_pairs={{0,4},{2,6},{4,0},{6,2},{8,12},{10,14},{12,8},{14,10},{16,20},{18,... | collective-permute-start | bytes 712712 | tf_op jit(solution)/shard_map/ppermute | solution.py:20
  168.4 21.7 %collective-permute-start.13 = (bf16[16,3712]{1,0:T(8,128)(2,1)S(1)}, bf16[16,3712]{1,0:T(8,128)(2,1)S(1)}, u32[]{:S(2)}, u32[]{:S(2)}) collective-permute-start(bf16[16,3712]{1,0:T(8,128)(2,1)S(1)} %slice.187), channel_id=1, source_target_pairs={{0,8},{2,10},{4,12},{6,14},{8,0},{10,2},{12,4},{14,6},{16,24},{18,... | collective-permute-start | bytes 356360 | tf_op jit(solution)/shard_map/ppermute | solution.py:20
  177.2 15.5 %collective-permute-start.19 = (bf16[16,3712]{1,0:T(8,128)(2,1)S(1)}, bf16[16,3712]{1,0:T(8,128)(2,1)S(1)}, u32[]{:S(2)}, u32[]{:S(2)}) collective-permute-start(bf16[16,3712]{1,0:T(8,128)(2,1)S(1)} %slice.186), channel_id=1, source_target_pairs={{0,8},{2,10},{4,12},{6,14},{8,0},{10,2},{12,4},{14,6},{16,24},{18,... | collective-permute-start | bytes 356360 | tf_op jit(solution)/shard_map/ppermute | solution.py:20
  190.2 7.1 %collective-permute-start.14 = (bf16[8,3712]{1,0:T(8,128)(2,1)S(1)}, bf16[8,3712]{1,0:T(8,128)(2,1)S(1)}, u32[]{:S(2)}, u32[]{:S(2)}) collective-permute-start(bf16[8,3712]{1,0:T(8,128)(2,1)S(1)} %slice.189), channel_id=1, source_target_pairs={{0,16},{2,18},{4,20},{6,22},{8,24},{10,26},{12,28},{14,30},{16,0},... | collective-permute-start | bytes 178184 | tf_op jit(solution)/shard_map/ppermute | solution.py:20
  192.8 16.3 %collective-permute-start.20 = (bf16[8,3712]{1,0:T(8,128)(2,1)S(1)}, bf16[8,3712]{1,0:T(8,128)(2,1)S(1)}, u32[]{:S(2)}, u32[]{:S(2)}) collective-permute-start(bf16[8,3712]{1,0:T(8,128)(2,1)S(1)} %slice.188), channel_id=1, source_target_pairs={{0,16},{2,18},{4,20},{6,22},{8,24},{10,26},{12,28},{14,30},{16,0},... | collective-permute-start | bytes 178184 | tf_op jit(solution)/shard_map/ppermute | solution.py:20
  197.4 20.9 %collective-permute-start.24 = (bf16[64,3584]{1,0:T(8,128)(2,1)S(1)}, bf16[64,3584]{1,0:T(8,128)(2,1)S(1)}, u32[]{:S(2)}, u32[]{:S(2)}) collective-permute-start(bf16[64,3584]{1,0:T(8,128)(2,1)S(1)} %add.95), channel_id=1, source_target_pairs={{0,16},{2,18},{4,20},{6,22},{8,24},{10,26},{12,28},{14,30},{16,0},... | collective-permute-start | bytes 1376264 | tf_op jit(solution)/shard_map/ppermute | solution.py:20

commit v3 on v0

v3 whole, which is shorter than its diff:
```python
import functools

import jax
import jax.numpy as jnp
from jax import lax
from jax.experimental import pallas as pl
from jax.experimental.pallas import tpu as pltpu
from jax.sharding import PartitionSpec as P

SLOT = 8
SPLIT = (8, 8)
CUTS = ((0, 2, 4), (0, 2, 4))
LANES = 128
FRACTION = 2
VMEM_LIMIT = 36 * 1024 * 1024
ROWS_LIMIT = 56 * 1024 * 1024


def swap(x, axis, mask):
    size = lax.axis_size(axis)
    return lax.ppermute(x, axis, [(i, i ^ mask) for i in range(size)])


def doublings(size):
    masks = []
    while size > 1:
        size //= 2
        masks.append(size)
    return masks


def gather_blocks(x):
    for mask in doublings(lax.axis_size("exp")):
        x = jnp.concatenate([x, swap(x, "exp", mask)], axis=0)
    return x


def block_offsets(size):
    offsets = [0]
    for mask in doublings(size):
        offsets = offsets + [o ^ mask for o in offsets]
    return offsets


def behind(x, *others):
    return lax.optimization_barrier((x, *others))[0]


def scatter_masks():
    return doublings(lax.axis_size("exp"))[::-1]


def add_swapped(keep, send, mask, wait):
    return keep + behind(swap(send, "exp", mask), *wait).astype(jnp.float32)


def halves(x, groups):
    low, high, start = [], [], 0
    for g in groups:
        low.append(x[start : start + g])
        high.append(x[start + g : start + 2 * g])
        start += 2 * g
    keep = jnp.concatenate(low, axis=0) if len(low) > 1 else low[0]
    send = jnp.concatenate(high, axis=0) if len(high) > 1 else high[0]
    return keep, send.astype(jnp.bfloat16)


def scatter_steps(keep, send, groups, first, waits):
    masks = scatter_masks()
    groups = [g >> (first + 1) for g in groups]
    for k in range(first, len(masks) - 1):
        x = add_swapped(keep, send, masks[k], waits.get(k, ()))
        keep, send = halves(x, groups)
        groups = [g // 2 for g in groups]
    return add_swapped(keep, send, masks[-1], waits.get(len(masks) - 1, ()))


def exchange(own, send):
    masks = doublings(lax.axis_size("feat"))
    for mask in masks[:-1]:
        own = own + swap(send, "feat", mask).astype(jnp.float32)
        send = own.astype(jnp.bfloat16)
    return own, swap(send, "feat", masks[-1])


def tile_of(size):
    return next(t for t in (512, 256, LANES) if size % t == 0)


def whole():
    return pl.BlockSpec(memory_space=pltpu.VMEM)


def untouched():
    return pl.BlockSpec(memory_space=pl.ANY)


def params(limit=VMEM_LIMIT):
    return pltpu.CompilerParams(vmem_limit_bytes=limit)


def cost(flops, size):
    return pl.CostEstimate(flops=flops, bytes_accessed=size, transcendentals=0)


def stream(weight_ref, rows, first, tile, tiles, held, sems):
    def copy(j):
        columns = pl.ds(pl.multiple_of(first + j * tile, tile), tile)
        return pltpu.make_async_copy(weight_ref.at[rows, columns], held.at[j], sems.at[j])

    for j in range(tiles):
        copy(j).start()
    return copy


def encode_kernel(first, count, tokens_ref, weight_ref, *refs):
    own_ref, send_ref, held, sems = refs[-4:]
    depth = weight_ref.shape[0]
    tiles, _, tile = held.shape
    copy = stream(weight_ref, slice(0, depth), first, tile, tiles, held, sems)

    def step(j, carry):
        copy(j).wait()
        here = pl.ds(pl.multiple_of(j * tile, tile), tile)
        part = jnp.dot(tokens_ref[:, :depth], held[j], preferred_element_type=jnp.float32)
        own_ref[:, here] = part
        send_ref[:, here] = part.astype(send_ref.dtype)
        return carry

    lax.fori_loop(0, tiles, step, 0)


def encode(rows, weight, first, last, after):
    depth, count = weight.shape[0], last - first
    tile = tile_of(count)
    tiles = count // tile
    return pl.pallas_call(
        functools.partial(encode_kernel, first, count),
        out_shape=[
            jax.ShapeDtypeStruct((rows.shape[0], count), jnp.float32),
            jax.ShapeDtypeStruct((rows.shape[0], count), jnp.bfloat16),
        ],
        in_specs=[whole(), pl.BlockSpec(memory_space=pltpu.HBM)] + [untouched()] * len(after),
        out_specs=[whole(), whole()],
        scratch_shapes=[
            pltpu.VMEM((tiles, depth, tile), weight.dtype),
            pltpu.SemaphoreType.DMA((tiles,)),
        ],
        compiler_params=params(),
        cost_estimate=cost(rows.shape[0] * depth * count // FRACTION, depth * count // FRACTION),
    )(rows, weight, *after)


def expert_kernel(pick0_ref, pick1_ref, rows0_ref, rows1_ref, gate_ref, up_ref, *refs):
    own_ref, send_ref, rows, held, sems = refs[-5:]
    _, depth, width = gate_ref.shape
    tiles, _, tile = held.shape
    each = tiles // 2

    def copy(ref, j, slot):
        columns = slice(j * tile, (j + 1) * tile)
        return pltpu.make_async_copy(ref.at[0, :, columns], held.at[slot], sems.at[slot])

    copies = [copy(gate_ref, j, j) for j in range(each)]
    copies += [copy(up_ref, j, each + j) for j in range(each)]
    for c in copies:
        c.start()
    for first in range(0, depth, 512):
        last = min(first + 512, depth)
        part = jnp.dot(
            pick0_ref[...], rows0_ref[:, first:last], preferred_element_type=jnp.float32
        )
        part += jnp.dot(
            pick1_ref[...], rows1_ref[:, first:last], preferred_element_type=jnp.float32
        )
        rows[:, first:last] = part.astype(rows.dtype)
    for j in range(tiles):
        copies[j].wait()
        part = jnp.dot(rows[...], held[j], preferred_element_type=jnp.float32)
        own_ref[:, j * tile : (j + 1) * tile] = part
        send_ref[:, j * tile : (j + 1) * tile] = part.astype(send_ref.dtype)


def expert_halves(picks, rows, gate, up, after):
    capacity, depth, width = picks[0].shape[0], gate.shape[1], gate.shape[2]
    tile = tile_of(width)
    tiles = 2 * (width // tile)
    hbm = pl.BlockSpec(memory_space=pltpu.HBM)
    return pl.pallas_call(
        expert_kernel,
        out_shape=[
            jax.ShapeDtypeStruct((capacity, 2 * width), jnp.float32),
            jax.ShapeDtypeStruct((capacity, 2 * width), jnp.bfloat16),
        ],
        in_specs=[whole()] * 4 + [hbm, hbm] + [untouched()] * len(after),
        out_specs=[whole(), whole()],
        scratch_shapes=[
            pltpu.VMEM((capacity, depth), jnp.bfloat16),
            pltpu.VMEM((tiles, depth, tile), gate.dtype),
            pltpu.SemaphoreType.DMA((tiles,)),
        ],
        compiler_params=params(ROWS_LIMIT),
        cost_estimate=cost(2 * capacity * depth * width // FRACTION, 2 * depth * width // FRACTION),
    )(*picks, *rows, gate, up, *after)


def decode_kernel(start, first, last, own_ref, recv_ref, bias_ref, pick_ref, want_ref, weight_ref, *refs):
    act, held, sems = refs[-3:]
    refs = refs[:-2]
    count, width = own_ref.shape[1], weight_ref.shape[1]
    tiles, _, tile = held.shape
    copy = stream(weight_ref, slice(start, start + count), 0, tile, tiles, held, sems)
    pre = own_ref[...] + recv_ref[...].astype(jnp.float32) + bias_ref[...]
    rows, extra = own_ref.shape[0], act.shape[0] - own_ref.shape[0]
    act[:rows] = jnp.maximum(pre, 0.0).astype(act.dtype)
    if extra:
        act[rows:] = want_ref[...]

    def put(part, columns):
        if not first:
            part = part + refs[0][:, columns]
        if last:
            start = 0
            for ref in refs[-3:-1]:
                ref[: rows // 2, columns] = part[start * rows // 2 : (start + 1) * rows // 2]
                if extra:
                    at = rows + start * extra // 2
                    ref[rows // 2 :, columns] = part[at : at + extra // 2]
                start += 1
        else:
            refs[-2][:, columns] = part

    def step(j, carry):
        columns = pl.ds(pl.multiple_of(j * tile, tile), tile)
        copy(j).wait()
        put(jnp.dot(act[...], held[j], preferred_element_type=jnp.float32), columns)
        return carry

    lax.fori_loop(0, tiles, step, 0)
    put(
        jnp.dot(act[...], pick_ref[...], preferred_element_type=jnp.float32),
        slice(width, width + LANES),
    )


def decode(own, recv, bias, pick, want, weight, start, total, last, after):
    rows, count = own.shape
    width = weight.shape[1]
    extra = 0 if want is None else want.shape[0]
    tile = tile_of(width)
    tiles = width // tile
    first = total is None
    if last:
        out_shape = [
            jax.ShapeDtypeStruct(((rows + extra) // 2, width + LANES), jnp.float32)
        ] * 2
    else:
        out_shape = [jax.ShapeDtypeStruct((rows + extra, width + LANES), jnp.float32)]
    operands = [
        own,
        recv,
        bias[start : start + count].reshape(1, count),
        pick[start : start + count],
        pick[:8, :8] if want is None else want[:, start : start + count],
        weight,
    ]
    in_specs = [whole()] * 5 + [pl.BlockSpec(memory_space=pltpu.HBM)]
    if not first:
        operands.append(total)
        in_specs.append(whole())
    out = pl.pallas_call(
        functools.partial(decode_kernel, start, first, last),
        out_shape=out_shape,
        in_specs=in_specs + [untouched()] * len(after),
        out_specs=[whole()] * len(out_shape),
        scratch_shapes=[
            pltpu.VMEM((rows + extra, count), jnp.bfloat16),
            pltpu.VMEM((tiles, count, tile), weight.dtype),
            pltpu.SemaphoreType.DMA((tiles,)),
        ],
        compiler_params=params(),
        cost_estimate=cost(rows * width * count // FRACTION, width * count // FRACTION),
    )(*operands, *after)
    return out if last else out[0]


def local(
    tokens,
    route_ids,
    route_weights,
    gate_proj,
    up_proj,
    down_proj,
    enc_weight,
    enc_bias,
    dec_weight,
    dec_bias,
    clamp_ids,
    clamp_values,
):
    expert_count = lax.axis_size("exp")
    me = lax.axis_index("exp")
    row_count, width = tokens.shape
    top = route_ids.shape[1]
    capacity = expert_count * SLOT
    feature_count = enc_weight.shape[1]
    edges = [0]
    for rows in SPLIT:
        edges.append(edges[-1] + rows)

    weights_high = route_weights.astype(jnp.bfloat16)
    weights_low = (route_weights - weights_high.astype(jnp.float32)).astype(jnp.bfloat16)
    routing = jnp.concatenate(
        [route_ids.astype(jnp.bfloat16), weights_high, weights_low], axis=1
    )
    outgoing = jnp.concatenate(
        [tokens, jnp.pad(routing, ((0, 0), (0, LANES - 3 * top)))], axis=1
    )
    gathered = [gather_blocks(outgoing[a:b]) for a, b in zip(edges, edges[1:])]

    local_ids = clamp_ids - me * feature_count
    offsets = jnp.array(block_offsets(expert_count), dtype=jnp.int32)
    clamp_count = clamp_ids.shape[0]
    each = clamp_count // expert_count
    turn = (me ^ offsets)[:, None] * each + jnp.arange(each, dtype=jnp.int32)[None, :]
    turn = turn.reshape(-1)[:, None] == jnp.arange(clamp_count, dtype=jnp.int32)[None, :]
    turned_ids = jnp.sum(jnp.where(turn, local_ids[None, :], 0), axis=1)
    features = jnp.arange(feature_count, dtype=jnp.int32)
    clamp_pick = (features[:, None] == local_ids[None, :]).astype(jnp.bfloat16)
    clamp_pick = jnp.pad(clamp_pick, ((0, 0), (0, -clamp_count % LANES)))
    clamp_want = (features[None, :] == turned_ids[:, None]).astype(jnp.bfloat16)

    cuts = [[feature_count * c // cut[-1] for c in cut] for cut in CUTS]
    own, recv, sends = {}, {}, {}

    def send_part(h, c, after):
        mine, send = encode(gathered[h], enc_weight, cuts[h][c], cuts[h][c + 1], after)
        sends[h, c] = send
        own[h, c], recv[h, c] = exchange(mine, send)

    send_part(0, 0, [])

    routed = jnp.concatenate(
        [
            g[:, width:].reshape(expert_count, rows, LANES)
            for g, rows in zip(gathered, SPLIT)
        ],
        axis=1,
    ).astype(jnp.float32)
    named = routed[:, :, :top].astype(jnp.int32) == me
    share = routed[:, :, top : 2 * top] + routed[:, :, 2 * top : 3 * top]
    share = jnp.sum(jnp.where(named, share, 0.0), axis=2)
    hit = jnp.any(named, axis=2)
    order = jnp.arange(row_count)
    earlier = order[None, :] < order[:, None]
    slot = jnp.sum((hit[:, None, :] & earlier[None]).astype(jnp.int32), axis=2)
    place = jnp.arange(expert_count, dtype=jnp.int32)[:, None] * SLOT + slot
    code = jnp.where(hit & (slot < SLOT), place, -1)
    targets = jnp.arange(capacity, dtype=jnp.int32)
    picks = [
        (code[:, a:b].reshape(-1)[None, :] == targets[:, None]).astype(jnp.bfloat16)
        for a, b in zip(edges, edges[1:])
    ]
    both_part, both_send = expert_halves(
        picks, gathered, gate_proj, up_proj, [sends[0, 0]]
    )
    both_own, both_recv = exchange(both_part, both_send)

    send_part(0, 1, [both_send])
    send_part(1, 0, [sends[0, 1], recv[0, 0]])

    both = both_own + behind(both_recv, sends[1, 0]).astype(jnp.float32)
    hidden_width = gate_proj.shape[2]
    hidden = (jax.nn.silu(both[:, :hidden_width]) * both[:, hidden_width:]).astype(jnp.bfloat16)
    expert_out = jnp.dot(hidden, down_proj[0], preferred_element_type=jnp.float32).astype(
        jnp.bfloat16
    )

    def returned(a, b):
        picker = (code[a:b].reshape(-1)[:, None] == targets[None, :]).astype(jnp.bfloat16)
        rows = jnp.dot(picker, expert_out, preferred_element_type=jnp.float32)
        return rows * share[a:b].reshape(-1)[:, None]

    send_part(1, 1, [sends[1, 0], recv[0, 1]])

    half = expert_count // 2
    moe_send = returned(half, expert_count).astype(jnp.bfloat16)

    moe_rows = moe_send.shape[0]
    mask = scatter_masks()[0]
    moe_keep, moe_next = halves(
        add_swapped(returned(0, half), moe_send, mask, [recv[1, 0]]), [moe_rows // 2]
    )

    def rebuild(h, c, total, want, after):
        start, last = cuts[h][c], c == len(cuts[h]) - 2
        return decode(
            own[h, c], recv[h, c], enc_bias, clamp_pick, want, dec_weight, start, total, last, after
        )

    part = rebuild(0, 0, None, clamp_want, [sends[1, 1]])
    keep, send = rebuild(0, 1, part, clamp_want, [recv[1, 0]])
    part = rebuild(1, 0, None, None, [send, moe_next])
    groups = [keep.shape[0] - clamp_count // 2, clamp_count // 2]
    first = add_swapped(keep, send, mask, [part, recv[1, 1]])
    first_keep, first_next = halves(first, [g // 2 for g in groups])
    last_keep, last_send = rebuild(1, 1, part, None, [first_next, moe_next])
    second_keep, second_next = halves(
        add_swapped(last_keep, last_send, mask, []), [last_keep.shape[0] // 2]
    )
    moe_out = scatter_steps(moe_keep, moe_next, [moe_rows], 1, {1: [second_next]})
    first = scatter_steps(first_keep, first_next, groups, 1, {1: [second_next]})
    rows_dec = gather_blocks(first[SPLIT[0] :, :width].astype(jnp.bfloat16))
    second = scatter_steps(second_keep, second_next, [last_keep.shape[0]], 1, {})
    summed = jnp.concatenate([first[: SPLIT[0]], second], axis=0)
    chosen = summed[:, width : width + clamp_count]
    change = clamp_values.astype(jnp.float32)[None, :] - chosen
    change = jnp.dot(change, turn.T.astype(jnp.float32), precision=lax.Precision.HIGHEST)
    shift = jnp.dot(change, rows_dec.astype(jnp.float32), precision=lax.Precision.HIGHEST)
    error_term = moe_out - summed[:, :width] - dec_bias
    steered = moe_out + shift
    return (error_term, steered)


def solution(mesh):
    placed = (
        P("exp", "feat"),
        P("exp", None),
        P("exp", None),
        P("exp", "feat", None),
        P("exp", "feat", None),
        P("exp", None, "feat"),
        P("feat", "exp"),
        P("exp"),
        P("exp", "feat"),
        P("feat"),
        P(),
        P(),
    )
    return jax.shard_map(
        local,
        mesh=mesh,
        in_specs=placed,
        out_specs=(P("exp", "feat"), P("exp", "feat")),
        check_vma=False,
    )
```

time: 334 us -> 183 us (0.55)
  waiting for transfers between devices: 202 us -> 53.2 us
  Pallas kernels: 0 us -> 59.8 us
  matrix products: 47.9 us -> 5.35 us
  blocking collectives: 33.7 us -> 0 us
  starting transfers between devices: 5.92 us -> 38.3 us
  local copies, waits for them, and re-layouts: 23.2 us -> 9.41 us
  between operations: 13.9 us -> 1.43 us
  other arithmetic: 6.77 us -> 14.6 us
    psum x1 -> x0, waiting for transfers between devices: 115 us -> none  [local(): lax.psum((partial_pre, gate_part, up_part), 'feat')]
    pallas_call x0 -> x9, Pallas kernels: none -> 59.8 us  [the longest x4 26.4 us: decode(): pl.pallas_call(functools.partial(decode_kernel, start, first, last), out_...]
    reduce_scatter x1 -> x0, waiting for transfers between devices: 59.7 us -> none  [local(): lax.psum_scatter(jnp.concatenate([rebuilt_rows, shift_part], axis=1), 'ex...]
    ppermute x0 -> x29, waiting for transfers between devices: none -> 53.2 us  [swap(): return lax.ppermute(x, axis, [(i, i ^ mask) for i in range(size)])]
    dot_general x7 -> x4, matrix products: 42.7 us -> 4.16 us  [the longest x2 2.98 us: returned(): rows = jnp.dot(picker, expert_out, preferred_element_type=jnp.float32)]
    ppermute x0 -> x29, starting transfers between devices: none -> 38.3 us  [swap(): return lax.ppermute(x, axis, [(i, i ^ mask) for i in range(size)])]
    all_to_all x1 -> x0, blocking collectives: 33.7 us -> none  [local(): lax.all_to_all(outgoing.reshape(expert_count, SLOT, shard_width), 'exp',...]
    all_to_all x1 -> x0, waiting for transfers between devices: 20.6 us -> none  [local(): lax.all_to_all(expert_out.reshape(expert_count, SLOT, shard_width), 'exp'...]
  transfers between devices with their start and end apart: 4 -> 29, of which waited for: 4 -> 16; matrix products, arithmetic and copies ran while one was open for 9% -> 9% of each run, Pallas kernels for 0% -> 26%
where the time goes in v3:
time: 183 us; the launch traced here: 182 us
  Pallas kernels  59.8 us (33%)
  waiting for transfers between devices  53.2 us (29%)
  starting transfers between devices  38.3 us (21%)
  other arithmetic  14.6 us (8%)
  local copies, waits for them, and re-layouts  9.41 us (5%)
  matrix products  5.35 us (3%)
    ppermute x29, waiting for transfers between devices, swap(): return lax.ppermute(x, axis, [(i, i ^ mask) for i in range(size)])  53.2 us
    ppermute x29, starting transfers between devices, swap(): return lax.ppermute(x, axis, [(i, i ^ mask) for i in range(size)])  38.3 us
    pallas_call x4, Pallas kernels, decode(): pl.pallas_call(functools.partial(decode_kernel, start, first, last), out_...  26.4 us
    pallas_call x4, Pallas kernels, encode(): pl.pallas_call(functools.partial(encode_kernel, first, count), out_shape=...  24.6 us
    pallas_call x1, Pallas kernels, expert_halves(): pl.pallas_call(expert_kernel, out_shape=[jax.ShapeDtypeStruct((capacity,...  8.75 us
    unnamed x59, local copies, waits for them, and re-layouts  6.29 us
  transfers between devices with their start and end apart: 29, of which 16 were waited for; matrix products, arithmetic and copies ran while one was open for 9% of the time, Pallas kernels for 26%

profile of v3, /device:TPU:0, one launch (start us, length us, event | category | flops | bytes accessed | tf_op | source)
XLA Modules:
  0.0 182.1 jit_solution(16773143512298611941)
XLA Ops:
  0.6 0.7 convert_element_type.97
  1.3 0.8 copy.25
  2.1 0.7 convert_element_type.96
  3.0 0.9 constant_dynamic-update-slice_fusion.9
  3.9 4.1 %collective-permute-start.4 = (bf16[8,3712]{1,0:T(8,128)(2,1)S(1)}, bf16[8,3712]{1,0:T(8,128)(2,1)S(1)}, u32[]{:S(2)}, u32[]{:S(2)}) collective-permute-start(bf16[8,3712]{1,0:T(8,128)(2,1)S(1)} %get-tuple-element.49), channel_id=1, source_target_pairs={{0,16},{2,18},{4,20},{6,22},{8,24},{10,26},{12,28},{14,30},{16,0},... | collective-permute-start | bytes 178184 | tf_op jit(solution)/shard_map/ppermute | solution.py:21
  8.1 0.7 xor_multiply_fusion
  8.9 0.7 broadcast_subtract_fusion
  10.1 0.8 fusion.41
  10.9 0.9 fusion.7
  12.1 1.9 %collective-permute-start.5 = (bf16[16,3712]{1,0:T(8,128)(2,1)S(1)}, bf16[16,3712]{1,0:T(8,128)(2,1)S(1)}, u32[]{:S(2)}, u32[]{:S(2)}) collective-permute-start(bf16[16,3712]{1,0:T(8,128)(2,1)S(1)} %pad_maximum_fusion.8), channel_id=1, source_target_pairs={{0,8},{2,10},{4,12},{6,14},{8,0},{10,2},{12,4},{14,6},{16,24},{18,... | collective-permute-start | bytes 356360 | tf_op jit(solution)/shard_map/ppermute | solution.py:21
  14.0 0.8 collective-permute-start.1
  14.8 3.4 %collective-permute-done.5 = bf16[16,3712]{1,0:T(8,128)(2,1)S(1)} collective-permute-done((bf16[16,3712]{1,0:T(8,128)(2,1)S(1)}, bf16[16,3712]{1,0:T(8,128)(2,1)S(1)}, u32[]{:S(2)}, u32[]{:S(2)}) %collective-permute-start.5) | collective-permute-done | bytes 118816 | tf_op jit(solution)/shard_map/ppermute | solution.py:21
  18.3 1.8 %collective-permute-start.6 = (bf16[32,3712]{1,0:T(8,128)(2,1)S(1)}, bf16[32,3712]{1,0:T(8,128)(2,1)S(1)}, u32[]{:S(2)}, u32[]{:S(2)}) collective-permute-start(bf16[32,3712]{1,0:T(8,128)(2,1)S(1)} %pad_maximum_fusion.4), channel_id=1, source_target_pairs={{0,4},{2,6},{4,0},{6,2},{8,12},{10,14},{12,8},{14,10},{16,20},{18,... | collective-permute-start | bytes 712712 | tf_op jit(solution)/shard_map/ppermute | solution.py:21
  20.1 0.9 pad_maximum_fusion.3
  21.0 1.2 collective-permute-start.2
  22.2 7.3 %collective-permute-done.2 = bf16[32,3712]{1,0:T(8,128)(2,1)S(1)} collective-permute-done((bf16[32,3712]{1,0:T(8,128)(2,1)S(1)}, bf16[32,3712]{1,0:T(8,128)(2,1)S(1)}, u32[]{:S(2)}, u32[]{:S(2)}) %collective-permute-start.2) | collective-permute-done | bytes 237600 | tf_op jit(solution)/shard_map/ppermute | solution.py:21
  29.5 0.9 pad_maximum_fusion
  31.2 1.2 collective-permute-done.3
  34.3 6.0 %shard_map.140 = (f32[128,2048]{1,0:T(8,128)S(1)}, bf16[128,2048]{1,0:T(8,128)(2,1)S(1)}) custom-call(bf16[128,3712]{1,0:T(8,128)(2,1)S(1)} %constant_dynamic-update-slice_fusion.tokens_ref.rows0_ref, bf16[3584,4096]{1,0:T(8,128)(2,1)} %weight_ref.11), custom_call_target="tpu_custom_call" | custom-call | flops 469762048 | bytes 3670016 | tf_op jit(solution)/shard_map/pallas_call | solution.py:137
  40.4 1.0 copy-done.8
  41.4 1.7 collective-permute-start.9
  43.7 8.8 %shard_map.141 = (f32[128,2048]{1,0:T(8,128)}, bf16[128,2048]{1,0:T(8,128)(2,1)}) custom-call(bf16[128,128]{1,0:T(8,128)(2,1)} %get-tuple-element.66.pick0_ref, bf16[128,128]{1,0:T(8,128)(2,1)} %get-tuple-element.67.pick1_ref, bf16[128,3712]{1,0:T(8,128)(2,1)} %copy-done.2, bf16[128,3712]{1,0:T(8,128)(2,1)} %copy-done, bf16[1,3584,1024]{2,1,0:T(8,128)(2,1)} %gate_ref.1, ...), custom_call_target="tpu_custom_call" | custom-call | flops 469762048 | bytes 3670016 | tf_op jit(solution)/shard_map/pallas_call | solution.py:189
  53.1 1.0 copy-done.12
  54.1 6.0 %shard_map.142 = (f32[128,2048]{1,0:T(8,128)S(1)}, bf16[128,2048]{1,0:T(8,128)(2,1)S(1)}) custom-call(bf16[128,3712]{1,0:T(8,128)(2,1)S(1)} %copy-done.3, bf16[3584,4096]{1,0:T(8,128)(2,1)} %weight_ref.11, bf16[128,2048]{1,0:T(8,128)(2,1)S(1)} %copy-done.12), custom_call_target="tpu_custom_call" | custom-call | flops 469762048 | bytes 3670016 | tf_op jit(solution)/shard_map/pallas_call | solution.py:137
  60.2 1.8 collective-permute-start.13
  61.9 6.6 %shard_map.143 = (f32[128,2048]{1,0:T(8,128)S(1)}, bf16[128,2048]{1,0:T(8,128)(2,1)S(1)}) custom-call(bf16[128,3712]{1,0:T(8,128)(2,1)S(1)} %copy-done.1, bf16[3584,4096]{1,0:T(8,128)(2,1)} %weight_ref.11, bf16[128,2048]{1,0:T(8,128)(2,1)S(1)} %get-tuple-element.24.refs_0_, bf16[128,2048]{1,0:T(8,128)(2,1)S(1)} %collective-permute-done.9.refs_1_.recv_ref), custom_call_target="tpu_custom_call" | custom-call | flops 469762048 | bytes 3670016 | tf_op jit(solution)/shard_map/pallas_call | solution.py:137
  68.7 1.4 convert_add_fusion.1
  70.2 1.2 fusion.3
  71.4 1.4 fusion.2
  72.8 6.0 %collective-permute-done.13.refs_1_.recv_ref = bf16[128,2048]{1,0:T(8,128)(2,1)S(1)} collective-permute-done((bf16[128,2048]{1,0:T(8,128)(2,1)S(1)}, bf16[128,2048]{1,0:T(8,128)(2,1)S(1)}, u32[]{:S(2)}, u32[]{:S(2)}) %collective-permute-start.13) | collective-permute-done | bytes 524320 | tf_op jit(solution)/shard_map/ppermute | solution.py:21
  78.8 6.0 %shard_map.144 = (f32[128,2048]{1,0:T(8,128)S(1)}, bf16[128,2048]{1,0:T(8,128)(2,1)S(1)}) custom-call(bf16[128,3712]{1,0:T(8,128)(2,1)S(1)} %copy-done.1, bf16[3584,4096]{1,0:T(8,128)(2,1)} %weight_ref.11, bf16[128,2048]{1,0:T(8,128)(2,1)S(1)} %get-tuple-element.25.refs_0_, bf16[128,2048]{1,0:T(8,128)(2,1)S(1)} %collective-permute-done.13.refs_1_.recv_ref), custom_call_target="tpu_custom_call" | custom-call | flops 469762048 | bytes 3670016 | tf_op jit(solution)/shard_map/pallas_call | solution.py:137
  84.8 1.0 copy-done.10
  85.8 6.3 %shard_map.145.refs_0_ = f32[192,3712]{1,0:T(8,128)S(1)} custom-call(f32[128,2048]{1,0:T(8,128)S(1)} %copy-done.9, bf16[128,2048]{1,0:T(8,128)(2,1)S(1)} %collective-permute-done.9.refs_1_.recv_ref, f32[1,2048]{1,0:T(1,128)S(1)} %bitcast.17, bf16[2048,128]{1,0:T(8,128)(2,1)S(1)} %get-tuple-element.52.pick_ref, ...), custom_call_target="tpu_custom_call" | custom-call | flops 469762048 | bytes 3670016 | tf_op jit(solution)/shard_map/pallas_call | solution.py:271
  92.1 7.5 %shard_map.146 = (f32[96,3712]{1,0:T(8,128)S(1)}, f32[96,3712]{1,0:T(8,128)}) custom-call(f32[128,2048]{1,0:T(8,128)S(1)} %get-tuple-element.31.own_ref, bf16[128,2048]{1,0:T(8,128)(2,1)S(1)} %collective-permute-done.13.refs_1_.recv_ref, f32[1,2048]{1,0:T(1,128)S(1)} %bitcast.15, bf16[2048,128]{1,0:T(8,128)(2,1)S(1)} %get-tuple-element.53.pick_ref, ...), custom_call_target="tpu_custom_call" | custom-call | flops 469762048 | bytes 3670016 | tf_op jit(solution)/shard_map/pallas_call | solution.py:271
  99.6 1.1 copy-done.4
  100.7 0.7 slice.236.want_ref
  101.6 1.5 collective-permute-start.14
  103.1 1.6 convolution_multiply_fusion.1
  104.7 1.5 convert_add_fusion
  106.3 6.2 %shard_map.147.refs_0_ = f32[128,3712]{1,0:T(8,128)S(1)} custom-call(f32[128,2048]{1,0:T(8,128)S(1)} %copy-done.7, bf16[128,2048]{1,0:T(8,128)(2,1)S(1)} %collective-permute-done.11.refs_1_.recv_ref, f32[1,2048]{1,0:T(1,128)S(1)} %bitcast.18, bf16[2048,128]{1,0:T(8,128)(2,1)S(1)} %get-tuple-element.52.pick_ref, bf16[8,8]{1,0:T(8,128)(2,1)S(1)} %slice.236.want_ref, ...), custom_call_target="tpu_custom_call" | custom-call | flops 469762048 | bytes 3670016 | tf_op jit(solution)/shard_map/pallas_call | solution.py:271
  112.5 3.4 %collective-permute-done.14.recv_ref = bf16[128,2048]{1,0:T(8,128)(2,1)S(1)} collective-permute-done((bf16[128,2048]{1,0:T(8,128)(2,1)S(1)}, bf16[128,2048]{1,0:T(8,128)(2,1)S(1)}, u32[]{:S(2)}, u32[]{:S(2)}) %collective-permute-start.14) | collective-permute-done | bytes 524320 | tf_op jit(solution)/shard_map/ppermute | solution.py:21
  115.9 1.6 fusion.37
  117.6 1.1 copy-done.11
  118.8 6.4 %shard_map.148 = (f32[64,3712]{1,0:T(8,128)S(1)}, f32[64,3712]{1,0:T(8,128)S(1)}) custom-call(f32[128,2048]{1,0:T(8,128)S(1)} %copy-done.11, bf16[128,2048]{1,0:T(8,128)(2,1)S(1)} %collective-permute-done.14.recv_ref, f32[1,2048]{1,0:T(1,128)S(1)} %bitcast.16, bf16[2048,128]{1,0:T(8,128)(2,1)S(1)} %get-tuple-element.53.pick_ref, ...), custom_call_target="tpu_custom_call" | custom-call | flops 469762048 | bytes 3670016 | tf_op jit(solution)/shard_map/pallas_call | solution.py:271
  125.2 1.6 collective-permute-start.19
  127.9 8.5 %collective-permute-done.19 = bf16[48,3712]{1,0:T(8,128)(2,1)S(1)} collective-permute-done((bf16[48,3712]{1,0:T(8,128)(2,1)S(1)}, bf16[48,3712]{1,0:T(8,128)(2,1)S(1)}, u32[]{:S(2)}, u32[]{:S(2)}) %collective-permute-start.19) | collective-permute-done | bytes 356384 | tf_op jit(solution)/shard_map/ppermute | solution.py:21
  136.6 1.6 collective-permute-start.22
  138.2 8.1 %collective-permute-done.12 = bf16[64,3584]{1,0:T(8,128)(2,1)S(1)} collective-permute-done((bf16[64,3584]{1,0:T(8,128)(2,1)S(1)}, bf16[64,3584]{1,0:T(8,128)(2,1)S(1)}, u32[]{:S(2)}, u32[]{:S(2)}) %collective-permute-start.12) | collective-permute-done | bytes 458784 | tf_op jit(solution)/shard_map/ppermute | solution.py:21
  146.3 1.1 collective-permute-start.20
  147.5 1.1 collective-permute-start.17
  148.5 5.2 %collective-permute-done.20 = bf16[24,3712]{1,0:T(8,128)(2,1)S(1)} collective-permute-done((bf16[24,3712]{1,0:T(8,128)(2,1)S(1)}, bf16[24,3712]{1,0:T(8,128)(2,1)S(1)}, u32[]{:S(2)}, u32[]{:S(2)}) %collective-permute-start.20) | collective-permute-done | bytes 178208 | tf_op jit(solution)/shard_map/ppermute | solution.py:21
  153.9 2.8 %collective-permute-start.21 = (bf16[12,3712]{1,0:T(8,128)(2,1)S(1)}, bf16[12,3712]{1,0:T(8,128)(2,1)S(1)}, u32[]{:S(2)}, u32[]{:S(2)}) collective-permute-start(bf16[12,3712]{1,0:T(8,128)(2,1)S(1)} %pad_maximum_fusion.9), channel_id=1, source_target_pairs={{0,16},{2,18},{4,20},{6,22},{8,24},{10,26},{12,28},{14,30},{16,0},... | collective-permute-start | bytes 267272 | tf_op jit(solution)/shard_map/ppermute | solution.py:21
  156.7 1.5 collective-permute-done.17
  158.2 2.8 %collective-permute-start.18 = (bf16[16,3584]{1,0:T(8,128)(2,1)S(1)}, bf16[16,3584]{1,0:T(8,128)(2,1)S(1)}, u32[]{:S(2)}, u32[]{:S(2)}) collective-permute-start(bf16[16,3584]{1,0:T(8,128)(2,1)S(1)} %slice.321), channel_id=1, source_target_pairs={{0,16},{2,18},{4,20},{6,22},{8,24},{10,26},{12,28},{14,30},{16,0},... | collective-permute-start | bytes 344072 | tf_op jit(solution)/shard_map/ppermute | solution.py:21
  161.1 2.3 %collective-permute-done.21 = bf16[12,3712]{1,0:T(8,128)(2,1)S(1)} collective-permute-done((bf16[12,3712]{1,0:T(8,128)(2,1)S(1)}, bf16[12,3712]{1,0:T(8,128)(2,1)S(1)}, u32[]{:S(2)}, u32[]{:S(2)}) %collective-permute-start.21) | collective-permute-done | bytes 89120 | tf_op jit(solution)/shard_map/ppermute | solution.py:21
  163.6 5.8 %collective-permute-start.23 = (bf16[16,3712]{1,0:T(8,128)(2,1)S(1)}, bf16[16,3712]{1,0:T(8,128)(2,1)S(1)}, u32[]{:S(2)}, u32[]{:S(2)}) collective-permute-start(bf16[16,3712]{1,0:T(8,128)(2,1)S(1)} %slice.320), channel_id=1, source_target_pairs={{0,8},{2,10},{4,12},{6,14},{8,0},{10,2},{12,4},{14,6},{16,24},{18,... | collective-permute-start | bytes 356360 | tf_op jit(solution)/shard_map/ppermute | solution.py:21
  169.5 1.8 collective-permute-start.26
  171.2 1.6 collective-permute-done.23
  172.9 1.5 collective-permute-start.24
  174.5 1.6 collective-permute-start.27
  176.0 2.0 %collective-permute-done.24 = bf16[8,3712]{1,0:T(8,128)(2,1)S(1)} collective-permute-done((bf16[8,3712]{1,0:T(8,128)(2,1)S(1)}, bf16[8,3712]{1,0:T(8,128)(2,1)S(1)}, u32[]{:S(2)}, u32[]{:S(2)}) %collective-permute-start.24) | collective-permute-done | bytes 59424 | tf_op jit(solution)/shard_map/ppermute | solution.py:21
  178.1 1.2 collective-permute-done.27
  179.5 0.7 fusion.13
  181.1 1.0 convolution_add_fusion
  (154 shorter events, 8.5 us)
Async XLA Ops:
  3.9 10.1 %copy-start.20 = (bf16[8,3712]{1,0:T(8,128)(2,1)}, bf16[8,3712]{1,0:T(8,128)(2,1)S(1)}, u32[]{:S(2)}) copy-start(bf16[8,3712]{1,0:T(8,128)(2,1)S(1)} %get-tuple-element.57) | copy-start | bytes 178180
  3.9 8.1 %collective-permute-start.4 = (bf16[8,3712]{1,0:T(8,128)(2,1)S(1)}, bf16[8,3712]{1,0:T(8,128)(2,1)S(1)}, u32[]{:S(2)}, u32[]{:S(2)}) collective-permute-start(bf16[8,3712]{1,0:T(8,128)(2,1)S(1)} %get-tuple-element.49), channel_id=1, source_target_pairs={{0,16},{2,18},{4,20},{6,22},{8,24},{10,26},{12,28},{14,30},{16,0},... | collective-permute-start | bytes 178184 | tf_op jit(solution)/shard_map/ppermute | solution.py:21
  8.0 6.0 %collective-permute-start = (bf16[8,3712]{1,0:T(8,128)(2,1)S(1)}, bf16[8,3712]{1,0:T(8,128)(2,1)S(1)}, u32[]{:S(2)}, u32[]{:S(2)}) collective-permute-start(bf16[8,3712]{1,0:T(8,128)(2,1)S(1)} %get-tuple-element.57), channel_id=1, source_target_pairs={{0,16},{2,18},{4,20},{6,22},{8,24},{10,26},{12,28},{14,30},{16,0},... | collective-permute-start | bytes 178184 | tf_op jit(solution)/shard_map/ppermute | solution.py:21
  9.9 8.4 %copy-start.14 = (bf16[4096,64]{1,0:T(8,128)(2,1)}, bf16[4096,64]{1,0:T(8,128)(2,1)S(1)}, u32[]{:S(2)}) copy-start(bf16[4096,64]{1,0:T(8,128)(2,1)S(1)} %fusion.6) | copy-start | bytes 1572868
  12.0 6.2 %copy-start.18 = (bf16[8,3712]{1,0:T(8,128)(2,1)}, bf16[8,3712]{1,0:T(8,128)(2,1)S(1)}, u32[]{:S(2)}) copy-start(bf16[8,3712]{1,0:T(8,128)(2,1)S(1)} %collective-permute-done.4) | copy-start | bytes 178180
  12.1 6.1 %collective-permute-start.5 = (bf16[16,3712]{1,0:T(8,128)(2,1)S(1)}, bf16[16,3712]{1,0:T(8,128)(2,1)S(1)}, u32[]{:S(2)}, u32[]{:S(2)}) collective-permute-start(bf16[16,3712]{1,0:T(8,128)(2,1)S(1)} %pad_maximum_fusion.8), channel_id=1, source_target_pairs={{0,8},{2,10},{4,12},{6,14},{8,0},{10,2},{12,4},{14,6},{16,24},{18,... | collective-permute-start | bytes 356360 | tf_op jit(solution)/shard_map/ppermute | solution.py:21
  14.0 4.2 %copy-start.21 = (bf16[8,3712]{1,0:T(8,128)(2,1)}, bf16[8,3712]{1,0:T(8,128)(2,1)S(1)}, u32[]{:S(2)}) copy-start(bf16[8,3712]{1,0:T(8,128)(2,1)S(1)} %collective-permute-done) | copy-start | bytes 178180
  14.0 6.1 %collective-permute-start.1 = (bf16[16,3712]{1,0:T(8,128)(2,1)S(1)}, bf16[16,3712]{1,0:T(8,128)(2,1)S(1)}, u32[]{:S(2)}, u32[]{:S(2)}) collective-permute-start(bf16[16,3712]{1,0:T(8,128)(2,1)S(1)} %pad_maximum_fusion.7), channel_id=1, source_target_pairs={{0,8},{2,10},{4,12},{6,14},{8,0},{10,2},{12,4},{14,6},{16,24},{18,... | collective-permute-start | bytes 356360 | tf_op jit(solution)/shard_map/ppermute | solution.py:21
  18.2 12.3 %copy-start.19 = (bf16[8,3712]{1,0:T(8,128)(2,1)S(1)}, bf16[8,3712]{1,0:T(8,128)(2,1)}, u32[]{:S(2)}) copy-start(bf16[8,3712]{1,0:T(8,128)(2,1)} %copy-done.18) | copy-start | bytes 178180
  18.3 12.2 %collective-permute-start.6 = (bf16[32,3712]{1,0:T(8,128)(2,1)S(1)}, bf16[32,3712]{1,0:T(8,128)(2,1)S(1)}, u32[]{:S(2)}, u32[]{:S(2)}) collective-permute-start(bf16[32,3712]{1,0:T(8,128)(2,1)S(1)} %pad_maximum_fusion.4), channel_id=1, source_target_pairs={{0,4},{2,6},{4,0},{6,2},{8,12},{10,14},{12,8},{14,10},{16,20},{18,... | collective-permute-start | bytes 712712 | tf_op jit(solution)/shard_map/ppermute | solution.py:21
  21.0 8.5 %collective-permute-start.2 = (bf16[32,3712]{1,0:T(8,128)(2,1)S(1)}, bf16[32,3712]{1,0:T(8,128)(2,1)S(1)}, u32[]{:S(2)}, u32[]{:S(2)}) collective-permute-start(bf16[32,3712]{1,0:T(8,128)(2,1)S(1)} %pad_maximum_fusion.3), channel_id=1, source_target_pairs={{0,4},{2,6},{4,0},{6,2},{8,12},{10,14},{12,8},{14,10},{16,20},{18,... | collective-permute-start | bytes 712712 | tf_op jit(solution)/shard_map/ppermute | solution.py:21
  30.4 1.9 %collective-permute-start.3 = (bf16[64,3712]{1,0:T(8,128)(2,1)S(1)}, bf16[64,3712]{1,0:T(8,128)(2,1)S(1)}, u32[]{:S(2)}, u32[]{:S(2)}) collective-permute-start(bf16[64,3712]{1,0:T(8,128)(2,1)S(1)} %pad_maximum_fusion), channel_id=1, source_target_pairs={{0,2},{2,0},{4,6},{6,4},{8,10},{10,8},{12,14},{14,12},{16,18},{18,... | collective-permute-start | bytes 1425416 | tf_op jit(solution)/shard_map/ppermute | solution.py:21
  30.6 2.4 %collective-permute-start.7 = (bf16[64,3712]{1,0:T(8,128)(2,1)S(1)}, bf16[64,3712]{1,0:T(8,128)(2,1)S(1)}, u32[]{:S(2)}, u32[]{:S(2)}) collective-permute-start(bf16[64,3712]{1,0:T(8,128)(2,1)S(1)} %pad_maximum_fusion.1), channel_id=1, source_target_pairs={{0,2},{2,0},{4,6},{6,4},{8,10},{10,8},{12,14},{14,12},{16,18},{18,... | collective-permute-start | bytes 1425416 | tf_op jit(solution)/shard_map/ppermute | solution.py:21
  32.4 8.0 %copy-start.2 = (bf16[128,3712]{1,0:T(8,128)(2,1)}, bf16[128,3712]{1,0:T(8,128)(2,1)S(1)}, u32[]{:S(2)}) copy-start(bf16[128,3712]{1,0:T(8,128)(2,1)S(1)} %constant_dynamic-update-slice_fusion.tokens_ref.rows0_ref) | copy-start | bytes 2850820
  33.0 7.3 %copy-start = (bf16[128,3712]{1,0:T(8,128)(2,1)}, bf16[128,3712]{1,0:T(8,128)(2,1)S(1)}, u32[]{:S(2)}) copy-start(bf16[128,3712]{1,0:T(8,128)(2,1)S(1)} %constant_dynamic-update-slice_fusion.5.rows1_ref.tokens_ref) | copy-start | bytes 2850820
  40.3 1.0 copy-start.8
  41.4 2.3 %copy-start.13 = (bf16[128,2048]{1,0:T(8,128)(2,1)}, bf16[128,2048]{1,0:T(8,128)(2,1)S(1)}, u32[]{:S(2)}) copy-start(bf16[128,2048]{1,0:T(8,128)(2,1)S(1)} %get-tuple-element.21.refs_0_) | copy-start | bytes 1572868
  41.4 20.6 %collective-permute-start.9 = (bf16[128,2048]{1,0:T(8,128)(2,1)S(1)}, bf16[128,2048]{1,0:T(8,128)(2,1)S(1)}, u32[]{:S(2)}, u32[]{:S(2)}) collective-permute-start(bf16[128,2048]{1,0:T(8,128)(2,1)S(1)} %get-tuple-element.21.refs_0_), channel_id=1, source_target_pairs={{0,1},{1,0},{2,3},{3,2},{4,5},{5,4},{6,7},{7,6},{8,9},{9,8},{10,11... | collective-permute-start | bytes 1572872 | tf_op jit(solution)/shard_map/ppermute | solution.py:21
  43.7 9.3 %copy-start.3 = (bf16[128,3712]{1,0:T(8,128)(2,1)S(1)}, bf16[128,3712]{1,0:T(8,128)(2,1)}, u32[]{:S(2)}) copy-start(bf16[128,3712]{1,0:T(8,128)(2,1)} %copy-done.2) | copy-start | bytes 2850820
  52.5 16.2 %collective-permute-start.8 = (bf16[128,2048]{1,0:T(8,128)(2,1)}, bf16[128,2048]{1,0:T(8,128)(2,1)}, u32[]{:S(2)}, u32[]{:S(2)}) collective-permute-start(bf16[128,2048]{1,0:T(8,128)(2,1)} %get-tuple-element.23.refs_0_), channel_id=1, source_target_pairs={{0,1},{1,0},{2,3},{3,2},{4,5},{5,4},{6,7},{7,6},{8,9},{9,8},{10,11... | collective-permute-start | bytes 1572872 | tf_op jit(solution)/shard_map/ppermute | solution.py:21
  53.0 1.0 copy-start.12
  54.1 7.8 %copy-start.1 = (bf16[128,3712]{1,0:T(8,128)(2,1)S(1)}, bf16[128,3712]{1,0:T(8,128)(2,1)}, u32[]{:S(2)}) copy-start(bf16[128,3712]{1,0:T(8,128)(2,1)} %copy-done) | copy-start | bytes 2850820
  60.1 10.0 %slice-start = ((s8[7340032]{0:T(1024)(128)(4,1)}), s8[4194304]{0:T(1024)(128)(4,1)S(1)}, s32[]{:S(2)}) async-start(s8[7340032]{0:T(1024)(128)(4,1)} %bitcast.19), calls=%async_computation | async-start | bytes 8388608
  60.2 8.5 %copy-start.17 = (f32[128,2048]{1,0:T(8,128)S(1)}, f32[128,2048]{1,0:T(8,128)}, u32[]{:S(2)}) copy-start(f32[128,2048]{1,0:T(8,128)} %get-tuple-element.22) | copy-start | bytes 3145732
  60.2 10.0 %slice-start.1 = ((s8[7340032]{0:T(1024)(128)(4,1)}), s8[3145728]{0:T(1024)(128)(4,1)S(1)}, s32[]{:S(2)}) async-start(s8[7340032]{0:T(1024)(128)(4,1)} %bitcast.19), calls=%async_computation.1 | async-start | bytes 6291456
  60.2 18.6 %collective-permute-start.13 = (bf16[128,2048]{1,0:T(8,128)(2,1)S(1)}, bf16[128,2048]{1,0:T(8,128)(2,1)S(1)}, u32[]{:S(2)}, u32[]{:S(2)}) collective-permute-start(bf16[128,2048]{1,0:T(8,128)(2,1)S(1)} %get-tuple-element.24.refs_0_), channel_id=1, source_target_pairs={{0,1},{1,0},{2,3},{3,2},{4,5},{5,4},{6,7},{7,6},{8,9},{9,8},{10,11... | collective-permute-start | bytes 1572872 | tf_op jit(solution)/shard_map/ppermute | solution.py:21
  68.6 2.8 %copy-start.6 = (f32[128,2048]{1,0:T(8,128)}, f32[128,2048]{1,0:T(8,128)S(1)}, u32[]{:S(2)}) copy-start(f32[128,2048]{1,0:T(8,128)S(1)} %get-tuple-element.30.own_ref) | copy-start | bytes 3145732
  68.6 23.5 %collective-permute-start.11 = (bf16[128,2048]{1,0:T(8,128)(2,1)S(1)}, bf16[128,2048]{1,0:T(8,128)(2,1)S(1)}, u32[]{:S(2)}, u32[]{:S(2)}) collective-permute-start(bf16[128,2048]{1,0:T(8,128)(2,1)S(1)} %get-tuple-element.25.refs_0_), channel_id=1, source_target_pairs={{0,1},{1,0},{2,3},{3,2},{4,5},{5,4},{6,7},{7,6},{8,9},{9,8},{10,11... | collective-permute-start | bytes 1572872 | tf_op jit(solution)/shard_map/ppermute | solution.py:21
  71.4 1.4 copy-start.15
  71.4 1.4 copy-start.16
  72.8 32.0 %collective-permute-start.10 = (bf16[128,3584]{1,0:T(8,128)(2,1)}, bf16[128,3584]{1,0:T(8,128)(2,1)}, u32[]{:S(2)}, u32[]{:S(2)}) collective-permute-start(bf16[128,3584]{1,0:T(8,128)(2,1)} %fusion.2), channel_id=1, source_target_pairs={{0,2},{2,0},{4,6},{6,4},{8,10},{10,8},{12,14},{14,12},{16,18},{18,... | collective-permute-start | bytes 2752520 | tf_op jit(solution)/shard_map/ppermute | solution.py:21
  72.8 13.0 %copy-start.9 = (f32[128,2048]{1,0:T(8,128)S(1)}, f32[128,2048]{1,0:T(8,128)}, u32[]{:S(2)}) copy-start(f32[128,2048]{1,0:T(8,128)} %copy-done.8) | copy-start | bytes 3145732
  84.8 1.0 copy-start.10
  99.6 1.1 copy-start.4
  100.7 15.2 %collective-permute-start.15 = (f32[96,3712]{1,0:T(8,128)}, f32[96,3712]{1,0:T(8,128)}, u32[]{:S(2)}, u32[]{:S(2)}) collective-permute-start(f32[96,3712]{1,0:T(8,128)} %get-tuple-element.33.refs_0_), channel_id=1, source_target_pairs={{0,2},{2,0},{4,6},{6,4},{8,10},{10,8},{12,14},{14,12},{16,18},{18,... | collective-permute-start | bytes 4276232 | tf_op jit(solution)/shard_map/ppermute | solution.py:21
  101.6 14.3 %collective-permute-start.14 = (bf16[128,2048]{1,0:T(8,128)(2,1)S(1)}, bf16[128,2048]{1,0:T(8,128)(2,1)S(1)}, u32[]{:S(2)}, u32[]{:S(2)}) collective-permute-start(bf16[128,2048]{1,0:T(8,128)(2,1)S(1)} %get-tuple-element.29.refs_0_), channel_id=1, source_target_pairs={{0,1},{1,0},{2,3},{3,2},{4,5},{5,4},{6,7},{7,6},{8,9},{9,8},{10,11... | collective-permute-start | bytes 1572872 | tf_op jit(solution)/shard_map/ppermute | solution.py:21
  104.7 1.6 copy-start.7
  106.3 9.6 %copy-start.5 = (f32[96,3712]{1,0:T(8,128)S(1)}, f32[96,3712]{1,0:T(8,128)}, u32[]{:S(2)}) copy-start(f32[96,3712]{1,0:T(8,128)} %copy-done.4) | copy-start | bytes 4276228
  117.5 1.2 copy-start.11
  118.8 8.1 %copy-start.23 = (bf16[64]{0:T(256)(128)(2,1)S(1)}, bf16[64]{0:T(256)(128)(2,1)}, u32[]{:S(2)}) copy-start(bf16[64]{0:T(256)(128)(2,1)} %param.24) | copy-start | bytes 388
  125.2 2.6 %collective-permute-start.16 = (f32[64,3712]{1,0:T(8,128)S(1)}, f32[64,3712]{1,0:T(8,128)S(1)}, u32[]{:S(2)}, u32[]{:S(2)}) collective-permute-start(f32[64,3712]{1,0:T(8,128)S(1)} %get-tuple-element.37), channel_id=1, source_target_pairs={{0,2},{2,0},{4,6},{6,4},{8,10},{10,8},{12,14},{14,12},{16,18},{18,... | collective-permute-start | bytes 2850824 | tf_op jit(solution)/shard_map/ppermute | solution.py:21
  125.2 11.2 %collective-permute-start.19 = (bf16[48,3712]{1,0:T(8,128)(2,1)S(1)}, bf16[48,3712]{1,0:T(8,128)(2,1)S(1)}, u32[]{:S(2)}, u32[]{:S(2)}) collective-permute-start(bf16[48,3712]{1,0:T(8,128)(2,1)S(1)} %pad_maximum_fusion.2.refs_1_), channel_id=1, source_target_pairs={{0,4},{2,6},{4,0},{6,2},{8,12},{10,14},{12,8},{14,10},{16,20},{18,... | collective-permute-start | bytes 1069064 | tf_op jit(solution)/shard_map/ppermute | solution.py:21
  126.8 19.4 %collective-permute-start.12 = (bf16[64,3584]{1,0:T(8,128)(2,1)S(1)}, bf16[64,3584]{1,0:T(8,128)(2,1)S(1)}, u32[]{:S(2)}, u32[]{:S(2)}) collective-permute-start(bf16[64,3584]{1,0:T(8,128)(2,1)S(1)} %slice.317.refs_1_.refs_2_), channel_id=1, source_target_pairs={{0,4},{2,6},{4,0},{6,2},{8,12},{10,14},{12,8},{14,10},{16,20},{18,... | collective-permute-start | bytes 1376264 | tf_op jit(solution)/shard_map/ppermute | solution.py:21
  136.6 24.5 %collective-permute-start.22 = (bf16[32,3712]{1,0:T(8,128)(2,1)S(1)}, bf16[32,3712]{1,0:T(8,128)(2,1)S(1)}, u32[]{:S(2)}, u32[]{:S(2)}) collective-permute-start(bf16[32,3712]{1,0:T(8,128)(2,1)S(1)} %slice.318), channel_id=1, source_target_pairs={{0,4},{2,6},{4,0},{6,2},{8,12},{10,14},{12,8},{14,10},{16,20},{18,... | collective-permute-start | bytes 712712 | tf_op jit(solution)/shard_map/ppermute | solution.py:21
  146.3 7.5 %collective-permute-start.20 = (bf16[24,3712]{1,0:T(8,128)(2,1)S(1)}, bf16[24,3712]{1,0:T(8,128)(2,1)S(1)}, u32[]{:S(2)}, u32[]{:S(2)}) collective-permute-start(bf16[24,3712]{1,0:T(8,128)(2,1)S(1)} %pad_maximum_fusion.6), channel_id=1, source_target_pairs={{0,8},{2,10},{4,12},{6,14},{8,0},{10,2},{12,4},{14,6},{16,24},{18,... | collective-permute-start | bytes 534536 | tf_op jit(solution)/shard_map/ppermute | solution.py:21
  147.5 10.7 %collective-permute-start.17 = (bf16[32,3584]{1,0:T(8,128)(2,1)S(1)}, bf16[32,3584]{1,0:T(8,128)(2,1)S(1)}, u32[]{:S(2)}, u32[]{:S(2)}) collective-permute-start(bf16[32,3584]{1,0:T(8,128)(2,1)S(1)} %slice.319), channel_id=1, source_target_pairs={{0,8},{2,10},{4,12},{6,14},{8,0},{10,2},{12,4},{14,6},{16,24},{18,... | collective-permute-start | bytes 688136 | tf_op jit(solution)/shard_map/ppermute | solution.py:21
  153.9 9.4 %collective-permute-start.21 = (bf16[12,3712]{1,0:T(8,128)(2,1)S(1)}, bf16[12,3712]{1,0:T(8,128)(2,1)S(1)}, u32[]{:S(2)}, u32[]{:S(2)}) collective-permute-start(bf16[12,3712]{1,0:T(8,128)(2,1)S(1)} %pad_maximum_fusion.9), channel_id=1, source_target_pairs={{0,16},{2,18},{4,20},{6,22},{8,24},{10,26},{12,28},{14,30},{16,0},... | collective-permute-start | bytes 267272 | tf_op jit(solution)/shard_map/ppermute | solution.py:21
  158.2 13.0 %collective-permute-start.18 = (bf16[16,3584]{1,0:T(8,128)(2,1)S(1)}, bf16[16,3584]{1,0:T(8,128)(2,1)S(1)}, u32[]{:S(2)}, u32[]{:S(2)}) collective-permute-start(bf16[16,3584]{1,0:T(8,128)(2,1)S(1)} %slice.321), channel_id=1, source_target_pairs={{0,16},{2,18},{4,20},{6,22},{8,24},{10,26},{12,28},{14,30},{16,0},... | collective-permute-start | bytes 344072 | tf_op jit(solution)/shard_map/ppermute | solution.py:21
  163.4 16.1 %copy-start.22 = (f32[3584]{0:T(1024)S(1)}, f32[3584]{0:T(1024)}, u32[]{:S(2)}) copy-start(f32[3584]{0:T(1024)} %param.22) | copy-start | bytes 43012
  163.4 6.0 %collective-permute-start.25 = (bf16[4,3584]{1,0:T(4,128)(2,1)S(1)}, bf16[4,3584]{1,0:T(4,128)(2,1)S(1)}, u32[]{:S(2)}, u32[]{:S(2)}) collective-permute-start(bf16[4,3584]{1,0:T(4,128)(2,1)S(1)} %slice.323), channel_id=1, source_target_pairs={{0,16},{2,18},{4,20},{6,22},{8,24},{10,26},{12,28},{14,30},{16,0},... | collective-permute-start | bytes 86024 | tf_op jit(solution)/shard_map/ppermute | solution.py:21
  163.6 9.3 %collective-permute-start.23 = (bf16[16,3712]{1,0:T(8,128)(2,1)S(1)}, bf16[16,3712]{1,0:T(8,128)(2,1)S(1)}, u32[]{:S(2)}, u32[]{:S(2)}) collective-permute-start(bf16[16,3712]{1,0:T(8,128)(2,1)S(1)} %slice.320), channel_id=1, source_target_pairs={{0,8},{2,10},{4,12},{6,14},{8,0},{10,2},{12,4},{14,6},{16,24},{18,... | collective-permute-start | bytes 356360 | tf_op jit(solution)/shard_map/ppermute | solution.py:21
  169.5 4.9 %collective-permute-start.26 = (bf16[8,3584]{1,0:T(8,128)(2,1)S(1)}, bf16[8,3584]{1,0:T(8,128)(2,1)S(1)}, u32[]{:S(2)}, u32[]{:S(2)}) collective-permute-start(bf16[8,3584]{1,0:T(8,128)(2,1)S(1)} %pad_maximum_fusion.12), channel_id=1, source_target_pairs={{0,8},{2,10},{4,12},{6,14},{8,0},{10,2},{12,4},{14,6},{16,24},{18,... | collective-permute-start | bytes 172040 | tf_op jit(solution)/shard_map/ppermute | solution.py:21
  172.9 5.2 %collective-permute-start.24 = (bf16[8,3712]{1,0:T(8,128)(2,1)S(1)}, bf16[8,3712]{1,0:T(8,128)(2,1)S(1)}, u32[]{:S(2)}, u32[]{:S(2)}) collective-permute-start(bf16[8,3712]{1,0:T(8,128)(2,1)S(1)} %slice.322), channel_id=1, source_target_pairs={{0,16},{2,18},{4,20},{6,22},{8,24},{10,26},{12,28},{14,30},{16,0},... | collective-permute-start | bytes 178184 | tf_op jit(solution)/shard_map/ppermute | solution.py:21
  174.5 4.9 %collective-permute-start.27 = (bf16[16,3584]{1,0:T(8,128)(2,1)S(1)}, bf16[16,3584]{1,0:T(8,128)(2,1)S(1)}, u32[]{:S(2)}, u32[]{:S(2)}) collective-permute-start(bf16[16,3584]{1,0:T(8,128)(2,1)S(1)} %pad_maximum_fusion.10), channel_id=1, source_target_pairs={{0,4},{2,6},{4,0},{6,2},{8,12},{10,14},{12,8},{14,10},{16,20},{18,... | collective-permute-start | bytes 344072 | tf_op jit(solution)/shard_map/ppermute | solution.py:21
  179.4 1.6 collective-permute-start.28

commit v4 on v3

--- a/solution.py
+++ b/solution.py
@@ -9,8 +9,9 @@
 
 SLOT = 8
 SPLIT = (8, 8)
-CUTS = ((0, 2, 4), (0, 2, 4))
+CUTS = ((0, 2, 8), (0, 5, 8))
 LANES = 128
+LASTS = (0, 1)
 FRACTION = 2
 VMEM_LIMIT = 36 * 1024 * 1024
 ROWS_LIMIT = 56 * 1024 * 1024
@@ -389,29 +390,41 @@
     moe_rows = moe_send.shape[0]
     mask = scatter_masks()[0]
     moe_keep, moe_next = halves(
-        add_swapped(returned(0, half), moe_send, mask, [recv[1, 0]]), [moe_rows // 2]
+        add_swapped(returned(0, half), moe_send, mask, []), [moe_rows // 2]
     )
 
     def rebuild(h, c, total, want, after):
-        start, last = cuts[h][c], c == len(cuts[h]) - 2
+        start, last = cuts[h][c], c == LASTS[h]
         return decode(
             own[h, c], recv[h, c], enc_bias, clamp_pick, want, dec_weight, start, total, last, after
         )
 
-    part = rebuild(0, 0, None, clamp_want, [sends[1, 1]])
-    keep, send = rebuild(0, 1, part, clamp_want, [recv[1, 0]])
-    part = rebuild(1, 0, None, None, [send, moe_next])
+    part = rebuild(0, 1, None, clamp_want, [sends[1, 1]])
+    keep, send = rebuild(0, 0, part, clamp_want, [recv[1, 0], moe_next])
+    masks = scatter_masks()
     groups = [keep.shape[0] - clamp_count // 2, clamp_count // 2]
-    first = add_swapped(keep, send, mask, [part, recv[1, 1]])
-    first_keep, first_next = halves(first, [g // 2 for g in groups])
-    last_keep, last_send = rebuild(1, 1, part, None, [first_next, moe_next])
+    first_keep, first_next = halves(
+        add_swapped(keep, send, masks[0], []), [g // 2 for g in groups]
+    )
+    part = rebuild(1, 0, None, None, [first_next, moe_next])
+    first_keep, first_next = halves(
+        add_swapped(first_keep, first_next, masks[1], [part]), [g // 4 for g in groups]
+    )
+    last_keep, last_send = rebuild(1, 1, part, None, [first_next])
+    moe_keep, moe_next = halves(
+        add_swapped(moe_keep, moe_next, masks[1], [last_send]), [moe_rows // 4]
+    )
     second_keep, second_next = halves(
-        add_swapped(last_keep, last_send, mask, []), [last_keep.shape[0] // 2]
-    )
-    moe_out = scatter_steps(moe_keep, moe_next, [moe_rows], 1, {1: [second_next]})
-    first = scatter_steps(first_keep, first_next, groups, 1, {1: [second_next]})
-    rows_dec = gather_blocks(first[SPLIT[0] :, :width].astype(jnp.bfloat16))
-    second = scatter_steps(second_keep, second_next, [last_keep.shape[0]], 1, {})
+        add_swapped(last_keep, last_send, masks[0], []), [last_keep.shape[0] // 2]
+    )
+    third_keep, third_next = halves(
+        add_swapped(second_keep, second_next, masks[1], []), [last_keep.shape[0] // 4]
+    )
+    first = scatter_steps(first_keep, first_next, groups, 2, {2: [last_send], 3: [second_next]})
+    rows_own = first[SPLIT[0] :, :width].astype(jnp.bfloat16)
+    rows_dec = gather_blocks(rows_own)
+    moe_out = scatter_steps(moe_keep, moe_next, [moe_rows], 2, {2: [second_next]})
+    second = scatter_steps(third_keep, third_next, [last_keep.shape[0]], 2, {})
     summed = jnp.concatenate([first[: SPLIT[0]], second], axis=0)
     chosen = summed[:, width : width + clamp_count]
     change = clamp_values.astype(jnp.float32)[None, :] - chosen

time: 183 us -> 153 us (0.84)
  waiting for transfers between devices: 53.2 us -> 28.6 us
  local copies, waits for them, and re-layouts: 9.41 us -> 5.77 us
  matrix products: 5.35 us -> 8.51 us
  other arithmetic: 14.6 us -> 11.7 us
    ppermute x29, waiting for transfers between devices: 53.2 us -> 28.6 us  [swap(): return lax.ppermute(x, axis, [(i, i ^ mask) for i in range(size)])]
    unnamed x59 -> x51, local copies, waits for them, and re-layouts: 6.29 us -> 3.19 us
    dot_general x1, matrix products: 1.19 us -> 4.28 us  [local(): jnp.dot(hidden, down_proj[0], preferred_element_type=jnp.float32)]
  transfers between devices with their start and end apart: 29 -> 29, of which waited for: 16 -> 14; matrix products, arithmetic and copies ran while one was open for 9% -> 12% of each run, Pallas kernels for 26% -> 36%
where the time goes in v4:
time: 153 us; the launch traced here: 152 us
  Pallas kernels  59.2 us (39%)
  starting transfers between devices  36.9 us (24%)
  waiting for transfers between devices  28.6 us (19%)
  other arithmetic  11.7 us (8%)
  matrix products  8.51 us (6%)
  local copies, waits for them, and re-layouts  5.77 us (4%)
  between operations  1.53 us (1%)
    ppermute x29, starting transfers between devices, swap(): return lax.ppermute(x, axis, [(i, i ^ mask) for i in range(size)])  36.9 us
    ppermute x29, waiting for transfers between devices, swap(): return lax.ppermute(x, axis, [(i, i ^ mask) for i in range(size)])  28.6 us
    pallas_call x4, Pallas kernels, encode(): pl.pallas_call(functools.partial(encode_kernel, first, count), out_shape=...  25.3 us
    pallas_call x4, Pallas kernels, decode(): pl.pallas_call(functools.partial(decode_kernel, start, first, last), out_...  25.2 us
    pallas_call x1, Pallas kernels, expert_halves(): pl.pallas_call(expert_kernel, out_shape=[jax.ShapeDtypeStruct((capacity,...  8.71 us
    dot_general x1, matrix products, local(): jnp.dot(hidden, down_proj[0], preferred_element_type=jnp.float32)  4.28 us
    unnamed x51, local copies, waits for them, and re-layouts  3.19 us
  transfers between devices with their start and end apart: 29, of which 14 were waited for; matrix products, arithmetic and copies ran while one was open for 12% of the time, Pallas kernels for 36%

profile of v4, /device:TPU:0, one launch (start us, length us, event | category | flops | bytes accessed | tf_op | source)
XLA Modules:
  0.0 152.3 jit_solution(11229206098616869562)
XLA Ops:
  0.6 0.8 copy.25
  1.4 0.7 convert_element_type.97
  2.2 0.7 convert_element_type.96
  3.0 0.9 constant_dynamic-update-slice_fusion.9
  3.9 4.1 %collective-permute-start = (bf16[8,3712]{1,0:T(8,128)(2,1)S(1)}, bf16[8,3712]{1,0:T(8,128)(2,1)S(1)}, u32[]{:S(2)}, u32[]{:S(2)}) collective-permute-start(bf16[8,3712]{1,0:T(8,128)(2,1)S(1)} %get-tuple-element.55), channel_id=1, source_target_pairs={{0,16},{2,18},{4,20},{6,22},{8,24},{10,26},{12,28},{14,30},{16,0},... | collective-permute-start | bytes 178184 | tf_op jit(solution)/shard_map/ppermute | solution.py:22
  8.1 0.7 broadcast_subtract_fusion
  8.7 1.3 fusion.6
  10.0 0.7 xor_multiply_fusion
  11.1 2.3 %collective-permute-start.1 = (bf16[16,3712]{1,0:T(8,128)(2,1)S(1)}, bf16[16,3712]{1,0:T(8,128)(2,1)S(1)}, u32[]{:S(2)}, u32[]{:S(2)}) collective-permute-start(bf16[16,3712]{1,0:T(8,128)(2,1)S(1)} %pad_maximum_fusion.7), channel_id=1, source_target_pairs={{0,8},{2,10},{4,12},{6,14},{8,0},{10,2},{12,4},{14,6},{16,24},{18,... | collective-permute-start | bytes 356360 | tf_op jit(solution)/shard_map/ppermute | solution.py:22
  13.4 1.3 collective-permute-start.5
  14.8 2.7 %collective-permute-done.1 = bf16[16,3712]{1,0:T(8,128)(2,1)S(1)} collective-permute-done((bf16[16,3712]{1,0:T(8,128)(2,1)S(1)}, bf16[16,3712]{1,0:T(8,128)(2,1)S(1)}, u32[]{:S(2)}, u32[]{:S(2)}) %collective-permute-start.1) | collective-permute-done | bytes 118816 | tf_op jit(solution)/shard_map/ppermute | solution.py:22
  17.5 1.7 %collective-permute-start.2 = (bf16[32,3712]{1,0:T(8,128)(2,1)S(1)}, bf16[32,3712]{1,0:T(8,128)(2,1)S(1)}, u32[]{:S(2)}, u32[]{:S(2)}) collective-permute-start(bf16[32,3712]{1,0:T(8,128)(2,1)S(1)} %pad_maximum_fusion.3), channel_id=1, source_target_pairs={{0,4},{2,6},{4,0},{6,2},{8,12},{10,14},{12,8},{14,10},{16,20},{18,... | collective-permute-start | bytes 712712 | tf_op jit(solution)/shard_map/ppermute | solution.py:22
  19.3 1.6 %collective-permute-start.6 = (bf16[32,3712]{1,0:T(8,128)(2,1)S(1)}, bf16[32,3712]{1,0:T(8,128)(2,1)S(1)}, u32[]{:S(2)}, u32[]{:S(2)}) collective-permute-start(bf16[32,3712]{1,0:T(8,128)(2,1)S(1)} %pad_maximum_fusion.4), channel_id=1, source_target_pairs={{0,4},{2,6},{4,0},{6,2},{8,12},{10,14},{12,8},{14,10},{16,20},{18,... | collective-permute-start | bytes 712712 | tf_op jit(solution)/shard_map/ppermute | solution.py:22
  20.9 5.3 %collective-permute-done.2 = bf16[32,3712]{1,0:T(8,128)(2,1)S(1)} collective-permute-done((bf16[32,3712]{1,0:T(8,128)(2,1)S(1)}, bf16[32,3712]{1,0:T(8,128)(2,1)S(1)}, u32[]{:S(2)}, u32[]{:S(2)}) %collective-permute-start.2) | collective-permute-done | bytes 237600 | tf_op jit(solution)/shard_map/ppermute | solution.py:22
  26.4 2.6 %collective-permute-done.6 = bf16[32,3712]{1,0:T(8,128)(2,1)S(1)} collective-permute-done((bf16[32,3712]{1,0:T(8,128)(2,1)S(1)}, bf16[32,3712]{1,0:T(8,128)(2,1)S(1)}, u32[]{:S(2)}, u32[]{:S(2)}) %collective-permute-start.6) | collective-permute-done | bytes 237600 | tf_op jit(solution)/shard_map/ppermute | solution.py:22
  29.2 4.2 %shard_map.140 = (f32[128,1024]{1,0:T(8,128)S(1)}, bf16[128,1024]{1,0:T(8,128)(2,1)S(1)}) custom-call(bf16[128,3712]{1,0:T(8,128)(2,1)S(1)} %constant_dynamic-update-slice_fusion.tokens_ref.rows0_ref, bf16[3584,4096]{1,0:T(8,128)(2,1)} %weight_ref.11), custom_call_target="tpu_custom_call" | custom-call | flops 234881024 | bytes 1835008 | tf_op jit(solution)/shard_map/pallas_call | solution.py:138
  33.4 1.4 collective-permute-start.9
  34.9 0.2 fusion.15
  35.2 0.3 reduce_or.9
  35.5 0.4 convert_reduce_fusion
  36.2 0.7 fusion.17
  36.9 8.7 %shard_map.141 = (f32[128,2048]{1,0:T(8,128)}, bf16[128,2048]{1,0:T(8,128)(2,1)}) custom-call(bf16[128,128]{1,0:T(8,128)(2,1)} %get-tuple-element.62.pick0_ref, bf16[128,128]{1,0:T(8,128)(2,1)} %get-tuple-element.63.pick1_ref, bf16[128,3712]{1,0:T(8,128)(2,1)} %copy-done.2, bf16[128,3712]{1,0:T(8,128)(2,1)} %copy-done, bf16[1,3584,1024]{2,1,0:T(8,128)(2,1)} %gate_ref.1, ...), custom_call_target="tpu_custom_call" | custom-call | flops 469762048 | bytes 3670016 | tf_op jit(solution)/shard_map/pallas_call | solution.py:190
  45.6 0.7 collective-permute-start.8
  46.3 1.1 copy-done.10
  47.4 9.0 %shard_map.142 = (f32[128,3072]{1,0:T(8,128)S(1)}, bf16[128,3072]{1,0:T(8,128)(2,1)}) custom-call(bf16[128,3712]{1,0:T(8,128)(2,1)S(1)} %copy-done.3, bf16[3584,4096]{1,0:T(8,128)(2,1)} %weight_ref.11, bf16[128,2048]{1,0:T(8,128)(2,1)S(1)} %copy-done.10), custom_call_target="tpu_custom_call" | custom-call | flops 704643072 | bytes 5505024 | tf_op jit(solution)/shard_map/pallas_call | solution.py:138
  56.4 1.2 copy-done.4
  57.6 1.4 collective-permute-start.12
  59.1 7.1 %shard_map.143 = (f32[128,2560]{1,0:T(8,128)S(1)}, bf16[128,2560]{1,0:T(8,128)(2,1)S(1)}) custom-call(bf16[128,3712]{1,0:T(8,128)(2,1)S(1)} %copy-done.1, bf16[3584,4096]{1,0:T(8,128)(2,1)} %weight_ref.11, bf16[128,3072]{1,0:T(8,128)(2,1)} %get-tuple-element.25.refs_0_, bf16[128,1024]{1,0:T(8,128)(2,1)S(1)} %collective-permute-done.9.refs_1_.recv_ref), custom_call_target="tpu_custom_call" | custom-call | flops 587202560 | bytes 4587520 | tf_op jit(solution)/shard_map/pallas_call | solution.py:138
  66.3 1.5 %convert_add_fusion.1 = f32[128,2048]{1,0:T(8,128)S(1)} fusion(f32[128,2048]{1,0:T(8,128)S(1)} %copy-done.18, bf16[128,2048]{1,0:T(8,128)(2,1)} %collective-permute-done.8), kind=kLoop, calls=%fused_computation.11 | loop fusion | flops 524288 | bytes 2621440 | tf_op jit(solution)/shard_map/add | solution.py:373
  67.8 4.3 %fusion.3 = bf16[128,3584]{1,0:T(8,128)(2,1)S(1)} fusion(bf16[1,1024,3584]{2,1,0:T(8,128)(2,1)} %param.18, f32[128,2048]{1,0:T(8,128)S(1)} %convert_add_fusion.1), kind=kOutput, calls=%fused_computation.5 | convolution fusion | flops 940769280 | bytes 9306112 | tf_op jit(solution)/shard_map/dot_general | solution.py:376
  72.2 1.4 fusion.2
  73.8 0.7 slice.249.want_ref
  74.9 0.7 collective-permute-start.14
  75.6 1.6 %convolution_multiply_fusion.1 = f32[128,3584]{1,0:T(8,128)S(1)} fusion(bf16[128,3584]{1,0:T(8,128)(2,1)} %copy-done.17, f32[128]{0:T(128)S(1)} %mul.45, s32[128]{0:T(128)S(1)} %eq.107), kind=kOutput, calls=%fused_computation.3 | convolution fusion | flops 117915648 | bytes 2753536 | tf_op jit(solution)/shard_map/dot_general | solution.py:382
  77.4 5.0 %shard_map.144 = (f32[128,1536]{1,0:T(8,128)S(1)}, bf16[128,1536]{1,0:T(8,128)(2,1)S(1)}) custom-call(bf16[128,3712]{1,0:T(8,128)(2,1)S(1)} %copy-done.1, bf16[3584,4096]{1,0:T(8,128)(2,1)} %weight_ref.11, bf16[128,2560]{1,0:T(8,128)(2,1)S(1)} %copy-done.9, bf16[128,3072]{1,0:T(8,128)(2,1)S(1)} %collective-permute-done.12.refs_1_.recv_ref), custom_call_target="tpu_custom_call" | custom-call | flops 352321536 | bytes 2752512 | tf_op jit(solution)/shard_map/pallas_call | solution.py:138
  82.4 8.7 %shard_map.145.refs_0_ = f32[192,3712]{1,0:T(8,128)S(1)} custom-call(f32[128,3072]{1,0:T(8,128)S(1)} %copy-done.5, bf16[128,3072]{1,0:T(8,128)(2,1)S(1)} %collective-permute-done.12.refs_1_.recv_ref, f32[1,3072]{1,0:T(1,128)S(1)} %bitcast.15, bf16[3072,128]{1,0:T(8,128)(2,1)S(1)} %pad_slice_fusion.pick_ref, bf16[64,3072]{1,0:T(8,128)(2,1)S(1)} %slice.250.want_ref, ...), custom_call_target="tpu_custom_call" | custom-call | flops 704643072 | bytes 5505024 | tf_op jit(solution)/shard_map/pallas_call | solution.py:272
  91.2 1.4 convert_add_fusion
  92.8 4.3 %shard_map.146 = (f32[96,3712]{1,0:T(8,128)S(1)}, f32[96,3712]{1,0:T(8,128)S(1)}) custom-call(f32[128,1024]{1,0:T(8,128)S(1)} %copy-done.13, bf16[128,1024]{1,0:T(8,128)(2,1)S(1)} %collective-permute-done.9.refs_1_.recv_ref, f32[1,1024]{1,0:T(1,128)S(1)} %bitcast.16, bf16[1024,128]{1,0:T(8,128)(2,1)S(1)} %pad_slice_fusion.1.pick_ref, ...), custom_call_target="tpu_custom_call" | custom-call | flops 234881024 | bytes 1835008 | tf_op jit(solution)/shard_map/pallas_call | solution.py:272
  97.3 3.0 %collective-permute-done.15 = f32[96,3712]{1,0:T(8,128)S(1)} collective-permute-done((f32[96,3712]{1,0:T(8,128)S(1)}, f32[96,3712]{1,0:T(8,128)S(1)}, u32[]{:S(2)}, u32[]{:S(2)}) %collective-permute-start.15) | collective-permute-done | bytes 1425440 | tf_op jit(solution)/shard_map/ppermute | solution.py:22
  100.6 1.6 %collective-permute-start.16 = (bf16[48,3712]{1,0:T(8,128)(2,1)S(1)}, bf16[48,3712]{1,0:T(8,128)(2,1)S(1)}, u32[]{:S(2)}, u32[]{:S(2)}) collective-permute-start(bf16[48,3712]{1,0:T(8,128)(2,1)S(1)} %pad_maximum_fusion.2.refs_0_), channel_id=1, source_target_pairs={{0,4},{2,6},{4,0},{6,2},{8,12},{10,14},{12,8},{14,10},{16,20},{18,... | collective-permute-start | bytes 1069064 | tf_op jit(solution)/shard_map/ppermute | solution.py:22
  102.3 1.3 collective-permute-start.13
  103.6 0.5 collective-permute-start.11
  104.2 7.3 %shard_map.147.refs_0_ = f32[128,3712]{1,0:T(8,128)S(1)} custom-call(f32[128,2560]{1,0:T(8,128)S(1)} %copy-done.7, bf16[128,2560]{1,0:T(8,128)(2,1)S(1)} %collective-permute-done.14.refs_1_.recv_ref, f32[1,2560]{1,0:T(1,128)S(1)} %reshape.69.bias_ref, bf16[2560,128]{1,0:T(8,128)(2,1)S(1)} %pad_slice_fusion.2.pick_ref, bf16[8,8]{1,0:T(8,128)(2,1)S(1)} %slice.248.want_ref, ...), custom_call_target="tpu_custom_call" | custom-call | flops 587202560 | bytes 4587520 | tf_op jit(solution)/shard_map/pallas_call | solution.py:272
  111.5 0.4 collective-permute-done.16
  112.0 1.7 %collective-permute-start.20 = (bf16[24,3712]{1,0:T(8,128)(2,1)S(1)}, bf16[24,3712]{1,0:T(8,128)(2,1)S(1)}, u32[]{:S(2)}, u32[]{:S(2)}) collective-permute-start(bf16[24,3712]{1,0:T(8,128)(2,1)S(1)} %pad_maximum_fusion.6.refs_1_), channel_id=1, source_target_pairs={{0,8},{2,10},{4,12},{6,14},{8,0},{10,2},{12,4},{14,6},{16,24},{18,... | collective-permute-start | bytes 534536 | tf_op jit(solution)/shard_map/ppermute | solution.py:22
  113.8 5.0 %shard_map.148 = (f32[64,3712]{1,0:T(8,128)S(1)}, f32[64,3712]{1,0:T(8,128)S(1)}) custom-call(f32[128,1536]{1,0:T(8,128)S(1)} %get-tuple-element.28.own_ref, bf16[128,1536]{1,0:T(8,128)(2,1)S(1)} %collective-permute-done.13.recv_ref, f32[1,1536]{1,0:T(1,128)S(1)} %reshape.68.bias_ref, bf16[1536,128]{1,0:T(8,128)(2,1)S(1)} %pad_slice_fusion.3.pick_ref, ...), custom_call_target="tpu_custom_call" | custom-call | flops 352321536 | bytes 2752512 | tf_op jit(solution)/shard_map/pallas_call | solution.py:272
  118.8 2.0 %collective-permute-done.11 = bf16[64,3584]{1,0:T(8,128)(2,1)S(1)} collective-permute-done((bf16[64,3584]{1,0:T(8,128)(2,1)S(1)}, bf16[64,3584]{1,0:T(8,128)(2,1)S(1)}, u32[]{:S(2)}, u32[]{:S(2)}) %collective-permute-start.11) | collective-permute-done | bytes 458784 | tf_op jit(solution)/shard_map/ppermute | solution.py:22
  121.0 3.6 %collective-permute-start.21 = (bf16[12,3712]{1,0:T(8,128)(2,1)S(1)}, bf16[12,3712]{1,0:T(8,128)(2,1)S(1)}, u32[]{:S(2)}, u32[]{:S(2)}) collective-permute-start(bf16[12,3712]{1,0:T(8,128)(2,1)S(1)} %pad_maximum_fusion.9), channel_id=1, source_target_pairs={{0,16},{2,18},{4,20},{6,22},{8,24},{10,26},{12,28},{14,30},{16,0},... | collective-permute-start | bytes 267272 | tf_op jit(solution)/shard_map/ppermute | solution.py:22
  124.7 1.5 %collective-permute-start.17 = (bf16[32,3584]{1,0:T(8,128)(2,1)S(1)}, bf16[32,3584]{1,0:T(8,128)(2,1)S(1)}, u32[]{:S(2)}, u32[]{:S(2)}) collective-permute-start(bf16[32,3584]{1,0:T(8,128)(2,1)S(1)} %slice.333), channel_id=1, source_target_pairs={{0,8},{2,10},{4,12},{6,14},{8,0},{10,2},{12,4},{14,6},{16,24},{18,... | collective-permute-start | bytes 688136 | tf_op jit(solution)/shard_map/ppermute | solution.py:22
  126.4 1.6 %collective-permute-start.22 = (bf16[32,3712]{1,0:T(8,128)(2,1)S(1)}, bf16[32,3712]{1,0:T(8,128)(2,1)S(1)}, u32[]{:S(2)}, u32[]{:S(2)}) collective-permute-start(bf16[32,3712]{1,0:T(8,128)(2,1)S(1)} %slice.332), channel_id=1, source_target_pairs={{0,4},{2,6},{4,0},{6,2},{8,12},{10,14},{12,8},{14,10},{16,20},{18,... | collective-permute-start | bytes 712712 | tf_op jit(solution)/shard_map/ppermute | solution.py:22
  128.0 1.8 %collective-permute-done.21 = bf16[12,3712]{1,0:T(8,128)(2,1)S(1)} collective-permute-done((bf16[12,3712]{1,0:T(8,128)(2,1)S(1)}, bf16[12,3712]{1,0:T(8,128)(2,1)S(1)}, u32[]{:S(2)}, u32[]{:S(2)}) %collective-permute-start.21) | collective-permute-done | bytes 89120 | tf_op jit(solution)/shard_map/ppermute | solution.py:22
  129.9 2.9 %collective-permute-done.17 = bf16[32,3584]{1,0:T(8,128)(2,1)S(1)} collective-permute-done((bf16[32,3584]{1,0:T(8,128)(2,1)S(1)}, bf16[32,3584]{1,0:T(8,128)(2,1)S(1)}, u32[]{:S(2)}, u32[]{:S(2)}) %collective-permute-start.17) | collective-permute-done | bytes 229408 | tf_op jit(solution)/shard_map/ppermute | solution.py:22
  132.8 0.8 collective-permute-start.25
  133.8 2.1 %collective-permute-start.19 = (bf16[16,3584]{1,0:T(8,128)(2,1)S(1)}, bf16[16,3584]{1,0:T(8,128)(2,1)S(1)}, u32[]{:S(2)}, u32[]{:S(2)}) collective-permute-start(bf16[16,3584]{1,0:T(8,128)(2,1)S(1)} %slice.335), channel_id=1, source_target_pairs={{0,16},{2,18},{4,20},{6,22},{8,24},{10,26},{12,28},{14,30},{16,0},... | collective-permute-start | bytes 344072 | tf_op jit(solution)/shard_map/ppermute | solution.py:22
  135.9 3.1 %collective-permute-done.25 = bf16[4,3584]{1,0:T(4,128)(2,1)S(1)} collective-permute-done((bf16[4,3584]{1,0:T(4,128)(2,1)S(1)}, bf16[4,3584]{1,0:T(4,128)(2,1)S(1)}, u32[]{:S(2)}, u32[]{:S(2)}) %collective-permute-start.25) | collective-permute-done | bytes 28704 | tf_op jit(solution)/shard_map/ppermute | solution.py:22
  139.0 0.2 collective-permute-start.26
  139.3 2.0 %collective-permute-start.23 = (bf16[16,3712]{1,0:T(8,128)(2,1)S(1)}, bf16[16,3712]{1,0:T(8,128)(2,1)S(1)}, u32[]{:S(2)}, u32[]{:S(2)}) collective-permute-start(bf16[16,3712]{1,0:T(8,128)(2,1)S(1)} %slice.334), channel_id=1, source_target_pairs={{0,8},{2,10},{4,12},{6,14},{8,0},{10,2},{12,4},{14,6},{16,24},{18,... | collective-permute-start | bytes 356360 | tf_op jit(solution)/shard_map/ppermute | solution.py:22
  141.2 2.0 %collective-permute-done.26 = bf16[8,3584]{1,0:T(8,128)(2,1)S(1)} collective-permute-done((bf16[8,3584]{1,0:T(8,128)(2,1)S(1)}, bf16[8,3584]{1,0:T(8,128)(2,1)S(1)}, u32[]{:S(2)}, u32[]{:S(2)}) %collective-permute-start.26) | collective-permute-done | bytes 57376 | tf_op jit(solution)/shard_map/ppermute | solution.py:22
  143.3 1.6 %collective-permute-start.27 = (bf16[16,3584]{1,0:T(8,128)(2,1)S(1)}, bf16[16,3584]{1,0:T(8,128)(2,1)S(1)}, u32[]{:S(2)}, u32[]{:S(2)}) collective-permute-start(bf16[16,3584]{1,0:T(8,128)(2,1)S(1)} %pad_maximum_fusion.10), channel_id=1, source_target_pairs={{0,4},{2,6},{4,0},{6,2},{8,12},{10,14},{12,8},{14,10},{16,20},{18,... | collective-permute-start | bytes 344072 | tf_op jit(solution)/shard_map/ppermute | solution.py:22
  145.0 2.6 %collective-permute-start.24 = (bf16[8,3712]{1,0:T(8,128)(2,1)S(1)}, bf16[8,3712]{1,0:T(8,128)(2,1)S(1)}, u32[]{:S(2)}, u32[]{:S(2)}) collective-permute-start(bf16[8,3712]{1,0:T(8,128)(2,1)S(1)} %slice.336), channel_id=1, source_target_pairs={{0,16},{2,18},{4,20},{6,22},{8,24},{10,26},{12,28},{14,30},{16,0},... | collective-permute-start | bytes 178184 | tf_op jit(solution)/shard_map/ppermute | solution.py:22
  147.6 0.6 collective-permute-done.27
  148.3 1.8 %collective-permute-done.24 = bf16[8,3712]{1,0:T(8,128)(2,1)S(1)} collective-permute-done((bf16[8,3712]{1,0:T(8,128)(2,1)S(1)}, bf16[8,3712]{1,0:T(8,128)(2,1)S(1)}, u32[]{:S(2)}, u32[]{:S(2)}) %collective-permute-start.24) | collective-permute-done | bytes 59424 | tf_op jit(solution)/shard_map/ppermute | solution.py:22
  150.2 0.7 fusion.13
  151.3 1.0 convolution_add_fusion
  (155 shorter events, 4.8 us)
Async XLA Ops:
  3.9 7.2 %collective-permute-start = (bf16[8,3712]{1,0:T(8,128)(2,1)S(1)}, bf16[8,3712]{1,0:T(8,128)(2,1)S(1)}, u32[]{:S(2)}, u32[]{:S(2)}) collective-permute-start(bf16[8,3712]{1,0:T(8,128)(2,1)S(1)} %get-tuple-element.55), channel_id=1, source_target_pairs={{0,16},{2,18},{4,20},{6,22},{8,24},{10,26},{12,28},{14,30},{16,0},... | collective-permute-start | bytes 178184 | tf_op jit(solution)/shard_map/ppermute | solution.py:22
  8.0 5.4 %collective-permute-start.4 = (bf16[8,3712]{1,0:T(8,128)(2,1)S(1)}, bf16[8,3712]{1,0:T(8,128)(2,1)S(1)}, u32[]{:S(2)}, u32[]{:S(2)}) collective-permute-start(bf16[8,3712]{1,0:T(8,128)(2,1)S(1)} %get-tuple-element.51), channel_id=1, source_target_pairs={{0,16},{2,18},{4,20},{6,22},{8,24},{10,26},{12,28},{14,30},{16,0},... | collective-permute-start | bytes 178184 | tf_op jit(solution)/shard_map/ppermute | solution.py:22
  11.1 6.4 %collective-permute-start.1 = (bf16[16,3712]{1,0:T(8,128)(2,1)S(1)}, bf16[16,3712]{1,0:T(8,128)(2,1)S(1)}, u32[]{:S(2)}, u32[]{:S(2)}) collective-permute-start(bf16[16,3712]{1,0:T(8,128)(2,1)S(1)} %pad_maximum_fusion.7), channel_id=1, source_target_pairs={{0,8},{2,10},{4,12},{6,14},{8,0},{10,2},{12,4},{14,6},{16,24},{18,... | collective-permute-start | bytes 356360 | tf_op jit(solution)/shard_map/ppermute | solution.py:22
  13.4 5.8 %collective-permute-start.5 = (bf16[16,3712]{1,0:T(8,128)(2,1)S(1)}, bf16[16,3712]{1,0:T(8,128)(2,1)S(1)}, u32[]{:S(2)}, u32[]{:S(2)}) collective-permute-start(bf16[16,3712]{1,0:T(8,128)(2,1)S(1)} %pad_maximum_fusion.8), channel_id=1, source_target_pairs={{0,8},{2,10},{4,12},{6,14},{8,0},{10,2},{12,4},{14,6},{16,24},{18,... | collective-permute-start | bytes 356360 | tf_op jit(solution)/shard_map/ppermute | solution.py:22
  17.5 8.8 %collective-permute-start.2 = (bf16[32,3712]{1,0:T(8,128)(2,1)S(1)}, bf16[32,3712]{1,0:T(8,128)(2,1)S(1)}, u32[]{:S(2)}, u32[]{:S(2)}) collective-permute-start(bf16[32,3712]{1,0:T(8,128)(2,1)S(1)} %pad_maximum_fusion.3), channel_id=1, source_target_pairs={{0,4},{2,6},{4,0},{6,2},{8,12},{10,14},{12,8},{14,10},{16,20},{18,... | collective-permute-start | bytes 712712 | tf_op jit(solution)/shard_map/ppermute | solution.py:22
  19.3 9.7 %collective-permute-start.6 = (bf16[32,3712]{1,0:T(8,128)(2,1)S(1)}, bf16[32,3712]{1,0:T(8,128)(2,1)S(1)}, u32[]{:S(2)}, u32[]{:S(2)}) collective-permute-start(bf16[32,3712]{1,0:T(8,128)(2,1)S(1)} %pad_maximum_fusion.4), channel_id=1, source_target_pairs={{0,4},{2,6},{4,0},{6,2},{8,12},{10,14},{12,8},{14,10},{16,20},{18,... | collective-permute-start | bytes 712712 | tf_op jit(solution)/shard_map/ppermute | solution.py:22
  26.3 2.8 %collective-permute-start.3 = (bf16[64,3712]{1,0:T(8,128)(2,1)S(1)}, bf16[64,3712]{1,0:T(8,128)(2,1)S(1)}, u32[]{:S(2)}, u32[]{:S(2)}) collective-permute-start(bf16[64,3712]{1,0:T(8,128)(2,1)S(1)} %pad_maximum_fusion), channel_id=1, source_target_pairs={{0,2},{2,0},{4,6},{6,4},{8,10},{10,8},{12,14},{14,12},{16,18},{18,... | collective-permute-start | bytes 1425416 | tf_op jit(solution)/shard_map/ppermute | solution.py:22
  29.0 5.8 %collective-permute-start.7 = (bf16[64,3712]{1,0:T(8,128)(2,1)S(1)}, bf16[64,3712]{1,0:T(8,128)(2,1)S(1)}, u32[]{:S(2)}, u32[]{:S(2)}) collective-permute-start(bf16[64,3712]{1,0:T(8,128)(2,1)S(1)} %pad_maximum_fusion.1), channel_id=1, source_target_pairs={{0,2},{2,0},{4,6},{6,4},{8,10},{10,8},{12,14},{14,12},{16,18},{18,... | collective-permute-start | bytes 1425416 | tf_op jit(solution)/shard_map/ppermute | solution.py:22
  29.2 5.6 %copy-start.2 = (bf16[128,3712]{1,0:T(8,128)(2,1)}, bf16[128,3712]{1,0:T(8,128)(2,1)S(1)}, u32[]{:S(2)}) copy-start(bf16[128,3712]{1,0:T(8,128)(2,1)S(1)} %constant_dynamic-update-slice_fusion.tokens_ref.rows0_ref) | copy-start | bytes 2850820
  33.4 1.5 copy-start.12
  33.4 3.5 %copy-start.14 = (bf16[128,1024]{1,0:T(8,128)(2,1)}, bf16[128,1024]{1,0:T(8,128)(2,1)S(1)}, u32[]{:S(2)}) copy-start(bf16[128,1024]{1,0:T(8,128)(2,1)S(1)} %get-tuple-element.22.refs_0_) | copy-start | bytes 786436
  33.4 25.7 %collective-permute-start.9 = (bf16[128,1024]{1,0:T(8,128)(2,1)S(1)}, bf16[128,1024]{1,0:T(8,128)(2,1)S(1)}, u32[]{:S(2)}, u32[]{:S(2)}) collective-permute-start(bf16[128,1024]{1,0:T(8,128)(2,1)S(1)} %get-tuple-element.22.refs_0_), channel_id=1, source_target_pairs={{0,1},{1,0},{2,3},{3,2},{4,5},{5,4},{6,7},{7,6},{8,9},{9,8},{10,11... | collective-permute-start | bytes 786440 | tf_op jit(solution)/shard_map/ppermute | solution.py:22
  34.9 2.0 %copy-start = (bf16[128,3712]{1,0:T(8,128)(2,1)}, bf16[128,3712]{1,0:T(8,128)(2,1)S(1)}, u32[]{:S(2)}) copy-start(bf16[128,3712]{1,0:T(8,128)(2,1)S(1)} %constant_dynamic-update-slice_fusion.5.rows1_ref.tokens_ref) | copy-start | bytes 2850820
  36.9 9.5 %copy-start.3 = (bf16[128,3712]{1,0:T(8,128)(2,1)S(1)}, bf16[128,3712]{1,0:T(8,128)(2,1)}, u32[]{:S(2)}) copy-start(bf16[128,3712]{1,0:T(8,128)(2,1)} %copy-done.2) | copy-start | bytes 2850820
  45.6 13.5 %copy-start.1 = (bf16[128,3712]{1,0:T(8,128)(2,1)S(1)}, bf16[128,3712]{1,0:T(8,128)(2,1)}, u32[]{:S(2)}) copy-start(bf16[128,3712]{1,0:T(8,128)(2,1)} %copy-done) | copy-start | bytes 2850820
  45.6 20.7 %collective-permute-start.8 = (bf16[128,2048]{1,0:T(8,128)(2,1)}, bf16[128,2048]{1,0:T(8,128)(2,1)}, u32[]{:S(2)}, u32[]{:S(2)}) collective-permute-start(bf16[128,2048]{1,0:T(8,128)(2,1)} %get-tuple-element.24.refs_0_), channel_id=1, source_target_pairs={{0,1},{1,0},{2,3},{3,2},{4,5},{5,4},{6,7},{7,6},{8,9},{9,8},{10,11... | collective-permute-start | bytes 1572872 | tf_op jit(solution)/shard_map/ppermute | solution.py:22
  46.3 1.1 copy-start.10
  56.4 1.2 copy-start.4
  57.6 19.8 %collective-permute-start.12 = (bf16[128,3072]{1,0:T(8,128)(2,1)}, bf16[128,3072]{1,0:T(8,128)(2,1)S(1)}, u32[]{:S(2)}, u32[]{:S(2)}) collective-permute-start(bf16[128,3072]{1,0:T(8,128)(2,1)} %get-tuple-element.25.refs_0_), channel_id=1, source_target_pairs={{0,1},{1,0},{2,3},{3,2},{4,5},{5,4},{6,7},{7,6},{8,9},{9,8},{10,11... | collective-permute-start | bytes 2359304 | tf_op jit(solution)/shard_map/ppermute | solution.py:22
  59.1 7.2 %copy-start.18 = (f32[128,2048]{1,0:T(8,128)S(1)}, f32[128,2048]{1,0:T(8,128)}, u32[]{:S(2)}) copy-start(f32[128,2048]{1,0:T(8,128)} %get-tuple-element.23) | copy-start | bytes 3145732
  66.3 5.9 %copy-start.6 = (f32[128,2560]{1,0:T(8,128)}, f32[128,2560]{1,0:T(8,128)S(1)}, u32[]{:S(2)}) copy-start(f32[128,2560]{1,0:T(8,128)S(1)} %get-tuple-element.30.own_ref) | copy-start | bytes 3932164
  66.3 5.9 %copy-start.8 = (bf16[128,2560]{1,0:T(8,128)(2,1)}, bf16[128,2560]{1,0:T(8,128)(2,1)S(1)}, u32[]{:S(2)}) copy-start(bf16[128,2560]{1,0:T(8,128)(2,1)S(1)} %get-tuple-element.26.refs_0_) | copy-start | bytes 1966084
  72.1 2.6 %copy-start.17 = (bf16[128,3584]{1,0:T(8,128)(2,1)}, bf16[128,3584]{1,0:T(8,128)(2,1)S(1)}, u32[]{:S(2)}) copy-start(bf16[128,3584]{1,0:T(8,128)(2,1)S(1)} %fusion.3) | copy-start | bytes 2752516
  72.1 1.6 %copy-start.19 = (f32[4096]{0:T(1024)S(1)}, f32[4096]{0:T(1024)}, u32[]{:S(2)}) copy-start(f32[4096]{0:T(1024)} %param.20) | copy-start | bytes 49156
  72.2 2.3 %copy-start.15 = (bf16[4096,64]{1,0:T(8,128)(2,1)S(1)}, bf16[4096,64]{1,0:T(8,128)(2,1)}, u32[]{:S(2)}) copy-start(bf16[4096,64]{1,0:T(8,128)(2,1)} %fusion.6) | copy-start | bytes 1572868
  73.6 17.6 %collective-permute-start.10 = (bf16[128,3584]{1,0:T(8,128)(2,1)}, bf16[128,3584]{1,0:T(8,128)(2,1)}, u32[]{:S(2)}, u32[]{:S(2)}) collective-permute-start(bf16[128,3584]{1,0:T(8,128)(2,1)} %fusion.2), channel_id=1, source_target_pairs={{0,2},{2,0},{4,6},{6,4},{8,10},{10,8},{12,14},{14,12},{16,18},{18,... | collective-permute-start | bytes 2752520 | tf_op jit(solution)/shard_map/ppermute | solution.py:22
  74.9 2.5 %copy-start.9 = (bf16[128,2560]{1,0:T(8,128)(2,1)S(1)}, bf16[128,2560]{1,0:T(8,128)(2,1)}, u32[]{:S(2)}) copy-start(bf16[128,2560]{1,0:T(8,128)(2,1)} %copy-done.8) | copy-start | bytes 1966084
  74.9 17.8 %collective-permute-start.14 = (bf16[128,2560]{1,0:T(8,128)(2,1)}, bf16[128,2560]{1,0:T(8,128)(2,1)S(1)}, u32[]{:S(2)}, u32[]{:S(2)}) collective-permute-start(bf16[128,2560]{1,0:T(8,128)(2,1)} %copy-done.8), channel_id=1, source_target_pairs={{0,1},{1,0},{2,3},{3,2},{4,5},{5,4},{6,7},{7,6},{8,9},{9,8},{10,11... | collective-permute-start | bytes 1966088 | tf_op jit(solution)/shard_map/ppermute | solution.py:22
  77.3 5.2 %copy-start.5 = (f32[128,3072]{1,0:T(8,128)S(1)}, f32[128,3072]{1,0:T(8,128)}, u32[]{:S(2)}) copy-start(f32[128,3072]{1,0:T(8,128)} %copy-done.4) | copy-start | bytes 4718596
  91.2 1.6 %copy-start.11 = (bf16[64,1024]{1,0:T(8,128)(2,1)S(1)}, bf16[64,1024]{1,0:T(8,128)(2,1)}, u32[]{:S(2)}) copy-start(bf16[64,1024]{1,0:T(8,128)(2,1)} %slice.249.want_ref) | copy-start | bytes 393220
  91.2 1.6 %copy-start.13 = (f32[128,1024]{1,0:T(8,128)S(1)}, f32[128,1024]{1,0:T(8,128)}, u32[]{:S(2)}) copy-start(f32[128,1024]{1,0:T(8,128)} %copy-done.12) | copy-start | bytes 1572868
  92.7 4.5 %copy-start.16 = (bf16[4096,64]{1,0:T(8,128)(2,1)S(1)}, bf16[4096,64]{1,0:T(8,128)(2,1)}, u32[]{:S(2)}) copy-start(bf16[4096,64]{1,0:T(8,128)(2,1)} %fusion.6) | copy-start | bytes 1572868
  92.7 4.5 %slice-start = ((f32[4096]{0:T(1024)}), f32[2560]{0:T(1024)S(1)}, s32[]{:S(2)}) async-start(f32[4096]{0:T(1024)} %param.20), calls=%async_computation | async-start | bytes 24576 | tf_op jit(solution)/shard_map/slice | solution.py:263
  92.7 4.5 %copy-start.21 = (bf16[64]{0:T(256)(128)(2,1)S(1)}, bf16[64]{0:T(256)(128)(2,1)}, u32[]{:S(2)}) copy-start(bf16[64]{0:T(256)(128)(2,1)} %param.24) | copy-start | bytes 388
  97.1 3.3 %collective-permute-start.15 = (f32[96,3712]{1,0:T(8,128)S(1)}, f32[96,3712]{1,0:T(8,128)S(1)}, u32[]{:S(2)}, u32[]{:S(2)}) collective-permute-start(f32[96,3712]{1,0:T(8,128)S(1)} %get-tuple-element.34), channel_id=1, source_target_pairs={{0,2},{2,0},{4,6},{6,4},{8,10},{10,8},{12,14},{14,12},{16,18},{18,... | collective-permute-start | bytes 4276232 | tf_op jit(solution)/shard_map/ppermute | solution.py:22
  100.5 3.6 %copy-start.7 = (f32[128,2560]{1,0:T(8,128)S(1)}, f32[128,2560]{1,0:T(8,128)}, u32[]{:S(2)}) copy-start(f32[128,2560]{1,0:T(8,128)} %copy-done.6) | copy-start | bytes 3932164
  100.6 11.2 %collective-permute-start.16 = (bf16[48,3712]{1,0:T(8,128)(2,1)S(1)}, bf16[48,3712]{1,0:T(8,128)(2,1)S(1)}, u32[]{:S(2)}, u32[]{:S(2)}) collective-permute-start(bf16[48,3712]{1,0:T(8,128)(2,1)S(1)} %pad_maximum_fusion.2.refs_0_), channel_id=1, source_target_pairs={{0,4},{2,6},{4,0},{6,2},{8,12},{10,14},{12,8},{14,10},{16,20},{18,... | collective-permute-start | bytes 1069064 | tf_op jit(solution)/shard_map/ppermute | solution.py:22
  102.3 11.4 %collective-permute-start.13 = (bf16[128,1536]{1,0:T(8,128)(2,1)S(1)}, bf16[128,1536]{1,0:T(8,128)(2,1)S(1)}, u32[]{:S(2)}, u32[]{:S(2)}) collective-permute-start(bf16[128,1536]{1,0:T(8,128)(2,1)S(1)} %get-tuple-element.29.refs_0_), channel_id=1, source_target_pairs={{0,1},{1,0},{2,3},{3,2},{4,5},{5,4},{6,7},{7,6},{8,9},{9,8},{10,11... | collective-permute-start | bytes 1179656 | tf_op jit(solution)/shard_map/ppermute | solution.py:22
  103.6 17.3 %collective-permute-start.11 = (bf16[64,3584]{1,0:T(8,128)(2,1)S(1)}, bf16[64,3584]{1,0:T(8,128)(2,1)S(1)}, u32[]{:S(2)}, u32[]{:S(2)}) collective-permute-start(bf16[64,3584]{1,0:T(8,128)(2,1)S(1)} %slice.331.refs_2_.refs_1_), channel_id=1, source_target_pairs={{0,4},{2,6},{4,0},{6,2},{8,12},{10,14},{12,8},{14,10},{16,20},{18,... | collective-permute-start | bytes 1376264 | tf_op jit(solution)/shard_map/ppermute | solution.py:22
  112.0 8.9 %collective-permute-start.20 = (bf16[24,3712]{1,0:T(8,128)(2,1)S(1)}, bf16[24,3712]{1,0:T(8,128)(2,1)S(1)}, u32[]{:S(2)}, u32[]{:S(2)}) collective-permute-start(bf16[24,3712]{1,0:T(8,128)(2,1)S(1)} %pad_maximum_fusion.6.refs_1_), channel_id=1, source_target_pairs={{0,8},{2,10},{4,12},{6,14},{8,0},{10,2},{12,4},{14,6},{16,24},{18,... | collective-permute-start | bytes 534536 | tf_op jit(solution)/shard_map/ppermute | solution.py:22
  118.7 7.5 %collective-permute-start.18 = (f32[64,3712]{1,0:T(8,128)S(1)}, f32[64,3712]{1,0:T(8,128)S(1)}, u32[]{:S(2)}, u32[]{:S(2)}) collective-permute-start(f32[64,3712]{1,0:T(8,128)S(1)} %get-tuple-element.36), channel_id=1, source_target_pairs={{0,2},{2,0},{4,6},{6,4},{8,10},{10,8},{12,14},{14,12},{16,18},{18,... | collective-permute-start | bytes 2850824 | tf_op jit(solution)/shard_map/ppermute | solution.py:22
  121.0 8.9 %collective-permute-start.21 = (bf16[12,3712]{1,0:T(8,128)(2,1)S(1)}, bf16[12,3712]{1,0:T(8,128)(2,1)S(1)}, u32[]{:S(2)}, u32[]{:S(2)}) collective-permute-start(bf16[12,3712]{1,0:T(8,128)(2,1)S(1)} %pad_maximum_fusion.9), channel_id=1, source_target_pairs={{0,16},{2,18},{4,20},{6,22},{8,24},{10,26},{12,28},{14,30},{16,0},... | collective-permute-start | bytes 267272 | tf_op jit(solution)/shard_map/ppermute | solution.py:22
  124.7 8.2 %collective-permute-start.17 = (bf16[32,3584]{1,0:T(8,128)(2,1)S(1)}, bf16[32,3584]{1,0:T(8,128)(2,1)S(1)}, u32[]{:S(2)}, u32[]{:S(2)}) collective-permute-start(bf16[32,3584]{1,0:T(8,128)(2,1)S(1)} %slice.333), channel_id=1, source_target_pairs={{0,8},{2,10},{4,12},{6,14},{8,0},{10,2},{12,4},{14,6},{16,24},{18,... | collective-permute-start | bytes 688136 | tf_op jit(solution)/shard_map/ppermute | solution.py:22
  126.4 12.8 %collective-permute-start.22 = (bf16[32,3712]{1,0:T(8,128)(2,1)S(1)}, bf16[32,3712]{1,0:T(8,128)(2,1)S(1)}, u32[]{:S(2)}, u32[]{:S(2)}) collective-permute-start(bf16[32,3712]{1,0:T(8,128)(2,1)S(1)} %slice.332), channel_id=1, source_target_pairs={{0,4},{2,6},{4,0},{6,2},{8,12},{10,14},{12,8},{14,10},{16,20},{18,... | collective-permute-start | bytes 712712 | tf_op jit(solution)/shard_map/ppermute | solution.py:22
  132.8 6.1 %collective-permute-start.25 = (bf16[4,3584]{1,0:T(4,128)(2,1)S(1)}, bf16[4,3584]{1,0:T(4,128)(2,1)S(1)}, u32[]{:S(2)}, u32[]{:S(2)}) collective-permute-start(bf16[4,3584]{1,0:T(4,128)(2,1)S(1)} %slice.337), channel_id=1, source_target_pairs={{0,16},{2,18},{4,20},{6,22},{8,24},{10,26},{12,28},{14,30},{16,0},... | collective-permute-start | bytes 86024 | tf_op jit(solution)/shard_map/ppermute | solution.py:22
  133.7 16.4 %copy-start.20 = (f32[3584]{0:T(1024)S(1)}, f32[3584]{0:T(1024)}, u32[]{:S(2)}) copy-start(f32[3584]{0:T(1024)} %param.22) | copy-start | bytes 43012
  133.8 11.1 %collective-permute-start.19 = (bf16[16,3584]{1,0:T(8,128)(2,1)S(1)}, bf16[16,3584]{1,0:T(8,128)(2,1)S(1)}, u32[]{:S(2)}, u32[]{:S(2)}) collective-permute-start(bf16[16,3584]{1,0:T(8,128)(2,1)S(1)} %slice.335), channel_id=1, source_target_pairs={{0,16},{2,18},{4,20},{6,22},{8,24},{10,26},{12,28},{14,30},{16,0},... | collective-permute-start | bytes 344072 | tf_op jit(solution)/shard_map/ppermute | solution.py:22
  139.0 4.2 %collective-permute-start.26 = (bf16[8,3584]{1,0:T(8,128)(2,1)S(1)}, bf16[8,3584]{1,0:T(8,128)(2,1)S(1)}, u32[]{:S(2)}, u32[]{:S(2)}) collective-permute-start(bf16[8,3584]{1,0:T(8,128)(2,1)S(1)} %pad_maximum_fusion.12), channel_id=1, source_target_pairs={{0,8},{2,10},{4,12},{6,14},{8,0},{10,2},{12,4},{14,6},{16,24},{18,... | collective-permute-start | bytes 172040 | tf_op jit(solution)/shard_map/ppermute | solution.py:22
  139.3 5.6 %collective-permute-start.23 = (bf16[16,3712]{1,0:T(8,128)(2,1)S(1)}, bf16[16,3712]{1,0:T(8,128)(2,1)S(1)}, u32[]{:S(2)}, u32[]{:S(2)}) collective-permute-start(bf16[16,3712]{1,0:T(8,128)(2,1)S(1)} %slice.334), channel_id=1, source_target_pairs={{0,8},{2,10},{4,12},{6,14},{8,0},{10,2},{12,4},{14,6},{16,24},{18,... | collective-permute-start | bytes 356360 | tf_op jit(solution)/shard_map/ppermute | solution.py:22
  143.3 4.9 %collective-permute-start.27 = (bf16[16,3584]{1,0:T(8,128)(2,1)S(1)}, bf16[16,3584]{1,0:T(8,128)(2,1)S(1)}, u32[]{:S(2)}, u32[]{:S(2)}) collective-permute-start(bf16[16,3584]{1,0:T(8,128)(2,1)S(1)} %pad_maximum_fusion.10), channel_id=1, source_target_pairs={{0,4},{2,6},{4,0},{6,2},{8,12},{10,14},{12,8},{14,10},{16,20},{18,... | collective-permute-start | bytes 344072 | tf_op jit(solution)/shard_map/ppermute | solution.py:22
  145.0 5.2 %collective-permute-start.24 = (bf16[8,3712]{1,0:T(8,128)(2,1)S(1)}, bf16[8,3712]{1,0:T(8,128)(2,1)S(1)}, u32[]{:S(2)}, u32[]{:S(2)}) collective-permute-start(bf16[8,3712]{1,0:T(8,128)(2,1)S(1)} %slice.336), channel_id=1, source_target_pairs={{0,16},{2,18},{4,20},{6,22},{8,24},{10,26},{12,28},{14,30},{16,0},... | collective-permute-start | bytes 178184 | tf_op jit(solution)/shard_map/ppermute | solution.py:22
  148.2 2.9 %collective-permute-start.28 = (bf16[32,3584]{1,0:T(8,128)(2,1)S(1)}, bf16[32,3584]{1,0:T(8,128)(2,1)S(1)}, u32[]{:S(2)}, u32[]{:S(2)}) collective-permute-start(bf16[32,3584]{1,0:T(8,128)(2,1)S(1)} %pad_maximum_fusion.5), channel_id=1, source_target_pairs={{0,2},{2,0},{4,6},{6,4},{8,10},{10,8},{12,14},{14,12},{16,18},{18,... | collective-permute-start | bytes 688136 | tf_op jit(solution)/shard_map/ppermute | solution.py:22
